TPU v7x, 32 devices: a whole 2x2x4 slice. The times are simulated.
32 devices in a mesh: dp: 8 (over y, x, core), seq: 4 (over z).
Axes of the slice: x: 2, y: 2, z: 4, core: 2. Of those that a mesh axis runs over, the one named last changes fastest.
Arguments:
- inputs: bfloat16 [16, 1024, 1408], P('dp', 'seq'), may hold values from -6 to 6
- skipped: bfloat16 [16, 1024, 1408], P('dp', 'seq'), may hold values from -6 to 6
- text_rows: bfloat16 [16, 256, 1024], P('dp', 'seq'), may hold values from -6 to 6
- condition: bfloat16 [16, 1408], P('dp'), may hold values from -6 to 6
- cotangent: bfloat16 [16, 1024, 1408], P('dp', 'seq'), may hold values from -6 to 6
- norm_gains: float32 [7040], replicated, may hold values from 0.1 to 1.9
- skip_weight: bfloat16 [2816, 1408], P('seq', 'dp'), may hold values from -0.109375 to 0.109375
- shift_weight: bfloat16 [1408, 1408], P('seq', 'dp'), may hold values from -0.15625 to 0.15625
- query_key_weight: bfloat16 [1408, 2816], P('seq', 'dp'), may hold values from -0.15625 to 0.15625
- value_weight: bfloat16 [1408, 1408], P('seq', 'dp'), may hold values from -0.15625 to 0.15625
- self_output: bfloat16 [1408, 1408], P('seq', 'dp'), may hold values from -0.875 to 0.875
- cross_query: bfloat16 [1408, 1408], P('seq', 'dp'), may hold values from -0.15625 to 0.15625
- cross_memory: bfloat16 [1024, 2816], P('seq', 'dp'), may hold values from -0.1875 to 0.1875
- cross_output: bfloat16 [1408, 1408], P('seq', 'dp'), may hold values from -0.875 to 0.875
- up_weight: bfloat16 [1408, 6144], P('seq', 'dp'), may hold values from -0.15625 to 0.15625
- down_weight: bfloat16 [6144, 1408], P('seq', 'dp'), may hold values from -0.078125 to 0.078125
Outputs:
- blended_out: bfloat16 [16, 1024, 1408], P('dp', 'seq')
- grad_input: float32 [16, 1024, 1408], P('dp', 'seq')
- grad_skipped: float32 [16, 1024, 1408], P('dp', 'seq')
- grad_text: float32 [16, 256, 1024], P('dp', 'seq')
- grad_gains: float32 [7040], replicated
- grad_skip_weight: float32 [2816, 1408], P('seq', 'dp')
- grad_shift_weight: float32 [1408, 1408], P('seq', 'dp')
- grad_query_key_weight: float32 [1408, 2816], P('seq', 'dp')
- grad_value_weight: float32 [1408, 1408], P('seq', 'dp')
- grad_self_output: float32 [1408, 1408], P('seq', 'dp')
- grad_cross_query: float32 [1408, 1408], P('seq', 'dp')
- grad_cross_memory: float32 [1024, 2816], P('seq', 'dp')
- grad_cross_output: float32 [1408, 1408], P('seq', 'dp')
- grad_up_weight: float32 [1408, 6144], P('seq', 'dp')
- grad_down_weight: float32 [6144, 1408], P('seq', 'dp')
All inputs are finite; a program needn't handle non-finite values.
Results may differ from a plain program's by a relative error of at most 0.02.
Values may be sent and summed in bfloat16 or wider, within the bound.
No kernel may reach another device: no remote copies, remote signals or barrier semaphores. Data moves between devices by JAX's collectives and lax.ppermute only.
A program may use at most 384 MiB of HBM per device.

v0:
```python
import jax
import jax.numpy as jnp
from jax import lax
from jax.sharding import PartitionSpec as P

H = 16
HD = 88
GRID = 32


epsilon = 1e-06


def as_sent(shard):

    def short(part):
        return part.astype(jnp.bfloat16) if part.dtype == jnp.float32 else part

    return jax.tree.map(short, shard)


def normalize(values):
    center = values - jnp.mean(values, axis=-1, keepdims=True)
    spread = jnp.mean(center * center, axis=-1, keepdims=True)
    return center * lax.rsqrt(spread + epsilon)


def norm_gain(values, gain_vec):
    return normalize(values) * gain_vec


def shifted_norm(values, gain_vec, offset):
    return normalize(values) * gain_vec + offset[:, None, :]


def gelu_tanh(values):
    return jax.nn.gelu(values, approximate=True)


def rotate(per_head, tables):
    row_cos, row_sin, col_cos, col_sin = tables
    quarter = per_head.shape[-1] // 4
    part_one = per_head[..., :quarter]
    part_two = per_head[..., quarter : 2 * quarter]
    part_three = per_head[..., 2 * quarter : 3 * quarter]
    part_four = per_head[..., 3 * quarter :]
    return jnp.concatenate(
        [
            part_one * row_cos - part_two * row_sin,
            part_two * row_cos + part_one * row_sin,
            part_three * col_cos - part_four * col_sin,
            part_four * col_cos + part_three * col_sin,
        ],
        axis=-1,
    )


def product(matrix_a, matrix_b):
    return jnp.dot(matrix_a, matrix_b, preferred_element_type=jnp.float32)


def product_tn(matrix_a, matrix_b):
    return lax.dot_general(
        matrix_a, matrix_b, (((0,), (0,)), ((), ())), preferred_element_type=jnp.float32
    )


def product_nt(matrix_a, matrix_b):
    return lax.dot_general(
        matrix_a, matrix_b, (((1,), (1,)), ((), ())), preferred_element_type=jnp.float32
    )


def split_heads(flat_rows):
    latents, token_total, width = flat_rows.shape
    return flat_rows.reshape(latents, token_total, H, HD).transpose(2, 0, 1, 3)


def join_heads(per_head):
    head_total, latents, token_total, head_size = per_head.shape
    return per_head.transpose(1, 2, 0, 3).reshape(latents, token_total, head_total * head_size)


def attend(query_h, key_h, value_h):
    scale = HD ** (-0.5)

    def one_head(operands):
        q_one, k_one, v_one = operands
        scores = (
            jnp.einsum("lsd,lkd->lsk", q_one, k_one, preferred_element_type=jnp.float32) * scale
        )
        row_peak = jnp.max(scores, axis=-1, keepdims=True)
        summed = jnp.sum(jnp.exp(scores - row_peak), axis=-1, keepdims=True)
        log_total = row_peak + jnp.log(summed)
        softmaxed = jnp.exp(scores - log_total).astype(jnp.bfloat16)
        blended = jnp.einsum("lsk,lkd->lsd", softmaxed, v_one, preferred_element_type=jnp.float32)
        return (blended.astype(jnp.bfloat16), log_total)

    return lax.map(one_head, (query_h, key_h, value_h))


def attend_back(query_h, key_h, value_h, log_totals, grad_h):
    scale = HD ** (-0.5)

    def one_head(operands):
        q_one, k_one, v_one, total_one, g_one = operands
        scores = (
            jnp.einsum("lsd,lkd->lsk", q_one, k_one, preferred_element_type=jnp.float32) * scale
        )
        exact = jnp.exp(scores - total_one)
        softmaxed = exact.astype(jnp.bfloat16)
        grad_probs = jnp.einsum("lsd,lkd->lsk", g_one, v_one, preferred_element_type=jnp.float32)
        row_dot = jnp.sum(exact * grad_probs, axis=-1, keepdims=True)
        grad_scores = (exact * (grad_probs - row_dot)).astype(jnp.bfloat16)
        grad_q = (
            jnp.einsum("lsk,lkd->lsd", grad_scores, k_one, preferred_element_type=jnp.float32)
            * scale
        )
        grad_k = (
            jnp.einsum("lsk,lsd->lkd", grad_scores, q_one, preferred_element_type=jnp.float32)
            * scale
        )
        grad_v = jnp.einsum("lsk,lsd->lkd", softmaxed, g_one, preferred_element_type=jnp.float32)
        return (grad_q, grad_k, grad_v)

    return lax.map(one_head, (query_h, key_h, value_h, log_totals, grad_h))


def fetch(group):
    wide = (
        lax.all_gather(as_sent(group[0]), "dp", axis=1, tiled=True),
        lax.all_gather(as_sent(group[1]), "dp", axis=1, tiled=True),
        lax.all_gather(as_sent(group[2]), "dp", axis=1, tiled=True),
        lax.all_gather(as_sent(group[3]), "dp", axis=1, tiled=True),
        lax.all_gather(as_sent(group[4]), "dp", axis=1, tiled=True),
    )
    return (
        lax.all_gather(as_sent(wide[0]), "seq", axis=0, tiled=True),
        lax.all_gather(as_sent(wide[1]), "seq", axis=0, tiled=True),
        lax.all_gather(as_sent(wide[2]), "seq", axis=0, tiled=True),
        lax.all_gather(as_sent(wide[3]), "seq", axis=0, tiled=True),
        lax.all_gather(as_sent(wide[4]), "seq", axis=0, tiled=True),
    )


def on_device(
    inputs,
    skipped,
    text_rows,
    condition,
    cotangent,
    norm_gains,
    skip_weight,
    shift_weight,
    query_key_weight,
    value_weight,
    self_output,
    cross_query,
    cross_memory,
    cross_output,
    up_weight,
    down_weight,
):
    groups = (
        (skip_weight, shift_weight, query_key_weight, value_weight, self_output),
        (cross_query, cross_memory, cross_output, up_weight, down_weight),
    )
    lat_count, local_rows, width = inputs.shape
    text_local = text_rows.shape[1]
    text_width = text_rows.shape[2]
    gain_skip = norm_gains[: 2 * width]
    gain_one = norm_gains[2 * width : 3 * width]
    gain_two = norm_gains[3 * width : 4 * width]
    gain_three = norm_gains[4 * width :]
    position = lax.axis_index("seq") * local_rows + jnp.arange(local_rows, dtype=jnp.int32)
    quarter = HD // 4
    frequency = jnp.power(10000.0, -jnp.arange(quarter, dtype=jnp.float32) / quarter)
    row_angle = (position // GRID).astype(jnp.float32)[None, :, None, None] * frequency
    col_angle = (position % GRID).astype(jnp.float32)[None, :, None, None] * frequency
    tables = (jnp.cos(row_angle), jnp.sin(row_angle), jnp.cos(col_angle), jnp.sin(col_angle))

    def prepare(flat_part):
        return rotate(normalize(flat_part.reshape(1, local_rows, H, HD)), tables)

    def query_norm(flat_part):
        return normalize(flat_part.reshape(1, local_rows, H, HD))

    def memory_norm(flat_part):
        return normalize(flat_part.reshape(1, text_local, H, HD))

    def forward_pass(fetcher, x_in, x_skip, x_text, x_cond):
        keep = {}
        skip_w, shift_w, pair_w, value_w, self_w = fetcher(0)
        joined = jnp.concatenate([x_in, x_skip], axis=-1).astype(jnp.float32)
        level_zero = norm_gain(joined, gain_skip).astype(jnp.bfloat16)
        stream_zero = product(level_zero, skip_w)
        cond_act = jax.nn.silu(x_cond.astype(jnp.float32)).astype(jnp.bfloat16)[None, :]
        shift_rows = product(cond_act, shift_w)
        stream_cube = stream_zero.reshape(1, local_rows, width)
        level_one = (
            shifted_norm(stream_cube, gain_one, shift_rows)
            .astype(jnp.bfloat16)
            .reshape(local_rows, width)
        )
        pair_proj = product(level_one, pair_w)
        value_proj = product(level_one, value_w)
        query_flat = pair_proj[:, :width]
        key_flat = pair_proj[:, width:]
        query_h = prepare(query_flat).astype(jnp.bfloat16).transpose(2, 0, 1, 3)
        key_local = prepare(key_flat).astype(jnp.bfloat16).reshape(1, local_rows, width)
        value_local = value_proj.astype(jnp.bfloat16).reshape(1, local_rows, width)
        key_every, value_every = (
            lax.all_gather(key_local, "seq", axis=1, tiled=True),
            lax.all_gather(value_local, "seq", axis=1, tiled=True),
        )
        key_h = split_heads(key_every)
        value_h = split_heads(value_every)
        self_heads, self_totals = attend(query_h, key_h, value_h)
        attended = join_heads(self_heads).reshape(local_rows, width)
        stream_one = stream_zero + product(attended, self_w)
        cq_w, memory_w, cout_w, up_w, down_w = fetcher(1)
        level_two = norm_gain(stream_one, gain_two).astype(jnp.bfloat16)
        cross_proj = product(level_two, cq_w)
        cross_h = query_norm(cross_proj).astype(jnp.bfloat16).transpose(2, 0, 1, 3)
        memory_proj = product(x_text, memory_w)
        memory_key = (
            memory_norm(memory_proj[:, :width]).astype(jnp.bfloat16).reshape(1, text_local, width)
        )
        memory_value = memory_proj[:, width:].astype(jnp.bfloat16).reshape(1, text_local, width)
        text_key, text_value = (
            lax.all_gather(memory_key, "seq", axis=1, tiled=True),
            lax.all_gather(memory_value, "seq", axis=1, tiled=True),
        )
        text_key_h = split_heads(text_key)
        text_value_h = split_heads(text_value)
        cross_heads, cross_totals = attend(cross_h, text_key_h, text_value_h)
        crossed = join_heads(cross_heads).reshape(local_rows, width)
        stream_two = stream_one + product(crossed, cout_w)
        level_three = norm_gain(stream_two, gain_three).astype(jnp.bfloat16)
        hidden = product(level_three, up_w)
        activated = gelu_tanh(hidden).astype(jnp.bfloat16)
        final_rows = stream_two + product(activated, down_w)
        keep["blended"] = final_rows.astype(jnp.bfloat16)
        keep["weights"] = (
            skip_w,
            shift_w,
            pair_w,
            value_w,
            self_w,
            cq_w,
            memory_w,
            cout_w,
            up_w,
            down_w,
        )
        keep["joined"] = joined
        keep["level_zero"] = level_zero
        keep["cond_act"] = cond_act
        keep["shift_rows"] = shift_rows
        keep["stream_cube"] = stream_cube
        keep["level_one"] = level_one
        keep["query_flat"] = query_flat
        keep["key_flat"] = key_flat
        keep["query_h"] = query_h
        keep["key_h"] = key_h
        keep["value_h"] = value_h
        keep["self_totals"] = self_totals
        keep["attended"] = attended
        keep["stream_one"] = stream_one
        keep["level_two"] = level_two
        keep["cross_proj"] = cross_proj
        keep["cross_h"] = cross_h
        keep["memory_proj"] = memory_proj
        keep["text_key_h"] = text_key_h
        keep["text_value_h"] = text_value_h
        keep["cross_totals"] = cross_totals
        keep["crossed"] = crossed
        keep["stream_two"] = stream_two
        keep["level_three"] = level_three
        keep["hidden"] = hidden
        keep["activated"] = activated
        return keep

    def fetcher(index):
        return fetch(groups[index])

    def backward_step(carry, item):
        x_in, x_skip, x_text, x_cond, x_grad = item
        keep = forward_pass(fetcher, x_in, x_skip, x_text, x_cond)
        back_weights = fetcher(1) + fetcher(0)
        (
            back_cq,
            back_memory,
            back_cout,
            back_up,
            back_down,
            back_skip,
            back_shift,
            back_pair,
            back_value,
            back_self,
        ) = back_weights
        grad_act = product_nt(x_grad, back_down)
        _, gelu_pull = jax.vjp(gelu_tanh, keep["hidden"])
        grad_hidden = gelu_pull(grad_act)[0].astype(jnp.bfloat16)
        grad_level_three = product_nt(grad_hidden, back_up)
        _, pull_three = jax.vjp(norm_gain, keep["stream_two"], gain_three)
        grad_from_three, grad_gain_three = pull_three(grad_level_three)
        grad_stream_two = x_grad.astype(jnp.float32) + grad_from_three
        cross_back = grad_stream_two.astype(jnp.bfloat16)
        grad_crossed = product_nt(cross_back, back_cout).astype(jnp.bfloat16)
        grad_crossed_h = grad_crossed.reshape(1, local_rows, H, HD).transpose(2, 0, 1, 3)
        grad_cq_h, grad_tk_h, grad_tv_h = attend_back(
            keep["cross_h"],
            keep["text_key_h"],
            keep["text_value_h"],
            keep["cross_totals"],
            grad_crossed_h,
        )
        grad_tk_own, grad_tv_own = (
            lax.psum_scatter(
                join_heads(grad_tk_h).astype(jnp.bfloat16), "seq", scatter_dimension=1, tiled=True
            ).astype(jnp.float32),
            lax.psum_scatter(
                join_heads(grad_tv_h).astype(jnp.bfloat16), "seq", scatter_dimension=1, tiled=True
            ).astype(jnp.float32),
        )
        _, pull_memory = jax.vjp(memory_norm, keep["memory_proj"][:, :width])
        grad_memory_key = pull_memory(grad_tk_own.reshape(1, text_local, H, HD))[0]
        grad_memory_proj = jnp.concatenate(
            [grad_memory_key, grad_tv_own.reshape(text_local, width)], axis=-1
        ).astype(jnp.bfloat16)
        grad_text = product_nt(grad_memory_proj, back_memory)
        _, pull_cq = jax.vjp(query_norm, keep["cross_proj"])
        grad_cq_flat = pull_cq(grad_cq_h.transpose(1, 2, 0, 3))[0].astype(jnp.bfloat16)
        grad_level_two = product_nt(grad_cq_flat, back_cq)
        _, pull_two = jax.vjp(norm_gain, keep["stream_one"], gain_two)
        grad_from_two, grad_gain_two = pull_two(grad_level_two)
        grad_stream_one = grad_stream_two + grad_from_two
        self_back = grad_stream_one.astype(jnp.bfloat16)
        grad_attended = product_nt(self_back, back_self).astype(jnp.bfloat16)
        grad_attended_h = grad_attended.reshape(1, local_rows, H, HD).transpose(2, 0, 1, 3)
        grad_q_h, grad_k_h, grad_v_h = attend_back(
            keep["query_h"], keep["key_h"], keep["value_h"], keep["self_totals"], grad_attended_h
        )
        grad_k_own, grad_v_own = (
            lax.psum_scatter(
                join_heads(grad_k_h).astype(jnp.bfloat16), "seq", scatter_dimension=1, tiled=True
            ).astype(jnp.float32),
            lax.psum_scatter(
                join_heads(grad_v_h).astype(jnp.bfloat16), "seq", scatter_dimension=1, tiled=True
            ).astype(jnp.float32),
        )
        _, pull_query = jax.vjp(prepare, keep["query_flat"])
        grad_query_flat = pull_query(grad_q_h.transpose(1, 2, 0, 3))[0]
        _, pull_key = jax.vjp(prepare, keep["key_flat"])
        grad_key_flat = pull_key(grad_k_own.reshape(1, local_rows, H, HD))[0]
        grad_pair_proj = jnp.concatenate([grad_query_flat, grad_key_flat], axis=-1).astype(
            jnp.bfloat16
        )
        grad_value_proj = grad_v_own.reshape(local_rows, width).astype(jnp.bfloat16)
        grad_level_one = (
            product_nt(grad_pair_proj, back_pair) + product_nt(grad_value_proj, back_value)
        ).reshape(1, local_rows, width)
        _, pull_one = jax.vjp(shifted_norm, keep["stream_cube"], gain_one, keep["shift_rows"])
        grad_from_one, grad_gain_one, grad_shift_rows = pull_one(grad_level_one)
        skip_back = (grad_stream_one + grad_from_one.reshape(local_rows, width)).astype(
            jnp.bfloat16
        )
        grad_level_zero = product_nt(skip_back, back_skip)
        _, pull_zero = jax.vjp(norm_gain, keep["joined"], gain_skip)
        grad_joined, grad_gain_skip = pull_zero(grad_level_zero)
        gain_terms = jnp.concatenate(
            [grad_gain_skip, grad_gain_one, grad_gain_two, grad_gain_three]
        )
        pieces = (
            keep["blended"],
            grad_joined[:, :width],
            grad_joined[:, width:],
            grad_text,
            gain_terms,
            keep["level_zero"],
            skip_back,
            keep["cond_act"][0],
            grad_shift_rows[0],
            keep["level_one"],
            grad_pair_proj,
            grad_value_proj,
            keep["attended"],
            self_back,
            keep["level_two"],
            grad_cq_flat,
            grad_memory_proj,
            keep["crossed"],
            cross_back,
            keep["level_three"],
            grad_hidden,
            keep["activated"],
        )
        return (carry, pieces)

    _, stacked = lax.scan(
        backward_step,
        jnp.zeros((), jnp.float32),
        (inputs, skipped, text_rows, condition, cotangent),
    )
    (
        blended_out,
        grad_input,
        grad_skipped,
        grad_text,
        gain_stack,
        level_zero_all,
        skip_back_all,
        cond_all,
        shift_grad_all,
        level_one_all,
        pair_grad_all,
        value_grad_all,
        attended_all,
        self_back_all,
        level_two_all,
        cq_grad_all,
        memory_grad_all,
        crossed_all,
        cross_back_all,
        level_three_all,
        hidden_grad_all,
        activated_all,
    ) = stacked
    row_total = lat_count * local_rows

    def flat(stack_rows):
        return stack_rows.reshape(row_total, stack_rows.shape[-1])

    text_all = text_rows.reshape(lat_count * text_local, text_width)
    grad_down = product_tn(flat(activated_all), flat(cotangent))
    grad_up = product_tn(flat(level_three_all), flat(hidden_grad_all))
    grad_cout = product_tn(flat(crossed_all), flat(cross_back_all))
    grad_memory = product_tn(text_all, memory_grad_all.reshape(lat_count * text_local, 2 * width))
    grad_cq = product_tn(flat(level_two_all), flat(cq_grad_all))
    grad_self = product_tn(flat(attended_all), flat(self_back_all))
    grad_pair = product_tn(flat(level_one_all), flat(pair_grad_all))
    grad_value = product_tn(flat(level_one_all), flat(value_grad_all))
    grad_shift = jnp.dot(
        cond_all.astype(jnp.float32).T, shift_grad_all, precision=lax.Precision.HIGHEST
    )
    grad_skip_w = product_tn(flat(level_zero_all), flat(skip_back_all))
    grad_gains = lax.psum(jnp.sum(gain_stack, axis=0), ("dp", "seq"))
    terms = (
        grad_skip_w,
        grad_shift,
        grad_pair,
        grad_value,
        grad_self,
        grad_cq,
        grad_memory,
        grad_cout,
        grad_up,
        grad_down,
    )
    partial_terms = (
        lax.psum_scatter(
            terms[0].astype(jnp.bfloat16), "seq", scatter_dimension=0, tiled=True
        ).astype(jnp.float32),
        lax.psum_scatter(
            terms[1].astype(jnp.bfloat16), "seq", scatter_dimension=0, tiled=True
        ).astype(jnp.float32),
        lax.psum_scatter(
            terms[2].astype(jnp.bfloat16), "seq", scatter_dimension=0, tiled=True
        ).astype(jnp.float32),
        lax.psum_scatter(
            terms[3].astype(jnp.bfloat16), "seq", scatter_dimension=0, tiled=True
        ).astype(jnp.float32),
        lax.psum_scatter(
            terms[4].astype(jnp.bfloat16), "seq", scatter_dimension=0, tiled=True
        ).astype(jnp.float32),
        lax.psum_scatter(
            terms[5].astype(jnp.bfloat16), "seq", scatter_dimension=0, tiled=True
        ).astype(jnp.float32),
        lax.psum_scatter(
            terms[6].astype(jnp.bfloat16), "seq", scatter_dimension=0, tiled=True
        ).astype(jnp.float32),
        lax.psum_scatter(
            terms[7].astype(jnp.bfloat16), "seq", scatter_dimension=0, tiled=True
        ).astype(jnp.float32),
        lax.psum_scatter(
            terms[8].astype(jnp.bfloat16), "seq", scatter_dimension=0, tiled=True
        ).astype(jnp.float32),
        lax.psum_scatter(
            terms[9].astype(jnp.bfloat16), "seq", scatter_dimension=0, tiled=True
        ).astype(jnp.float32),
    )
    owned = (
        lax.psum_scatter(partial_terms[0], "dp", scatter_dimension=1, tiled=True),
        lax.psum_scatter(partial_terms[1], "dp", scatter_dimension=1, tiled=True),
        lax.psum_scatter(partial_terms[2], "dp", scatter_dimension=1, tiled=True),
        lax.psum_scatter(partial_terms[3], "dp", scatter_dimension=1, tiled=True),
        lax.psum_scatter(partial_terms[4], "dp", scatter_dimension=1, tiled=True),
        lax.psum_scatter(partial_terms[5], "dp", scatter_dimension=1, tiled=True),
        lax.psum_scatter(partial_terms[6], "dp", scatter_dimension=1, tiled=True),
        lax.psum_scatter(partial_terms[7], "dp", scatter_dimension=1, tiled=True),
        lax.psum_scatter(partial_terms[8], "dp", scatter_dimension=1, tiled=True),
        lax.psum_scatter(partial_terms[9], "dp", scatter_dimension=1, tiled=True),
    )
    return (
        blended_out,
        grad_input,
        grad_skipped,
        grad_text,
        grad_gains,
        owned[0],
        owned[1],
        owned[2],
        owned[3],
        owned[4],
        owned[5],
        owned[6],
        owned[7],
        owned[8],
        owned[9],
    )


def solution(mesh):
    return jax.shard_map(
        on_device,
        mesh=mesh,
        in_specs=(
            P("dp", "seq", None),
            P("dp", "seq", None),
            P("dp", "seq", None),
            P("dp", None),
            P("dp", "seq", None),
            P(),
            P("seq", "dp"),
            P("seq", "dp"),
            P("seq", "dp"),
            P("seq", "dp"),
            P("seq", "dp"),
            P("seq", "dp"),
            P("seq", "dp"),
            P("seq", "dp"),
            P("seq", "dp"),
            P("seq", "dp"),
        ),
        out_specs=(
            P("dp", "seq", None),
            P("dp", "seq", None),
            P("dp", "seq", None),
            P("dp", "seq", None),
            P(),
            P("seq", "dp"),
            P("seq", "dp"),
            P("seq", "dp"),
            P("seq", "dp"),
            P("seq", "dp"),
            P("seq", "dp"),
            P("seq", "dp"),
            P("seq", "dp"),
            P("seq", "dp"),
            P("seq", "dp"),
        ),
        check_vma=False,
    )
```

profile of v0, /device:TPU:0, one launch (start us, length us, event | category | flops | bytes accessed | tf_op | source)
XLA Modules:
  0.0 6251.7 jit_solution(12836844494364286762)
XLA Ops:
  11.5 4336.5 %while.174 = (s32[]{:T(128)}, bf16[2,256,1408]{2,1,0:T(8,128)(2,1)}, f32[2,256,1408]{2,1,0:T(8,128)}, f32[2,256,1408]{2,1,0:T(8,128)}, f32[2,64,1024]{2,1,0:T(8,...) while((s32[]{:T(128)}, bf16[2,256,1408]{2,1,0:T(8,128)(2,1)}, ...), condition=%wide.region_56.57_spmd.clone.clone, body=%wide.region_0.56_spmd.clone.clone.sunk | while | flops 35298840576 | bytes 1166665088 | solution.py:402
  108.0 76.0 %all-gather.37.cloned.1.call-done = bf16[1408,1408]{1,0:T(8,128)(2,1)} async-done(((bf16[352,1408]{1,0:T(8,128)(2,1)}), bf16[1408,1408]{1,0:T(8,128)(2,1)}) %all-gather.37.cloned.1.call-update) | async-done | bytes 3964944 | tf_op jit(solution)/shard_map/while/body/eval_jaxpr/all_gather | solution.py:139
  186.7 139.4 %all-gather.35.cloned.1.call-done = bf16[2816,1408]{1,0:T(8,128)(2,1)} async-done(((bf16[704,1408]{1,0:T(8,128)(2,1)}), bf16[2816,1408]{1,0:T(8,128)(2,1)}) %all-gather.35.cloned.1.call-update) | async-done | bytes 7929872 | tf_op jit(solution)/shard_map/while/body/eval_jaxpr/all_gather | solution.py:138
  334.4 133.5 %all-gather.41.cloned.1.call-done = bf16[1408,2816]{1,0:T(8,128)(2,1)} async-done(((bf16[352,2816]{1,0:T(8,128)(2,1)}), bf16[1408,2816]{1,0:T(8,128)(2,1)}) %all-gather.41.cloned.1.call-update) | async-done | bytes 7929872 | tf_op jit(solution)/shard_map/while/body/eval_jaxpr/all_gather | solution.py:140
  478.0 67.3 %all-gather.45.cloned.1.call-done = bf16[1408,1408]{1,0:T(8,128)(2,1)} async-done(((bf16[352,1408]{1,0:T(8,128)(2,1)}), bf16[1408,1408]{1,0:T(8,128)(2,1)}) %all-gather.45.cloned.1.call-update) | async-done | bytes 3964944 | tf_op jit(solution)/shard_map/while/body/eval_jaxpr/all_gather | solution.py:141
  627.1 107.6 %all-gather.55.cloned.1.call-done = bf16[1024,2816]{0,1:T(8,128)(2,1)} async-done(((bf16[256,2816]{0,1:T(8,128)(2,1)}), bf16[1024,2816]{0,1:T(8,128)(2,1)}) %all-gather.55.cloned.1.call-update) | async-done | bytes 5767184 | tf_op jit(solution)/shard_map/while/body/eval_jaxpr/all_gather | solution.py:139
  887.8 67.1 %while.175 = (s32[]{:T(128)}, bf16[16,1,256,88]{2,3,1,0:T(8,128)(2,1)}, f32[16,1,256,1]{2,3,1,0:T(1,128)}, bf16[16,1,256,88]{3,2,1,0:T(8,128)(2,1)}, bf16[16,1,1...) while((s32[]{:T(128)}, bf16[16,1,256,88]{2,3,1,0:T(8,128)(2,1)}, ...), condition=%wide.region_12.12_spmd, body=%wide.region_9.11_spmd.sunk | while | flops 93869824 | bytes 3792461 | solution.py:99
  961.7 68.7 %all-gather.51.cloned.1.call-done = bf16[1408,1408]{1,0:T(8,128)(2,1)} async-done(((bf16[352,1408]{1,0:T(8,128)(2,1)}), bf16[1408,1408]{1,0:T(8,128)(2,1)}) %all-gather.51.cloned.1.call-update) | async-done | bytes 3964944 | tf_op jit(solution)/shard_map/while/body/eval_jaxpr/all_gather | solution.py:138
  1114.3 290.1 %all-gather.65.cloned.1.call-done = bf16[1408,6144]{1,0:T(8,128)(2,1)} async-done(((bf16[352,6144]{1,0:T(8,128)(2,1)}), bf16[1408,6144]{1,0:T(8,128)(2,1)}) %all-gather.65.cloned.1.call-update) | async-done | bytes 17301520 | tf_op jit(solution)/shard_map/while/body/eval_jaxpr/all_gather | solution.py:141
  1417.4 284.3 %all-gather.61.cloned.1.call-done = bf16[6144,1408]{0,1:T(8,128)(2,1)} async-done(((bf16[1536,1408]{0,1:T(8,128)(2,1)}), bf16[6144,1408]{0,1:T(8,128)(2,1)}) %all-gather.61.cloned.1.call-update) | async-done | bytes 17301520 | tf_op jit(solution)/shard_map/while/body/eval_jaxpr/all_gather | solution.py:142
  1747.5 125.1 %while.177 = (s32[]{:T(128)}, f32[16,1,256,88]{2,3,1,0:T(8,128)}, bf16[16,1,256,88]{2,3,1,0:T(8,128)(2,1)}, bf16[16,1,256,88]{2,3,1,0:T(8,128)(2,1)}, bf16[16,1,...) while((s32[]{:T(128)}, f32[16,1,256,88]{2,3,1,0:T(8,128)}, ...), condition=%wide.region_29.29_spmd, body=%wide.region_27.28_spmd.sunk | while | flops 58240768 | bytes 2664553 | solution.py:126
  1896.8 143.5 %while.178 = (s32[]{:T(128)}, f32[16,1,256,88]{2,3,1,0:T(8,128)}, bf16[16,1,1024,88]{2,3,1,0:T(8,128)(2,1)}, bf16[16,1,1024,88]{2,3,1,0:T(8,128)(2,1)}, bf16[16,...) while((s32[]{:T(128)}, f32[16,1,256,88]{2,3,1,0:T(8,128)}, ...), condition=%wide.region_36.36_spmd, body=%wide.region_34.35_spmd.sunk | while | flops 232896256 | bytes 9693289 | solution.py:126
  2270.4 76.1 %all-gather.37.cloned.1.call-done = bf16[1408,1408]{1,0:T(8,128)(2,1)} async-done(((bf16[352,1408]{1,0:T(8,128)(2,1)}), bf16[1408,1408]{1,0:T(8,128)(2,1)}) %all-gather.37.cloned.1.call-update) | async-done | bytes 3964944 | tf_op jit(solution)/shard_map/while/body/eval_jaxpr/all_gather | solution.py:139
  2349.3 139.4 %all-gather.35.cloned.1.call-done = bf16[2816,1408]{1,0:T(8,128)(2,1)} async-done(((bf16[704,1408]{1,0:T(8,128)(2,1)}), bf16[2816,1408]{1,0:T(8,128)(2,1)}) %all-gather.35.cloned.1.call-update) | async-done | bytes 7929872 | tf_op jit(solution)/shard_map/while/body/eval_jaxpr/all_gather | solution.py:138
  2497.0 133.5 %all-gather.41.cloned.1.call-done = bf16[1408,2816]{1,0:T(8,128)(2,1)} async-done(((bf16[352,2816]{1,0:T(8,128)(2,1)}), bf16[1408,2816]{1,0:T(8,128)(2,1)}) %all-gather.41.cloned.1.call-update) | async-done | bytes 7929872 | tf_op jit(solution)/shard_map/while/body/eval_jaxpr/all_gather | solution.py:140
  2789.5 107.8 %all-gather.55.cloned.1.call-done = bf16[1024,2816]{0,1:T(8,128)(2,1)} async-done(((bf16[256,2816]{0,1:T(8,128)(2,1)}), bf16[1024,2816]{0,1:T(8,128)(2,1)}) %all-gather.55.cloned.1.call-update) | async-done | bytes 5767184 | tf_op jit(solution)/shard_map/while/body/eval_jaxpr/all_gather | solution.py:139
  3124.2 68.9 %all-gather.51.cloned.1.call-done = bf16[1408,1408]{1,0:T(8,128)(2,1)} async-done(((bf16[352,1408]{1,0:T(8,128)(2,1)}), bf16[1408,1408]{1,0:T(8,128)(2,1)}) %all-gather.51.cloned.1.call-update) | async-done | bytes 3964944 | tf_op jit(solution)/shard_map/while/body/eval_jaxpr/all_gather | solution.py:138
  3277.0 290.1 %all-gather.65.cloned.1.call-done = bf16[1408,6144]{1,0:T(8,128)(2,1)} async-done(((bf16[352,6144]{1,0:T(8,128)(2,1)}), bf16[1408,6144]{1,0:T(8,128)(2,1)}) %all-gather.65.cloned.1.call-update) | async-done | bytes 17301520 | tf_op jit(solution)/shard_map/while/body/eval_jaxpr/all_gather | solution.py:141
  3580.2 284.4 %all-gather.61.cloned.1.call-done = bf16[6144,1408]{0,1:T(8,128)(2,1)} async-done(((bf16[1536,1408]{0,1:T(8,128)(2,1)}), bf16[6144,1408]{0,1:T(8,128)(2,1)}) %all-gather.61.cloned.1.call-update) | async-done | bytes 17301520 | tf_op jit(solution)/shard_map/while/body/eval_jaxpr/all_gather | solution.py:142
  3910.5 125.1 %while.177 = (s32[]{:T(128)}, f32[16,1,256,88]{2,3,1,0:T(8,128)}, bf16[16,1,256,88]{2,3,1,0:T(8,128)(2,1)}, bf16[16,1,256,88]{2,3,1,0:T(8,128)(2,1)}, bf16[16,1,...) while((s32[]{:T(128)}, f32[16,1,256,88]{2,3,1,0:T(8,128)}, ...), condition=%wide.region_29.29_spmd, body=%wide.region_27.28_spmd.sunk | while | flops 58240768 | bytes 2664553 | solution.py:126
  4059.8 143.5 %while.178 = (s32[]{:T(128)}, f32[16,1,256,88]{2,3,1,0:T(8,128)}, bf16[16,1,1024,88]{2,3,1,0:T(8,128)(2,1)}, bf16[16,1,1024,88]{2,3,1,0:T(8,128)(2,1)}, bf16[16,...) while((s32[]{:T(128)}, f32[16,1,256,88]{2,3,1,0:T(8,128)}, ...), condition=%wide.region_36.36_spmd, body=%wide.region_34.35_spmd.sunk | while | flops 232896256 | bytes 9693289 | solution.py:126
  4499.4 71.4 %reduce-scatter.47.cloned.1.call-done = bf16[352,1408]{1,0:T(8,128)(2,1)} async-done(((bf16[1408,1408]{1,0:T(8,128)(2,1)}), bf16[352,1408]{1,0:T(8,128)(2,1)}) %reduce-scatter.47.cloned.1.call-update) | async-done | bytes 991248 | tf_op jit(solution)/shard_map/reduce_scatter | solution.py:472
  4573.6 73.0 %reduce-scatter.57.cloned.1.call-done = bf16[352,1408]{1,0:T(8,128)(2,1)} async-done(((bf16[1408,1408]{1,0:T(8,128)(2,1)}), bf16[352,1408]{1,0:T(8,128)(2,1)}) %reduce-scatter.57.cloned.1.call-update) | async-done | bytes 991248 | tf_op jit(solution)/shard_map/reduce_scatter | solution.py:484
  4649.2 73.1 %reduce-scatter.51.cloned.1.call-done = bf16[352,1408]{1,0:T(8,128)(2,1)} async-done(((bf16[1408,1408]{1,0:T(8,128)(2,1)}), bf16[352,1408]{1,0:T(8,128)(2,1)}) %reduce-scatter.51.cloned.1.call-update) | async-done | bytes 991248 | tf_op jit(solution)/shard_map/reduce_scatter | solution.py:478
  4725.1 73.1 %reduce-scatter.49.cloned.1.call-done = bf16[352,1408]{1,0:T(8,128)(2,1)} async-done(((bf16[1408,1408]{1,0:T(8,128)(2,1)}), bf16[352,1408]{1,0:T(8,128)(2,1)}) %reduce-scatter.49.cloned.1.call-update) | async-done | bytes 991248 | tf_op jit(solution)/shard_map/reduce_scatter | solution.py:475
  4800.9 73.1 %reduce-scatter.43.cloned.1.call-done = bf16[352,1408]{1,0:T(8,128)(2,1)} async-done(((bf16[1408,1408]{1,0:T(8,128)(2,1)}), bf16[352,1408]{1,0:T(8,128)(2,1)}) %reduce-scatter.43.cloned.1.call-update) | async-done | bytes 991248 | tf_op jit(solution)/shard_map/reduce_scatter | solution.py:466
  4876.8 102.0 %reduce-scatter.53.cloned.1.call-done = bf16[256,2816]{0,1:T(8,128)(2,1)} async-done(((bf16[1024,2816]{0,1:T(8,128)(2,1)}), bf16[256,2816]{0,1:T(8,128)(2,1)}) %reduce-scatter.53.cloned.1.call-update) | async-done | bytes 1441808 | tf_op jit(solution)/shard_map/reduce_scatter | solution.py:481
  4982.0 136.7 %reduce-scatter.41.cloned.1.call-done = bf16[704,1408]{1,0:T(8,128)(2,1)} async-done(((bf16[2816,1408]{1,0:T(8,128)(2,1)}), bf16[704,1408]{1,0:T(8,128)(2,1)}) %reduce-scatter.41.cloned.1.call-update) | async-done | bytes 1982480 | tf_op jit(solution)/shard_map/reduce_scatter | solution.py:463
  5123.0 287.1 %reduce-scatter.59.cloned.1.call-done = bf16[352,6144]{1,0:T(8,128)(2,1)} async-done(((bf16[1408,6144]{1,0:T(8,128)(2,1)}), bf16[352,6144]{1,0:T(8,128)(2,1)}) %reduce-scatter.59.cloned.1.call-update) | async-done | bytes 4325392 | tf_op jit(solution)/shard_map/reduce_scatter | solution.py:487
  5416.9 285.1 %reduce-scatter.63.cloned.1.call-done = bf16[1536,1408]{1,0:T(8,128)(2,1)} async-done(((bf16[6144,1408]{1,0:T(8,128)(2,1)}), bf16[1536,1408]{1,0:T(8,128)(2,1)}) %reduce-scatter.63.cloned.1.call-update) | async-done | bytes 4325392 | tf_op jit(solution)/shard_map/reduce_scatter | solution.py:490
  6090.8 76.5 %reduce-scatter.61.cloned.1.call-done = f32[352,768]{1,0:T(8,128)} async-done(((f32[352,6144]{1,0:T(8,128)}), f32[352,768]{1,0:T(8,128)}) %reduce-scatter.61.cloned.1.call-update) | async-done | bytes 1081360 | tf_op jit(solution)/shard_map/reduce_scatter | solution.py:503
  6167.3 77.0 %reduce-scatter.79.cloned.1.call-done = f32[176,1536]{1,0:T(8,128)} async-done(((f32[1408,1536]{1,0:T(8,128)}), f32[176,1536]{1,0:T(8,128)}) %reduce-scatter.79.cloned.1.call-update) | async-done | bytes 1081360
  (1863 shorter events, 2802.2 us)
Async XLA Ops:
  80.2 465.1 %all-gather.45.cloned.1.call-start = ((), (), s32[]{:S(2)}) async-start(), calls=%async_computation.50 | async-start | bytes 4956160 | tf_op jit(solution)/shard_map/while/body/eval_jaxpr/all_gather | solution.py:141
  95.7 502.9 %all-gather.63.cloned.1.call-start = ((), (), s32[]{:S(2)}) async-start(), calls=%async_computation.59 | async-start | bytes 4866048 | tf_op jit(solution)/shard_map/while/body/eval_jaxpr/all_gather | solution.py:134
  96.5 530.5 %all-gather.59.cloned.1.call-start = ((), (), s32[]{:S(2)}) async-start(), calls=%async_computation.57 | async-start | bytes 4866048 | tf_op jit(solution)/shard_map/while/body/eval_jaxpr/all_gather | solution.py:135
  97.2 637.5 %all-gather.55.cloned.1.call-start = ((), (), s32[]{:S(2)}) async-start(), calls=%async_computation.55 | async-start | bytes 7208960 | tf_op jit(solution)/shard_map/while/body/eval_jaxpr/all_gather | solution.py:139
  105.0 713.5 %all-gather.43.cloned.1.call-start = ((), (), s32[]{:S(2)}) async-start(), calls=%async_computation.49 | async-start | bytes 3604480 | tf_op jit(solution)/shard_map/while/body/eval_jaxpr/all_gather | solution.py:213
  586.0 521.5 %all-gather.57.cloned.1.call-start = ((), (), s32[]{:S(2)}) async-start(), calls=%async_computation.56 | async-start | bytes 4956160 | tf_op jit(solution)/shard_map/while/body/eval_jaxpr/all_gather | solution.py:140
  598.6 805.8 %all-gather.65.cloned.1.call-start = ((), (), s32[]{:S(2)}) async-start(), calls=%async_computation.60 | async-start | bytes 21626880 | tf_op jit(solution)/shard_map/while/body/eval_jaxpr/all_gather | solution.py:141
  599.2 1102.6 %all-gather.61.cloned.1.call-start = ((), (), s32[]{:S(2)}) async-start(), calls=%async_computation.58 | async-start | bytes 21626880 | tf_op jit(solution)/shard_map/while/body/eval_jaxpr/all_gather | solution.py:142
  627.1 1448.1 %reduce-scatter.87.cloned.1.call-start = ((), (), s32[]{:S(2)}) async-start(), calls=%async_computation.64 | async-start | bytes 901120 | tf_op jit(solution)/shard_map/while/body/eval_jaxpr/reduce_scatter | solution.py:321
  2258.2 503.0 %all-gather.63.cloned.1.call-start = ((), (), s32[]{:S(2)}) async-start(), calls=%async_computation.59 | async-start | bytes 4866048 | tf_op jit(solution)/shard_map/while/body/eval_jaxpr/all_gather | solution.py:134
  2258.9 530.5 %all-gather.59.cloned.1.call-start = ((), (), s32[]{:S(2)}) async-start(), calls=%async_computation.57 | async-start | bytes 4866048 | tf_op jit(solution)/shard_map/while/body/eval_jaxpr/all_gather | solution.py:135
  2259.5 637.8 %all-gather.55.cloned.1.call-start = ((), (), s32[]{:S(2)}) async-start(), calls=%async_computation.55 | async-start | bytes 7208960 | tf_op jit(solution)/shard_map/while/body/eval_jaxpr/all_gather | solution.py:139
  2267.4 713.4 %all-gather.43.cloned.1.call-start = ((), (), s32[]{:S(2)}) async-start(), calls=%async_computation.49 | async-start | bytes 3604480 | tf_op jit(solution)/shard_map/while/body/eval_jaxpr/all_gather | solution.py:213
  2748.5 521.6 %all-gather.57.cloned.1.call-start = ((), (), s32[]{:S(2)}) async-start(), calls=%async_computation.56 | async-start | bytes 4956160 | tf_op jit(solution)/shard_map/while/body/eval_jaxpr/all_gather | solution.py:140
  2761.1 806.0 %all-gather.65.cloned.1.call-start = ((), (), s32[]{:S(2)}) async-start(), calls=%async_computation.60 | async-start | bytes 21626880 | tf_op jit(solution)/shard_map/while/body/eval_jaxpr/all_gather | solution.py:141
  2761.7 1102.9 %all-gather.61.cloned.1.call-start = ((), (), s32[]{:S(2)}) async-start(), calls=%async_computation.58 | async-start | bytes 21626880 | tf_op jit(solution)/shard_map/while/body/eval_jaxpr/all_gather | solution.py:142
  2789.4 1448.6 %reduce-scatter.87.cloned.1.call-start = ((), (), s32[]{:S(2)}) async-start(), calls=%async_computation.64 | async-start | bytes 901120 | tf_op jit(solution)/shard_map/while/body/eval_jaxpr/reduce_scatter | solution.py:321
  4382.7 491.3 %reduce-scatter.43.cloned.1.call-start = ((), (), s32[]{:S(2)}) async-start(), calls=%async_computation.25 | async-start | bytes 4956160 | tf_op jit(solution)/shard_map/reduce_scatter | solution.py:466
  4388.5 590.2 %reduce-scatter.53.cloned.1.call-start = ((), (), s32[]{:S(2)}) async-start(), calls=%async_computation.30 | async-start | bytes 7208960 | tf_op jit(solution)/shard_map/reduce_scatter | solution.py:481
  4393.8 724.9 %reduce-scatter.41.cloned.1.call-start = ((), (), s32[]{:S(2)}) async-start(), calls=%async_computation.24 | async-start | bytes 9912320 | tf_op jit(solution)/shard_map/reduce_scatter | solution.py:463
  4403.8 1006.3 %reduce-scatter.59.cloned.1.call-start = ((), (), s32[]{:S(2)}) async-start(), calls=%async_computation.33 | async-start | bytes 21626880 | tf_op jit(solution)/shard_map/reduce_scatter | solution.py:487
  4419.9 1282.1 %reduce-scatter.63.cloned.1.call-start = ((), (), s32[]{:S(2)}) async-start(), calls=%async_computation.35 | async-start | bytes 21626880 | tf_op jit(solution)/shard_map/reduce_scatter | solution.py:490
  4437.0 1321.0 %reduce-scatter.69.cloned.1.call-start = ((), (), s32[]{:S(2)}) async-start(), calls=%async_computation.38 | async-start | bytes 4866048
  4499.4 1304.1 %reduce-scatter.71.cloned.1.call-start = ((), (), s32[]{:S(2)}) async-start(), calls=%async_computation.39 | async-start | bytes 2433024
  4573.5 1275.6 %reduce-scatter.77.cloned.1.call-start = ((), (), s32[]{:S(2)}) async-start(), calls=%async_computation.42 | async-start | bytes 2433024
  4649.2 1245.3 %reduce-scatter.75.cloned.1.call-start = ((), (), s32[]{:S(2)}) async-start(), calls=%async_computation.41 | async-start | bytes 2433024
  4725.1 1215.2 %reduce-scatter.73.cloned.1.call-start = ((), (), s32[]{:S(2)}) async-start(), calls=%async_computation.40 | async-start | bytes 2433024
  4800.8 1184.8 %reduce-scatter.67.cloned.1.call-start = ((), (), s32[]{:S(2)}) async-start(), calls=%async_computation.37 | async-start | bytes 2433024
  4876.7 1158.1 %reduce-scatter.55.cloned.1.call-start = ((), (), s32[]{:S(2)}) async-start(), calls=%async_computation.31 | async-start | bytes 3244032 | tf_op jit(solution)/shard_map/reduce_scatter | solution.py:501
  4982.0 1108.8 %reduce-scatter.65.cloned.1.call-start = ((), (), s32[]{:S(2)}) async-start(), calls=%async_computation.36 | async-start | bytes 4866048
  5123.0 1044.3 %reduce-scatter.61.cloned.1.call-start = ((), (), s32[]{:S(2)}) async-start(), calls=%async_computation.34 | async-start | bytes 9732096 | tf_op jit(solution)/shard_map/reduce_scatter | solution.py:503
  5416.8 827.4 %reduce-scatter.79.cloned.1.call-start = ((), (), s32[]{:S(2)}) async-start(), calls=%async_computation.43 | async-start | bytes 9732096
  (302 other events, 13517.2 us)
Sparse Core Ops, SparseCore 0:
  106.9 76.9 all-gather.36
  185.4 140.7 all-gather.34
  327.5 140.3 all-gather.40
  470.1 75.1 all-gather.44
  547.2 41.1 all-gather.62
  590.4 36.6 all-gather.58
  628.4 106.2 all-gather.54
  736.3 80.0 all-gather.42
  817.8 57.6 all-gather.46
  877.7 75.6 all-gather.48
  954.8 75.5 all-gather.50
  1031.8 75.5 all-gather.56
  1108.9 295.4 all-gather.64
  1405.8 295.9 all-gather.60
  2040.4 55.3 reduce-scatter.80
  2098.1 56.0 reduce-scatter.82
  2269.5 76.9 all-gather.36
  2347.9 140.6 all-gather.34
  2490.1 140.3 all-gather.40
  2632.6 75.1 all-gather.44
  2709.8 41.1 all-gather.62
  2752.7 36.6 all-gather.58
  2791.0 106.2 all-gather.54
  2898.9 80.0 all-gather.42
  2980.4 57.6 all-gather.46
  3040.3 75.6 all-gather.48
  3117.5 75.5 all-gather.50
  3194.5 75.5 all-gather.56
  3271.6 295.4 all-gather.64
  3568.7 295.9 all-gather.60
  4203.5 55.3 reduce-scatter.80
  4261.1 56.0 reduce-scatter.82
  (10 shorter events, 255.7 us)
Sparse Core Ops, SparseCore 1:
  4358.0 137.1 reduce-scatter.44
  4497.2 73.6 reduce-scatter.46
  4573.0 73.4 reduce-scatter.56
  4648.9 73.4 reduce-scatter.50
  4724.7 73.4 reduce-scatter.48
  4800.5 73.4 reduce-scatter.42
  4876.2 102.5 reduce-scatter.52
  4980.9 137.7 reduce-scatter.40
  5121.0 289.1 reduce-scatter.58
  5412.5 289.4 reduce-scatter.62
  5705.2 52.7 reduce-scatter.68
  5761.9 41.5 reduce-scatter.70
  5807.6 41.4 reduce-scatter.76
  5853.0 41.4 reduce-scatter.74
  5898.8 41.4 reduce-scatter.72
  5944.2 41.4 reduce-scatter.66
  5990.0 44.7 reduce-scatter.54
  6038.8 51.9 reduce-scatter.64
  6094.7 72.5 reduce-scatter.60
  6171.8 72.4 reduce-scatter.78
where the time goes:
time: 6280 us; the launch traced here: 6250 us
  waiting for transfers between devices  4450 us (71%)
  matrix products  1010 us (16%)
  local copies, waits for them, and re-layouts  341 us (5%)
  blocking collectives  290 us (5%)
  other arithmetic  126 us (2%)
    all_gather x4, waiting for transfers between devices, fetch(): lax.all_gather(as_sent(wide[3]), 'seq', axis=0, tiled=True)  715 us
    all_gather x4, waiting for transfers between devices, fetch(): lax.all_gather(as_sent(wide[4]), 'seq', axis=0, tiled=True)  569 us
    all_gather x4, waiting for transfers between devices, fetch(): lax.all_gather(as_sent(wide[0]), 'seq', axis=0, tiled=True)  416 us
    all_gather x4, waiting for transfers between devices, fetch(): lax.all_gather(as_sent(wide[1]), 'seq', axis=0, tiled=True)  368 us
    unnamed x28, waiting for transfers between devices  365 us
    reduce_scatter x1, waiting for transfers between devices, on_device(): lax.psum_scatter(terms[8].astype(jnp.bfloat16), 'seq', scatter_dimension=...  287 us
    reduce_scatter x1, waiting for transfers between devices, on_device(): lax.psum_scatter(terms[9].astype(jnp.bfloat16), 'seq', scatter_dimension=...  285 us
    all_gather x4, waiting for transfers between devices, fetch(): lax.all_gather(as_sent(wide[2]), 'seq', axis=0, tiled=True)  280 us
  transfers between devices with their start and end apart: 62, of which 52 were waited for; matrix products, arithmetic and copies ran while one was open for 16% of the time, Pallas kernels for 0%

commit v1 on v0

v1 whole, which is shorter than its diff:
```python
import functools
import math

import jax
import jax.numpy as jnp
from jax import lax
from jax.experimental import pallas as pl
from jax.experimental.pallas import tpu as pltpu
from jax.sharding import Mesh
from jax.sharding import PartitionSpec as P

H = 16
HD = 88
GRID = 32
PAIR = 2 * HD

epsilon = 1e-06
SCALE = HD ** (-0.5)
SCALE_LOG2 = SCALE * math.log2(math.e)

f32 = jnp.float32
bf16 = jnp.bfloat16


def normalize(values, axis):
    center = values - jnp.mean(values, axis=axis, keepdims=True)
    spread = jnp.mean(center * center, axis=axis, keepdims=True)
    return center * lax.rsqrt(spread + epsilon)


def norm_gain(values, gain_vec):
    return normalize(values, 0) * gain_vec[:, None]


def shifted_norm(values, gain_vec, offset):
    return normalize(values, 0) * gain_vec[:, None] + offset[:, None]


def norm_gain_rows(values, gain_vec):
    return normalize(values, -1) * gain_vec


def gelu_tanh(values):
    return jax.nn.gelu(values, approximate=True)


def head_norm(flat):
    return normalize(flat.reshape(H, HD, flat.shape[-1]), 1).reshape(flat.shape)


def rotate(per_head, tables):
    row_cos, row_sin, col_cos, col_sin = tables
    quarter = per_head.shape[1] // 4
    part_one = per_head[:, :quarter]
    part_two = per_head[:, quarter : 2 * quarter]
    part_three = per_head[:, 2 * quarter : 3 * quarter]
    part_four = per_head[:, 3 * quarter :]
    return jnp.concatenate(
        [
            part_one * row_cos - part_two * row_sin,
            part_two * row_cos + part_one * row_sin,
            part_three * col_cos - part_four * col_sin,
            part_four * col_cos + part_three * col_sin,
        ],
        axis=1,
    )


def dot(a, b, dims=((1,), (0,))):
    return lax.dot_general(a, b, (dims, ((), ())), preferred_element_type=f32)


NN = ((1,), (0,))
TN = ((0,), (0,))
NT = ((1,), (1,))


def heads_of(ref):
    pair = ref[...].astype(f32)
    return pair[:HD].astype(bf16), pair[HD:].astype(bf16)


def attend_kernel(blocks, *refs):
    q_ref = refs[0]
    k_refs = refs[1 : 1 + blocks]
    v_refs = refs[1 + blocks : 1 + 2 * blocks]
    o_ref, inv_ref = refs[1 + 2 * blocks :]
    q_heads = heads_of(q_ref)
    k_heads = [heads_of(r) for r in k_refs]
    v_heads = [heads_of(r) for r in v_refs]
    for i in range(2):
        total = None
        summed = None
        for k_pair, v_pair in zip(k_heads, v_heads):
            scores = dot(k_pair[i], q_heads[i], TN)
            probs = jnp.exp2(scores * SCALE_LOG2)
            part_sum = jnp.sum(probs, axis=0, keepdims=True)
            part = dot(v_pair[i], probs.astype(bf16), NN)
            total = part if total is None else total + part
            summed = part_sum if summed is None else summed + part_sum
        inverse = 1.0 / summed
        o_ref[i * HD : (i + 1) * HD, :] = total * inverse
        inv_ref[0, i : i + 1, :] = inverse


def attend(query, keys, values):
    blocks = len(keys)
    tokens = query.shape[1]
    per_key = keys[0].shape[1]
    spec_q = pl.BlockSpec((PAIR, tokens), lambda h: (h, 0))
    spec_k = pl.BlockSpec((PAIR, per_key), lambda h: (h, 0))
    return pl.pallas_call(
        functools.partial(attend_kernel, blocks),
        grid=(H // 2,),
        in_specs=[spec_q] + [spec_k] * (2 * blocks),
        out_specs=[spec_q, pl.BlockSpec((1, 2, tokens), lambda h: (h, 0, 0))],
        out_shape=[
            jax.ShapeDtypeStruct((H * HD, tokens), f32),
            jax.ShapeDtypeStruct((H // 2, 2, tokens), f32),
        ],
        compiler_params=pltpu.CompilerParams(vmem_limit_bytes=48 * 2**20),
        cost_estimate=pl.CostEstimate(
            flops=2 * 2 * H * 128 * tokens * per_key * blocks,
            bytes_accessed=2 * H * HD * (3 * tokens + 2 * per_key * blocks),
            transcendentals=H * tokens * per_key * blocks,
        ),
        name="attend",
    )(query, *keys, *values)


def attend_back_kernel(blocks, *refs):
    q_ref, g_ref, o_ref, inv_ref = refs[:4]
    k_refs = refs[4 : 4 + blocks]
    v_refs = refs[4 + blocks : 4 + 2 * blocks]
    dq_ref = refs[4 + 2 * blocks]
    dk_refs = refs[5 + 2 * blocks : 5 + 3 * blocks]
    dv_refs = refs[5 + 3 * blocks : 5 + 4 * blocks]
    q_heads = heads_of(q_ref)
    g_heads = heads_of(g_ref)
    gated = g_ref[...].astype(f32) * o_ref[...].astype(f32)
    k_heads = [heads_of(r) for r in k_refs]
    v_heads = [heads_of(r) for r in v_refs]
    for i in range(2):
        rows = slice(i * HD, (i + 1) * HD)
        row_dot = jnp.sum(gated[rows], axis=0, keepdims=True)
        inverse = inv_ref[0, i : i + 1, :]
        grad_q = None
        for b in range(blocks):
            k_one, v_one = k_heads[b][i], v_heads[b][i]
            scores = dot(k_one, q_heads[i], TN)
            exact = jnp.exp2(scores * SCALE_LOG2) * inverse
            grad_probs = dot(v_one, g_heads[i], TN)
            grad_scores = (exact * (grad_probs - row_dot)).astype(bf16)
            part = dot(k_one, grad_scores, NN)
            grad_q = part if grad_q is None else grad_q + part
            dk_refs[b][rows, :] = (dot(q_heads[i], grad_scores, NT) * SCALE).astype(
                dk_refs[b].dtype
            )
            dv_refs[b][rows, :] = dot(g_heads[i], exact.astype(bf16), NT).astype(dv_refs[b].dtype)
        dq_ref[rows, :] = grad_q * SCALE


def attend_back(query, grad, out, inverse, keys, values):
    blocks = len(keys)
    tokens = query.shape[1]
    per_key = keys[0].shape[1]
    spec_q = pl.BlockSpec((PAIR, tokens), lambda h: (h, 0))
    spec_k = pl.BlockSpec((PAIR, per_key), lambda h: (h, 0))
    shape_k = jax.ShapeDtypeStruct((H * HD, per_key), f32)
    outs = pl.pallas_call(
        functools.partial(attend_back_kernel, blocks),
        grid=(H // 2,),
        in_specs=[spec_q] * 3
        + [pl.BlockSpec((1, 2, tokens), lambda h: (h, 0, 0))]
        + [spec_k] * (2 * blocks),
        out_specs=[spec_q] + [spec_k] * (2 * blocks),
        out_shape=[jax.ShapeDtypeStruct((H * HD, tokens), f32)] + [shape_k] * (2 * blocks),
        compiler_params=pltpu.CompilerParams(vmem_limit_bytes=56 * 2**20),
        cost_estimate=pl.CostEstimate(
            flops=5 * 2 * H * 128 * tokens * per_key * blocks,
            bytes_accessed=2 * H * HD * (6 * tokens + 6 * per_key * blocks),
            transcendentals=H * tokens * per_key * blocks,
        ),
        name="attend_back",
    )(query, grad, out, inverse, *keys, *values)
    return outs[0], outs[1 : 1 + blocks], outs[1 + blocks :]


def assemble_kernel(heights, layout, *refs):
    count = len(layout)
    place_ref = refs[0]
    pieces = refs[1 : 1 + count]
    wholes = refs[1 + count : 1 + count + len(heights)]
    held = refs[1 + count + len(heights) : -2]
    sem_in, sem_out = refs[-2:]
    loads = [
        pltpu.make_async_copy(piece, room, sem_in.at[i])
        for i, (piece, room) in enumerate(zip(pieces, held))
    ]
    for load in loads:
        load.start()
    stores = []
    for load, room, (rank, low, high) in zip(loads, held, layout):
        load.wait()
        top = 0
        for height, whole in zip(heights, wholes):
            begin, end = max(low, top), min(high, top + height)
            if begin < end:
                row = pl.multiple_of(place_ref[rank] * height, 16) + (begin - top)
                store = pltpu.make_async_copy(
                    room.at[pl.ds(begin - low, end - begin)],
                    whole.at[pl.ds(row, end - begin)],
                    sem_out.at[len(stores)],
                )
                store.start()
                stores.append(store)
            top += height
    for store in stores:
        store.wait()


def assemble(pieces, layout, heights, places):
    width = pieces[0].shape[1]
    total = sum(heights)
    return pl.pallas_call(
        functools.partial(assemble_kernel, heights, layout),
        in_specs=[pl.BlockSpec(memory_space=pltpu.SMEM)]
        + [pl.BlockSpec(memory_space=pl.ANY)] * len(pieces),
        out_specs=[pl.BlockSpec(memory_space=pl.ANY)] * len(heights),
        out_shape=[jax.ShapeDtypeStruct((8 * height, width), bf16) for height in heights],
        scratch_shapes=[pltpu.VMEM(piece.shape, bf16) for piece in pieces]
        + [
            pltpu.SemaphoreType.DMA((len(pieces),)),
            pltpu.SemaphoreType.DMA((len(pieces) * len(heights),)),
        ],
        compiler_params=pltpu.CompilerParams(vmem_limit_bytes=24 * 2**20),
        cost_estimate=pl.CostEstimate(
            flops=0, bytes_accessed=2 * 2 * 8 * total * width, transcendentals=0
        ),
        name="assemble",
    )(places, *pieces)


def outer_kernel(place_ref, dy_ref, dy_other_ref, x_ref, x_other_ref, out_ref):
    out_ref[...] = (
        dot(dy_ref[...], x_ref[...], NT) + dot(dy_other_ref[...], x_other_ref[...], NT)
    ).astype(bf16)


def outer_blocks(places, dy_pair, x_pair, blocks):
    height = dy_pair[0].shape[0] // blocks
    tokens = dy_pair[0].shape[1]
    width = x_pair[0].shape[0]
    count = places.shape[0]
    spec_dy = pl.BlockSpec((height, tokens), lambda i, place: (place[i], 0))
    spec_x = pl.BlockSpec((width, tokens), lambda i, place: (0, 0))
    return pl.pallas_call(
        outer_kernel,
        grid_spec=pltpu.PrefetchScalarGridSpec(
            num_scalar_prefetch=1,
            grid=(count,),
            in_specs=[spec_dy, spec_dy, spec_x, spec_x],
            out_specs=pl.BlockSpec((height, width), lambda i, place: (i, 0)),
        ),
        out_shape=jax.ShapeDtypeStruct((count * height, width), bf16),
        compiler_params=pltpu.CompilerParams(vmem_limit_bytes=56 * 2**20),
        cost_estimate=pl.CostEstimate(
            flops=2 * 2 * count * height * width * tokens,
            bytes_accessed=2 * (2 * tokens * (count * height + width) + count * height * width),
            transcendentals=0,
        ),
        name="outer_blocks",
    )(places, *dy_pair, *x_pair)


def after(value, *others):
    return lax.optimization_barrier((value,) + others)[0]


SWAP = ((0, 1), (1, 0))


def swap(values, axis):
    return lax.ppermute(values, axis, SWAP)


def on_device(
    sizes,
    inputs,
    skipped,
    text_rows,
    condition,
    cotangent,
    norm_gains,
    skip_weight,
    shift_weight,
    query_key_weight,
    value_weight,
    self_output,
    cross_query,
    cross_memory,
    cross_output,
    up_weight,
    down_weight,
):
    outer, inner, cores, seq = sizes
    plane = outer * inner
    square = outer == 2 and inner == 2
    lat_count, local_rows, width = inputs.shape
    text_local = text_rows.shape[1]
    at_a = lax.axis_index("a")
    at_b = lax.axis_index("b")
    at_c = lax.axis_index("c")
    at_z = lax.axis_index("z")
    tokens = lat_count * local_rows

    def route(step):
        return [
            (
                core * seq + z,
                (z // lat_count) * seq + core * lat_count + (z % lat_count + step) % lat_count,
            )
            for core in range(cores)
            for z in range(seq)
        ]

    slot = at_z % lat_count

    def to_latent(values):
        parts = []
        for step in range(lat_count):
            chosen = lax.dynamic_index_in_dim(
                values, (slot + step) % lat_count, 0, keepdims=False
            )
            parts.append(lax.ppermute(chosen, ("c", "z"), route(step)))
        return jnp.concatenate(parts, axis=0)

    def from_latent(rows):
        height = rows.shape[0] // lat_count
        parts = []
        for step in range(lat_count):
            back = [(target, source) for source, target in route(step)]
            parts.append(
                lax.ppermute(rows[step * height : (step + 1) * height], ("c", "z"), back)
            )
        stacked = jnp.stack(parts + parts)
        return lax.dynamic_slice_in_dim(stacked, (lat_count - slot) % lat_count, lat_count, 0)

    places = jnp.stack(
        [
            ((at_a + da) % outer * inner + (at_b + db) % inner) * cores + (at_c + dc) % cores
            for dc in range(2)
            for da in range(2)
            for db in range(2)
        ]
    ).astype(jnp.int32)
    here = {"a": at_a, "b": at_b, "c": at_c}

    def z_shift(values, step):
        return lax.ppermute(values, "z", [(z, (z + step) % seq) for z in range(seq)])

    def z_blocks(values):
        arrived = [values] + [z_shift(values, step) for step in range(1, seq)]
        blocks = []
        for z in range(seq):
            block = arrived[0]
            for step in range(1, seq):
                block = jnp.where(at_z == (z + step) % seq, arrived[step], block)
            blocks.append(block)
        return blocks

    def flip(shards):
        return jnp.concatenate([shard.T for shard in shards], axis=0)

    def z_gather(flipped, direct):
        if direct:
            blocks = z_blocks(flipped)
        else:
            blocks = list(lax.all_gather(flipped, "z", axis=0, tiled=False))
        return jnp.concatenate(blocks, axis=1)

    def gather_rows(values, axes):
        if not square:
            return lax.all_gather(values, axes[::-1], axis=0, tiled=True)
        for axis in axes:
            other = swap(values, axis)
            lower = here[axis] == 0
            values = jnp.concatenate(
                [jnp.where(lower, values, other), jnp.where(lower, other, values)], axis=0
            )
        return values

    def total_of(values):
        if not square:
            return lax.psum(values, ("a", "b", "c", "z"))
        for axis in ("c", "b", "a"):
            values = values + swap(values, axis)
        stride = 1
        while stride < seq:
            values = values + lax.ppermute(values, "z", [(z, z ^ stride) for z in range(seq)])
            stride *= 2
        return values

    def gather(piece, heights):
        if not square:
            starts = [sum(heights[:i]) for i in range(len(heights))]
            return [
                lax.all_gather(piece[s : s + h], ("a", "b", "c"), axis=0, tiled=True)
                for s, h in zip(starts, heights)
            ], piece
        rows = piece.shape[0]
        half = rows // 32 * 16
        over_b = swap(piece, "b")
        over_a = swap(piece, "a")
        low = swap(over_b[:half], "a")
        high = swap(over_a[half:], "b")
        mine = (piece, over_b, over_a, low, high)
        spans = ((0, 0, rows), (1, 0, rows), (2, 0, rows), (3, 0, half), (3, half, rows))
        others = tuple(swap(part, "c") for part in mine)
        layout = spans + tuple((rank + 4, begin, end) for rank, begin, end in spans)
        return assemble(mine + others, layout, heights, places), (over_a, over_b)

    def blocks_of(dy_pair, x_pair):
        if square:
            return outer_blocks(places[:4][::-1], dy_pair, x_pair, plane * cores)
        kept = []
        for dy in dy_pair:
            cube = dy.reshape(plane, cores, -1, dy.shape[1])
            kept.append(
                lax.dynamic_index_in_dim(cube, at_c, 1, keepdims=False).reshape(-1, dy.shape[1])
            )
        return (dot(kept[0], x_pair[0], NT) + dot(kept[1], x_pair[1], NT)).astype(bf16)

    def scatter(grads, direct):
        if not square:
            cubes = [grad.reshape(plane, -1, grad.shape[1]) for grad in grads]
            summed = [
                lax.psum_scatter(cube, ("a", "b"), scatter_dimension=0, tiled=True)[0]
                for cube in cubes
            ]
            return z_scatter(summed, False)
        heights = [grad.shape[0] // 4 for grad in grads]

        def rank(i):
            return jnp.concatenate(
                [grad[i * h : (i + 1) * h] for grad, h in zip(grads, heights)], axis=0
            )

        far, over_a, over_b, own = rank(0), rank(1), rank(2), rank(3)
        rows = own.shape[0]
        half = rows // 32 * 16
        low = swap(far[:half], "b")
        high = swap(far[half:], "a")
        over_a = jnp.concatenate([over_a[:half] + low, over_a[half:]], axis=0)
        over_b = jnp.concatenate([over_b[:half], over_b[half:] + high], axis=0)
        got_a = swap(over_a, "a")
        got_b = swap(over_b, "b")
        total = (own.astype(f32) + got_a.astype(f32) + got_b.astype(f32)).astype(bf16)
        starts = [sum(heights[:i]) for i in range(len(heights))]
        return z_scatter([total[s : s + h] for s, h in zip(starts, heights)], direct)

    def z_scatter(outs, direct):
        heights = [out.shape[0] for out in outs]
        joined = jnp.concatenate(outs, axis=0)
        cut = joined.reshape(joined.shape[0], seq, -1).transpose(1, 0, 2)
        if direct:
            owned = lax.dynamic_index_in_dim(cut, at_z, 0, keepdims=False).astype(f32)
            for step in range(1, seq):
                block = lax.dynamic_index_in_dim(cut, (at_z + step) % seq, 0, keepdims=False)
                owned = owned + z_shift(block, step).astype(f32)
        else:
            owned = lax.psum_scatter(cut, "z", scatter_dimension=0, tiled=True)[0].astype(f32)
        results = []
        start = 0
        for height in heights:
            results.append(owned[start : start + height].T)
            start += height
        return results

    gain_skip = norm_gains[: 2 * width]
    gain_one = norm_gains[2 * width : 3 * width]
    gain_two = norm_gains[3 * width : 4 * width]
    gain_three = norm_gains[4 * width :]

    skip_piece = z_gather(flip([skip_weight]), True)
    pair_piece = z_gather(
        after(flip([query_key_weight, value_weight, shift_weight]), skip_piece), True
    )
    self_piece = z_gather(
        after(flip([self_output, cross_query, cross_output]), skip_piece), False
    )
    chip_in = to_latent(after(inputs, pair_piece))
    chip_skip = to_latent(after(skipped, pair_piece))
    memory_piece = z_gather(after(flip([cross_memory]), chip_skip), True)
    up_piece = z_gather(after(flip([up_weight]), pair_piece, self_piece), False)
    chip_text = to_latent(after(text_rows, memory_piece)).T
    down_piece = z_gather(after(flip([down_weight]), up_piece), False)
    chip_grad = to_latent(after(cotangent, chip_text)).T

    (skip_t,), ready = gather(skip_piece, [skip_weight.shape[1]])
    (pair_t, value_t, shift_t), ready = gather(
        after(pair_piece, *ready),
        [query_key_weight.shape[1], value_weight.shape[1], shift_weight.shape[1]],
    )
    (self_t, cq_t, cout_t), ready = gather(
        after(self_piece, *ready),
        [self_output.shape[1], cross_query.shape[1], cross_output.shape[1]],
    )
    (memory_t,), ready = gather(after(memory_piece, *ready), [cross_memory.shape[1]])
    (up_t,), ready = gather(after(up_piece, *ready), [up_weight.shape[1]])
    (down_t,), ready = gather(after(down_piece, *ready), [down_weight.shape[1]])

    quarter = HD // 4
    frequency = jnp.power(10000.0, -jnp.arange(quarter, dtype=f32) / quarter)
    position = jnp.concatenate(
        [
            (at_c * lat_count + (slot - step) % lat_count) * local_rows
            + jnp.arange(local_rows, dtype=jnp.int32)
            for step in range(lat_count)
        ]
    )
    row_angle = (position // GRID).astype(f32)[None, :] * frequency[:, None]
    col_angle = (position % GRID).astype(f32)[None, :] * frequency[:, None]
    tables = (jnp.cos(row_angle), jnp.sin(row_angle), jnp.cos(col_angle), jnp.sin(col_angle))

    def prepare(flat):
        cube = flat.reshape(H, HD, flat.shape[-1])
        return rotate(normalize(cube, 1), tables).reshape(flat.shape)

    cond_pair = (condition, swap(condition, "c"))
    same_core = at_z // lat_count == at_c
    cond_two = jnp.where(same_core, cond_pair[0], cond_pair[1])
    chip_cond = lax.dynamic_index_in_dim(cond_two, slot, 0, keepdims=False)
    shift = dot(shift_t, jax.nn.silu(chip_cond.astype(f32)).astype(bf16)[:, None], NN)[:, 0]

    joined = jnp.concatenate([chip_in.T, chip_skip.T], axis=0).astype(f32)
    level_zero = norm_gain(joined, gain_skip).astype(bf16)
    stream_zero = dot(skip_t, level_zero)
    level_one = shifted_norm(stream_zero, gain_one, shift).astype(bf16)
    pair_proj = dot(pair_t, level_one)
    value_proj = dot(value_t, level_one).astype(bf16)
    query_flat = pair_proj[:width]
    key_flat = pair_proj[width:]
    query = prepare(query_flat).astype(bf16)
    key = prepare(key_flat).astype(bf16)
    keys = [key, swap(key, "c")]
    values = [value_proj, swap(value_proj, "c")]
    attended, self_inverse = attend(query, keys, values)
    attended = attended.astype(bf16)
    stream_one = stream_zero + dot(self_t, attended)
    level_two = norm_gain(stream_one, gain_two).astype(bf16)
    cross_proj = dot(cq_t, level_two)
    cross = head_norm(cross_proj).astype(bf16)
    memory_proj = dot(memory_t, chip_text)
    memory_key_flat = memory_proj[:width]
    memory_key = head_norm(memory_key_flat).astype(bf16)
    memory_value = memory_proj[width:].astype(bf16)
    text_keys = [memory_key, swap(memory_key, "c")]
    text_values = [memory_value, swap(memory_value, "c")]
    crossed, cross_inverse = attend(cross, text_keys, text_values)
    crossed = crossed.astype(bf16)
    stream_two = stream_one + dot(cout_t, crossed)
    level_three = norm_gain(stream_two, gain_three).astype(bf16)
    hidden = dot(up_t, level_three)
    activated = gelu_tanh(hidden).astype(bf16)
    blended = (stream_two + dot(down_t, activated)).astype(bf16)
    blended_out = from_latent(blended.T)

    def with_other(values):
        return values, swap(values, "c")

    zero_pair = with_other(level_zero)
    one_pair = with_other(level_one)
    attended_pair = with_other(attended)
    two_pair = with_other(level_two)
    text_pair = with_other(chip_text)
    crossed_pair = with_other(crossed)
    three_pair = with_other(level_three)
    activated_pair = with_other(activated)

    down_blocks = blocks_of(with_other(chip_grad), activated_pair)
    (grad_down,) = scatter([down_blocks], False)
    grad_act = dot(down_t, chip_grad, TN)
    _, gelu_pull = jax.vjp(gelu_tanh, hidden)
    grad_hidden = gelu_pull(grad_act)[0].astype(bf16)
    up_blocks = blocks_of(with_other(grad_hidden), three_pair)
    (grad_up,) = scatter([up_blocks], False)
    grad_level_three = dot(up_t, after(grad_hidden, down_blocks), TN)
    _, pull_three = jax.vjp(norm_gain, stream_two, gain_three)
    grad_from_three, grad_gain_three = pull_three(grad_level_three)
    grad_stream_two = chip_grad.astype(f32) + grad_from_three
    cross_back = grad_stream_two.astype(bf16)
    grad_crossed = dot(cout_t, after(cross_back, up_blocks), TN).astype(bf16)
    grad_cross, grad_tk, grad_tv = attend_back(
        cross, grad_crossed, crossed, cross_inverse, text_keys, text_values
    )
    grad_memory_key = grad_tk[0] + swap(grad_tk[1].astype(bf16), "c").astype(f32)
    grad_memory_value = grad_tv[0] + swap(grad_tv[1].astype(bf16), "c").astype(f32)
    _, pull_memory = jax.vjp(head_norm, memory_key_flat)
    grad_memory_proj = jnp.concatenate(
        [pull_memory(grad_memory_key)[0], grad_memory_value], axis=0
    ).astype(bf16)
    grad_text_rows = dot(grad_memory_proj, memory_t, TN).astype(bf16)
    grad_text = from_latent(grad_text_rows).astype(f32)
    _, pull_cq = jax.vjp(head_norm, cross_proj)
    grad_cq_flat = pull_cq(grad_cross)[0].astype(bf16)
    grad_level_two = dot(cq_t, grad_cq_flat, TN)
    _, pull_two = jax.vjp(norm_gain, stream_one, gain_two)
    grad_from_two, grad_gain_two = pull_two(grad_level_two)
    grad_stream_one = grad_stream_two + grad_from_two
    self_back = grad_stream_one.astype(bf16)
    grad_attended = dot(self_t, self_back, TN).astype(bf16)
    grad_q, grad_k, grad_v = attend_back(
        query, grad_attended, attended, self_inverse, keys, values
    )
    grad_key = grad_k[0] + swap(grad_k[1].astype(bf16), "c").astype(f32)
    grad_value_proj = (grad_v[0] + swap(grad_v[1].astype(bf16), "c").astype(f32)).astype(bf16)
    _, pull_query = jax.vjp(prepare, query_flat)
    _, pull_key = jax.vjp(prepare, key_flat)
    grad_pair_proj = jnp.concatenate([pull_query(grad_q)[0], pull_key(grad_key)[0]], axis=0).astype(
        bf16
    )
    grad_level_one = dot(pair_t, grad_pair_proj, TN) + dot(value_t, grad_value_proj, TN)
    _, pull_one = jax.vjp(shifted_norm, stream_zero, gain_one, shift)
    grad_from_one, grad_gain_one, grad_shift_part = pull_one(grad_level_one)
    skip_back = (grad_stream_one + grad_from_one).astype(bf16)

    (grad_memory,) = scatter([blocks_of(with_other(grad_memory_proj), text_pair)], True)
    grad_cout, grad_cq, grad_self = scatter(
        [
            blocks_of(with_other(cross_back), crossed_pair),
            blocks_of(with_other(grad_cq_flat), two_pair),
            blocks_of(with_other(self_back), attended_pair),
        ],
        False,
    )
    grad_pair, grad_value = scatter(
        [
            blocks_of(with_other(grad_pair_proj), one_pair),
            blocks_of(with_other(grad_value_proj), one_pair),
        ],
        False,
    )
    (grad_skip_w,) = scatter([blocks_of(with_other(skip_back), zero_pair)], True)

    cond_act = jax.nn.silu(gather_rows(condition, ("c", "b", "a")).astype(f32)).astype(bf16)
    block_in, block_out = shift_weight.shape
    cond_block = lax.dynamic_slice_in_dim(cond_act, at_z * block_in, block_in, 1).astype(f32)
    shift_latent = grad_shift_part + swap(grad_shift_part, "c")
    shift_column = jnp.concatenate(z_blocks(shift_latent[None, :]), axis=0)
    shift_grads = gather_rows(shift_column, ("b", "a"))
    own_columns = ((at_a * inner + at_b) * cores + at_c) * block_out
    grad_shift = jnp.dot(
        cond_block.T,
        lax.dynamic_slice_in_dim(shift_grads, own_columns, block_out, 1),
        precision=lax.Precision.HIGHEST,
    )

    skip_back_rows = from_latent(skip_back.T).reshape(tokens, width)
    grad_level_zero = dot(skip_back_rows, skip_t, NN)
    joined_rows = jnp.concatenate([inputs, skipped], axis=-1).astype(f32).reshape(tokens, -1)
    _, pull_zero = jax.vjp(norm_gain_rows, joined_rows, gain_skip)
    grad_joined, grad_gain_skip = pull_zero(grad_level_zero)
    grad_input = grad_joined[:, :width].reshape(inputs.shape)
    grad_skipped = grad_joined[:, width:].reshape(inputs.shape)
    grad_gains = total_of(
        jnp.concatenate([grad_gain_skip, grad_gain_one, grad_gain_two, grad_gain_three])
    )
    return (
        blended_out,
        grad_input,
        grad_skipped,
        grad_text,
        grad_gains,
        grad_skip_w,
        grad_shift,
        grad_pair,
        grad_value,
        grad_self,
        grad_cq,
        grad_memory,
        grad_cout,
        grad_up,
        grad_down,
    )


def solution(mesh):
    dp, seq = mesh.shape["dp"], mesh.shape["seq"]
    inner, cores = 2, 2
    sizes = (dp // (inner * cores), inner, cores, seq)
    split = Mesh(mesh.devices.reshape(sizes), ("a", "b", "c", "z"))
    rows = P(("a", "b", "c"), "z", None)
    blocks = P("z", ("a", "b", "c"))
    return jax.shard_map(
        functools.partial(on_device, sizes),
        mesh=split,
        in_specs=(rows, rows, rows, P(("a", "b", "c"), None), rows, P()) + (blocks,) * 10,
        out_specs=(rows, rows, rows, rows, P()) + (blocks,) * 10,
        check_vma=False,
    )
```

time: 6280 us -> 1480 us (0.24)
  waiting for transfers between devices: 4450 us -> 555 us
  matrix products: 1010 us -> 148 us
  blocking collectives: 290 us -> 0 us
  Pallas kernels: 0 us -> 208 us
  starting transfers between devices: 4.39 us -> 175 us
  local copies, waits for them, and re-layouts: 341 us -> 185 us
    all_gather x34 -> x3, waiting for transfers between devices: 2600 us -> 0.02 us  [z_gather(): blocks = list(lax.all_gather(flipped, 'z', axis=0, tiled=False))]
    reduce_scatter x20 -> x4, waiting for transfers between devices: 1480 us -> 0.01 us  [z_scatter(): lax.psum_scatter(cut, 'z', scatter_dimension=0, tiled=True)[0].astype(f32)]
    dot_general x496 -> x20, matrix products: 1010 us -> 148 us  [the longest x19 146 us: dot(): return lax.dot_general(a, b, (dims, ((), ())), preferred_element_type=f32)]
    ppermute x0 -> x146, waiting for transfers between devices: none -> 555 us  [the longest x112 322 us: swap(): return lax.ppermute(values, axis, SWAP)]
    unnamed x28 -> x7, waiting for transfers between devices: 365 us -> 0.12 us
    all_gather x14 -> x0, blocking collectives: 249 us -> none  [the longest x2 56.6 us: forward_pass(): lax.all_gather(memory_value, 'seq', axis=1, tiled=True)]
    pallas_call x0 -> x19, Pallas kernels: none -> 208 us  [the longest x9 98.8 us: outer_blocks(): pl.pallas_call(outer_kernel, grid_spec=pltpu.PrefetchScalarGridSpec(num_s...]
    ppermute x0 -> x146, starting transfers between devices: none -> 174 us  [the longest x112 89.5 us: swap(): return lax.ppermute(values, axis, SWAP)]
  transfers between devices with their start and end apart: 62 -> 153, of which waited for: 52 -> 43; matrix products, arithmetic and copies ran while one was open for 16% -> 28% of each run, Pallas kernels for 0% -> 14%
where the time goes in v1:
time: 1480 us; the launch traced here: 1460 us
  waiting for transfers between devices  555 us (38%)
  Pallas kernels  208 us (14%)
  local copies, waits for them, and re-layouts  185 us (12%)
  starting transfers between devices  175 us (12%)
  other arithmetic  173 us (12%)
  matrix products  148 us (10%)
  between operations  17.5 us (1%)
    ppermute x112, waiting for transfers between devices, swap(): return lax.ppermute(values, axis, SWAP)  322 us
    dot_general x19, matrix products, dot(): return lax.dot_general(a, b, (dims, ((), ())), preferred_element_type=f32)  146 us
    ppermute x18, waiting for transfers between devices, z_shift(): lax.ppermute(values, 'z', [(z, (z + step) % seq) for z in range(seq)])  114 us
    pallas_call x9, Pallas kernels, outer_blocks(): pl.pallas_call(outer_kernel, grid_spec=pltpu.PrefetchScalarGridSpec(num_s...  98.8 us
    ppermute x8, waiting for transfers between devices, to_latent(): parts.append(lax.ppermute(chosen, ('c', 'z'), route(step)))  95.3 us
    ppermute x112, starting transfers between devices, swap(): return lax.ppermute(values, axis, SWAP)  89.5 us
    pallas_call x6, Pallas kernels, assemble(): pl.pallas_call(functools.partial(assemble_kernel, heights, layout), in_sp...  49.2 us
    unnamed x388, local copies, waits for them, and re-layouts  49.1 us
  transfers between devices with their start and end apart: 153, of which 43 were waited for; matrix products, arithmetic and copies ran while one was open for 28% of the time, Pallas kernels for 14%

profile of v1, /device:TPU:0, one launch (start us, length us, event | category | flops | bytes accessed | tf_op | source)
XLA Modules:
  0.0 1462.5 jit_solution(16527663705197567863)
XLA Ops:
  19.6 16.0 %collective-permute-done.1 = bf16[176,704]{1,0:T(8,128)(2,1)S(1)} collective-permute-done((bf16[176,704]{1,0:T(8,128)(2,1)}, bf16[176,704]{1,0:T(8,128)(2,1)S(1)}, u32[]{:S(2)}, u32[]{:S(2)}) %collective-permute-start.1) | collective-permute-done | bytes 247840 | tf_op jit(solution)/shard_map/ppermute | solution.py:360
  50.6 35.9 %collective-permute-done.13 = bf16[704,352]{1,0:T(8,128)(2,1)S(1)} collective-permute-done((bf16[704,352]{1,0:T(8,128)(2,1)S(1)}, bf16[704,352]{1,0:T(8,128)(2,1)S(1)}, u32[]{:S(2)}, u32[]{:S(2)}) %collective-permute-start.13) | collective-permute-done | bytes 495648 | tf_op jit(solution)/shard_map/ppermute | solution.py:360
  111.0 46.5 %collective-permute-done.18 = bf16[256,1408]{0,1:T(8,128)(2,1)} collective-permute-done((bf16[256,1408]{0,1:T(8,128)(2,1)}, bf16[256,1408]{0,1:T(8,128)(2,1)}, u32[]{:S(2)}, u32[]{:S(2)}) %collective-permute-start.18) | collective-permute-done | bytes 720928 | tf_op jit(solution)/shard_map/ppermute | solution.py:335
  166.1 10.9 collective-permute-done.41
  263.5 46.7 %collective-permute-done.77 = bf16[256,1408]{0,1:T(8,128)(2,1)S(1)} collective-permute-done((bf16[256,1408]{0,1:T(8,128)(2,1)}, bf16[256,1408]{0,1:T(8,128)(2,1)S(1)}, u32[]{:S(2)}, u32[]{:S(2)}) %collective-permute-start.77) | collective-permute-done | bytes 720928 | tf_op jit(solution)/shard_map/ppermute | solution.py:335
  403.3 47.1 %collective-permute-done.24.refs_5_ = bf16[272,1408]{1,0:T(8,128)(2,1)} collective-permute-done((bf16[272,1408]{1,0:T(8,128)(2,1)S(1)}, bf16[272,1408]{1,0:T(8,128)(2,1)}, u32[]{:S(2)}, u32[]{:S(2)}) %collective-permute-start.24) | collective-permute-done | bytes 765984 | tf_op jit(solution)/shard_map/ppermute | solution.py:284
  484.8 15.1 %collective-permute-done.57.refs_3_ = bf16[768,1408]{1,0:T(8,128)(2,1)} collective-permute-done((bf16[768,1408]{1,0:T(8,128)(2,1)S(1)}, bf16[768,1408]{1,0:T(8,128)(2,1)}, u32[]{:S(2)}, u32[]{:S(2)}) %collective-permute-start.57) | collective-permute-done | bytes 2162720 | tf_op jit(solution)/shard_map/ppermute | solution.py:284
  502.0 12.5 attend.2
  527.7 18.4 %collective-permute-done.59.refs_5_ = bf16[384,1408]{1,0:T(8,128)(2,1)} collective-permute-done((bf16[384,1408]{1,0:T(8,128)(2,1)S(1)}, bf16[384,1408]{1,0:T(8,128)(2,1)}, u32[]{:S(2)}, u32[]{:S(2)}) %collective-permute-start.59) | collective-permute-done | bytes 1081376 | tf_op jit(solution)/shard_map/ppermute | solution.py:284
  547.6 24.9 %collective-permute-done.66.refs_3_ = bf16[176,6144]{1,0:T(8,128)(2,1)S(1)} collective-permute-done((bf16[176,6144]{1,0:T(8,128)(2,1)}, bf16[176,6144]{1,0:T(8,128)(2,1)S(1)}, u32[]{:S(2)}, u32[]{:S(2)}) %collective-permute-start.66) | collective-permute-done | bytes 2162720 | tf_op jit(solution)/shard_map/ppermute | solution.py:284
  622.1 12.4 assemble.10
  643.0 16.5 %fusion.116 = f32[6144,512]{1,0:T(8,128)} fusion(bf16[1408,6144]{1,0:T(8,128)(2,1)} %assemble.11, bf16[512,1408]{0,1:T(8,128)(2,1)S(1)} %copy-done.51), kind=kOutput, calls=%fused_computation.398 | convolution fusion | flops 8858370048 | bytes 31326208 | tf_op jit(solution)/shard_map/dot_general | solution.py:70
  659.6 26.4 %fusion.6 = (bf16[6144,512]{1,0:T(8,128)(2,1)}, bf16[6144,512]{1,0:T(8,128)(2,1)}) fusion(f32[6144,512]{1,0:T(8,128)} %fusion.116, bf16[6144,1408]{1,0:T(8,128)(2,1)} %assemble.10, bf16[1408,512]{1,0:T(8,128)(2,1)S(1)} %copy-done.96), kind=kOutput, calls=%fused_computation.8 | convolution fusion | flops 8927576064 | bytes 43909120 | tf_op jit(solution)/shard_map/dot_general | solution.py:70
  697.3 14.9 %fusion.20 = bf16[512,1408]{0,1:T(8,128)(2,1)S(1)} fusion(bf16[1408,6144]{1,0:T(8,128)(2,1)} %assemble.11, bf16[6144,512]{1,0:T(8,128)(2,1)} %get-tuple-element.134.x_ref, f32[1408,512]{1,0:T(8,128)S(1)} %copy-done.45), kind=kOutput, calls=%fused_computation.46 | convolution fusion | flops 8859811840 | bytes 27918336 | tf_op jit(solution)/shard_map/dot_general | solution.py:70
  721.6 18.3 %collective-permute-start.130 = (bf16[1024,128]{1,0:T(8,128)(2,1)}, bf16[1024,128]{1,0:T(8,128)(2,1)}, u32[]{:S(2)}, u32[]{:S(2)}) collective-permute-start(bf16[1024,128]{1,0:T(8,128)(2,1)} %fusion.66.x_ref), channel_id=1, source_target_pairs={{0,4},{4,0},{1,5},{5,1},{2,6},{6,2},{3,7},{7,3},{8,12},{12,8},{9,1... | collective-permute-start | bytes 786440 | tf_op jit(solution)/shard_map/ppermute | solution.py:284
  753.8 24.0 %outer_blocks.9 = bf16[704,6144]{1,0:T(8,128)(2,1)} custom-call(s32[4]{0:T(128)} %rev.2.place_ref, bf16[1408,512]{1,0:T(8,128)(2,1)} %bitcast.256, bf16[1408,512]{1,0:T(8,128)(2,1)} %collective-permute-done.78.dy_other_ref, bf16[6144,512]{1,0:T(8,128)(2,1)} %get-tuple-element.134.x_ref, bf16[6144,512]{1,0:T(8,128)(2,1)} %collective-permute-done.79.x_other_ref), custom_call_target="tpu_custom_call" | custom-call | flops 8858370048 | bytes 22675456 | tf_op jit(solution)/shard_map/outer_blocks/pallas_call | solution.py:257
  777.8 16.5 %multiply_reduce_fusion = (f32[1408]{0:T(1024)}, f32[512]{0:T(512)S(1)}, f32[1408,512]{1,0:T(8,128)S(1)}) fusion(f32[1408,512]{1,0:T(8,128)S(1)} %copy-done.45, f32[512]{0:T(512)S(1)} %fusion.83, f32[512]{0:T(512)S(1)} %broadcast_multiply_fusion.4, f32[1408]{0:T(1024)S(1)} %get-tuple-element.256, bf16[6144,1408]{1,0:T(8,128)(2,1)} %assemble.10, ...), kind=kOutput, calls=%fused_computation.84 | convolution fusion | flops 8863414272 | bytes 29377536 | tf_op jit(solution)/shard_map/dot_general | solution.py:70
  803.2 15.1 %outer_blocks.10 = bf16[3072,1408]{1,0:T(8,128)(2,1)} custom-call(s32[4]{0:T(128)} %rev.2.place_ref, bf16[6144,512]{1,0:T(8,128)(2,1)} %get-tuple-element.73.dy_ref, bf16[6144,512]{1,0:T(8,128)(2,1)} %collective-permute-done.80.dy_other_ref, bf16[1408,512]{1,0:T(8,128)(2,1)} %multiply_convert_fusion.1.x_ref, bf16[1408,512]{1,0:T(8,128)(2,1)} %copy-done.183), custom_call_target="tpu_custom_call" | custom-call | flops 8858370048 | bytes 17825792 | tf_op jit(solution)/shard_map/outer_blocks/pallas_call | solution.py:257
  828.3 13.3 attend_back.2
  863.2 27.5 %attend_back.3 = (f32[1408,512]{1,0:T(8,128)}, f32[1408,512]{1,0:T(8,128)}, f32[1408,512]{1,0:T(8,128)}, f32[1408,512]{1,0:T(8,128)}, f32[1408,512]{1,0:T(8,128)}) custom-call(bf16[1408,512]{1,0:T(8,128)(2,1)} %bitcast.234, bf16[1408,512]{1,0:T(8,128)(2,1)} %convolution_convert_fusion.refs_1_, bf16[1408,512]{1,0:T(8,128)(2,1)} %convert_element_type.275.refs_2_.x_ref, ...), custom_call_target="tpu_custom_call" | custom-call | flops 10737418240 | bytes 25952256 | tf_op jit(solution)/shard_map/attend_back/pallas_call | solution.py:170
  1051.0 22.9 %collective-permute-done.111 = f32[8,1408]{1,0:T(8,128)S(1)} collective-permute-done((f32[8,1408]{1,0:T(8,128)S(1)}, f32[8,1408]{1,0:T(8,128)S(1)}, u32[]{:S(2)}, u32[]{:S(2)}) %collective-permute-start.111) | collective-permute-done | bytes 45088 | tf_op jit(solution)/shard_map/ppermute | solution.py:284
  1087.2 13.0 collective-permute-done.127
  1110.5 15.3 %collective-permute-done.85 = bf16[256,1408]{0,1:T(8,128)(2,1)S(1)} collective-permute-done((bf16[256,1408]{0,1:T(8,128)(2,1)S(1)}, bf16[256,1408]{0,1:T(8,128)(2,1)S(1)}, u32[]{:S(2)}, u32[]{:S(2)}) %collective-permute-start.85) | collective-permute-done | bytes 720928 | tf_op jit(solution)/shard_map/ppermute | solution.py:344
  1131.2 11.1 fusion.19
  1143.9 17.6 %collective-permute-done.128 = bf16[528,1408]{1,0:T(8,128)(2,1)} collective-permute-done((bf16[528,1408]{1,0:T(8,128)(2,1)}, bf16[528,1408]{1,0:T(8,128)(2,1)}, u32[]{:S(2)}, u32[]{:S(2)}) %collective-permute-start.128) | collective-permute-done | bytes 1486880 | tf_op jit(solution)/shard_map/ppermute | solution.py:284
  1178.7 25.0 %collective-permute-done.91 = f32[7040]{0:T(1024)S(1)} collective-permute-done((f32[7040]{0:T(1024)S(1)}, f32[7040]{0:T(1024)S(1)}, u32[]{:S(2)}, u32[]{:S(2)}) %collective-permute-start.91) | collective-permute-done | bytes 28192 | tf_op jit(solution)/shard_map/ppermute | solution.py:284
  1228.2 13.3 outer_blocks.11
  1287.6 29.9 %collective-permute-done.115 = bf16[256,1408]{1,0:T(8,128)(2,1)} collective-permute-done((bf16[256,1408]{1,0:T(8,128)(2,1)}, bf16[256,1408]{1,0:T(8,128)(2,1)}, u32[]{:S(2)}, u32[]{:S(2)}) %collective-permute-start.115) | collective-permute-done | bytes 720928 | tf_op jit(solution)/shard_map/ppermute | solution.py:284
  1320.3 15.4 %collective-permute-done.117 = bf16[272,1408]{1,0:T(8,128)(2,1)S(1)} collective-permute-done((bf16[272,1408]{1,0:T(8,128)(2,1)S(1)}, bf16[272,1408]{1,0:T(8,128)(2,1)S(1)}, u32[]{:S(2)}, u32[]{:S(2)}) %collective-permute-start.117) | collective-permute-done | bytes 765984 | tf_op jit(solution)/shard_map/ppermute | solution.py:284
  1342.8 25.7 %collective-permute-done.116 = bf16[528,1408]{1,0:T(8,128)(2,1)S(1)} collective-permute-done((bf16[528,1408]{1,0:T(8,128)(2,1)S(1)}, bf16[528,1408]{1,0:T(8,128)(2,1)S(1)}, u32[]{:S(2)}, u32[]{:S(2)}) %collective-permute-start.116) | collective-permute-done | bytes 1486880 | tf_op jit(solution)/shard_map/ppermute | solution.py:284
  1408.7 13.6 collective-permute-done.136
  1423.1 22.4 %collective-permute-done.102 = bf16[176,704]{1,0:T(8,128)(2,1)S(1)} collective-permute-done((bf16[176,704]{1,0:T(8,128)(2,1)S(1)}, bf16[176,704]{1,0:T(8,128)(2,1)S(1)}, u32[]{:S(2)}, u32[]{:S(2)}) %collective-permute-start.102) | collective-permute-done | bytes 247840 | tf_op jit(solution)/shard_map/ppermute | solution.py:360
  (953 shorter events, 760.9 us)
Async XLA Ops:
  7.2 233.3 %all-gather.7.cloned.1.call-start = ((), (), s32[]{:S(2)}) async-start(), calls=%async_computation.8 | async-start | bytes 2027520 | tf_op jit(solution)/shard_map/all_gather | solution.py:379
  109.7 75.0 %collective-permute-start.7 = (bf16[176,2816]{1,0:T(8,128)(2,1)S(1)}, bf16[176,2816]{1,0:T(8,128)(2,1)}, u32[]{:S(2)}, u32[]{:S(2)}) collective-permute-start(bf16[176,2816]{1,0:T(8,128)(2,1)S(1)} %concatenate.186.refs_1_), channel_id=1, source_target_pairs={{0,4},{4,0},{1,5},{5,1},{2,6},{6,2},{3,7},{7,3},{8,12},{12,8},{9,1... | collective-permute-start | bytes 2973704 | tf_op jit(solution)/shard_map/ppermute | solution.py:284
  109.8 255.2 %all-gather.9.cloned.1.call-start = ((), (), s32[]{:S(2)}) async-start(), calls=%async_computation.9 | async-start | bytes 2949120 | tf_op jit(solution)/shard_map/all_gather | solution.py:379
  195.1 58.7 %collective-permute-start.19 = (bf16[704,1408]{1,0:T(8,128)(2,1)S(1)}, bf16[704,1408]{1,0:T(8,128)(2,1)}, u32[]{:S(2)}, u32[]{:S(2)}) collective-permute-start(bf16[704,1408]{1,0:T(8,128)(2,1)S(1)} %concatenate.188.refs_1_), channel_id=1, source_target_pairs={{0,16},{16,0},{1,17},{17,1},{2,18},{18,2},{3,19},{19,3},{4,20},{20... | collective-permute-start | bytes 5947400 | tf_op jit(solution)/shard_map/ppermute | solution.py:284
  246.1 235.3 %all-gather.11.cloned.1.call-start = ((), (), s32[]{:S(2)}) async-start(), calls=%async_computation.10 | async-start | bytes 2703360 | tf_op jit(solution)/shard_map/all_gather | solution.py:379
  246.4 63.8 %collective-permute-start.77 = (bf16[256,1408]{0,1:T(8,128)(2,1)}, bf16[256,1408]{0,1:T(8,128)(2,1)S(1)}, u32[]{:S(2)}, u32[]{:S(2)}) collective-permute-start(bf16[256,1408]{0,1:T(8,128)(2,1)} %bitcast.292), channel_id=1, source_target_pairs={{0,1},{1,0},{2,5},{3,4},{4,3},{5,2},{6,7},{7,6},{8,9},{9,8},{10,13... | collective-permute-start | bytes 2162696 | tf_op jit(solution)/shard_map/ppermute | solution.py:335
  372.1 1074.4 %reduce-scatter.7.cloned.1.call-start = ((), (), s32[]{:S(2)}) async-start(), calls=%async_computation.5 | async-start | bytes 2027520 | tf_op jit(solution)/shard_map/reduce_scatter | solution.py:472
  379.8 98.9 %collective-permute-start.56 = (bf16[768,1408]{1,0:T(8,128)(2,1)S(1)}, bf16[768,1408]{1,0:T(8,128)(2,1)}, u32[]{:S(2)}, u32[]{:S(2)}) collective-permute-start(bf16[768,1408]{1,0:T(8,128)(2,1)S(1)} %concatenate.199.refs_1_), channel_id=1, source_target_pairs={{0,8},{8,0},{1,9},{9,1},{2,10},{10,2},{3,11},{11,3},{4,12},{12,4},... | collective-permute-start | bytes 6488072 | tf_op jit(solution)/shard_map/ppermute | solution.py:284
  389.2 61.1 %collective-permute-start.24 = (bf16[272,1408]{1,0:T(8,128)(2,1)S(1)}, bf16[272,1408]{1,0:T(8,128)(2,1)}, u32[]{:S(2)}, u32[]{:S(2)}) collective-permute-start(bf16[272,1408]{1,0:T(8,128)(2,1)S(1)} %copy-done.114), channel_id=1, source_target_pairs={{0,8},{8,0},{1,9},{9,1},{2,10},{10,2},{3,11},{11,3},{4,12},{12,4},... | collective-permute-start | bytes 2297864 | tf_op jit(solution)/shard_map/ppermute | solution.py:284
  391.3 67.5 %collective-permute-start.26 = (bf16[528,1408]{1,0:T(8,128)(2,1)}, bf16[528,1408]{1,0:T(8,128)(2,1)}, u32[]{:S(2)}, u32[]{:S(2)}) collective-permute-start(bf16[528,1408]{1,0:T(8,128)(2,1)} %collective-permute-done.21.refs_2_), channel_id=1, source_target_pairs={{0,4},{4,0},{1,5},{5,1},{2,6},{6,2},{3,7},{7,3},{8,12},{12,8},{9,1... | collective-permute-start | bytes 4460552 | tf_op jit(solution)/shard_map/ppermute | solution.py:284
  391.6 67.5 %collective-permute-start.27 = (bf16[528,1408]{1,0:T(8,128)(2,1)}, bf16[528,1408]{1,0:T(8,128)(2,1)}, u32[]{:S(2)}, u32[]{:S(2)}) collective-permute-start(bf16[528,1408]{1,0:T(8,128)(2,1)} %collective-permute-done.22.refs_3_), channel_id=1, source_target_pairs={{0,4},{4,0},{1,5},{5,1},{2,6},{6,2},{3,7},{7,3},{8,12},{12,8},{9,1... | collective-permute-start | bytes 4460552 | tf_op jit(solution)/shard_map/ppermute | solution.py:284
  461.4 62.3 %collective-permute-start.60 = (bf16[768,1408]{1,0:T(8,128)(2,1)S(1)}, bf16[768,1408]{1,0:T(8,128)(2,1)}, u32[]{:S(2)}, u32[]{:S(2)}) collective-permute-start(bf16[768,1408]{1,0:T(8,128)(2,1)S(1)} %concatenate.199.refs_1_), channel_id=1, source_target_pairs={{0,4},{4,0},{1,5},{5,1},{2,6},{6,2},{3,7},{7,3},{8,12},{12,8},{9,1... | collective-permute-start | bytes 6488072 | tf_op jit(solution)/shard_map/ppermute | solution.py:284
  501.7 70.8 %collective-permute-start.66 = (bf16[176,6144]{1,0:T(8,128)(2,1)}, bf16[176,6144]{1,0:T(8,128)(2,1)S(1)}, u32[]{:S(2)}, u32[]{:S(2)}) collective-permute-start(bf16[176,6144]{1,0:T(8,128)(2,1)} %pad_maximum_fusion.3.refs_1_), channel_id=1, source_target_pairs={{0,16},{16,0},{1,17},{17,1},{2,18},{18,2},{3,19},{19,3},{4,20},{20... | collective-permute-start | bytes 6488072 | tf_op jit(solution)/shard_map/ppermute | solution.py:284
  519.7 63.7 %collective-permute-start.61 = (bf16[768,1408]{1,0:T(8,128)(2,1)}, bf16[768,1408]{1,0:T(8,128)(2,1)}, u32[]{:S(2)}, u32[]{:S(2)}) collective-permute-start(bf16[768,1408]{1,0:T(8,128)(2,1)} %collective-permute-done.56.refs_2_), channel_id=1, source_target_pairs={{0,4},{4,0},{1,5},{5,1},{2,6},{6,2},{3,7},{7,3},{8,12},{12,8},{9,1... | collective-permute-start | bytes 6488072 | tf_op jit(solution)/shard_map/ppermute | solution.py:284
  523.8 62.5 %collective-permute-start.62 = (bf16[768,1408]{1,0:T(8,128)(2,1)}, bf16[768,1408]{1,0:T(8,128)(2,1)}, u32[]{:S(2)}, u32[]{:S(2)}) collective-permute-start(bf16[768,1408]{1,0:T(8,128)(2,1)} %collective-permute-done.57.refs_3_), channel_id=1, source_target_pairs={{0,4},{4,0},{1,5},{5,1},{2,6},{6,2},{3,7},{7,3},{8,12},{12,8},{9,1... | collective-permute-start | bytes 6488072 | tf_op jit(solution)/shard_map/ppermute | solution.py:284
  526.7 65.7 %collective-permute-start.65 = (bf16[176,6144]{1,0:T(8,128)(2,1)}, bf16[176,6144]{1,0:T(8,128)(2,1)}, u32[]{:S(2)}, u32[]{:S(2)}) collective-permute-start(bf16[176,6144]{1,0:T(8,128)(2,1)} %pad_maximum_fusion.3.refs_1_), channel_id=1, source_target_pairs={{0,8},{8,0},{1,9},{9,1},{2,10},{10,2},{3,11},{11,3},{4,12},{12,4},... | collective-permute-start | bytes 6488072 | tf_op jit(solution)/shard_map/ppermute | solution.py:284
  685.9 67.9 %collective-permute-start.79 = (bf16[6144,512]{1,0:T(8,128)(2,1)}, bf16[6144,512]{1,0:T(8,128)(2,1)}, u32[]{:S(2)}, u32[]{:S(2)}) collective-permute-start(bf16[6144,512]{1,0:T(8,128)(2,1)} %get-tuple-element.134.x_ref), channel_id=1, source_target_pairs={{0,4},{4,0},{1,5},{5,1},{2,6},{6,2},{3,7},{7,3},{8,12},{12,8},{9,1... | collective-permute-start | bytes 18874376 | tf_op jit(solution)/shard_map/ppermute | solution.py:284
  720.9 81.1 %collective-permute-start.80 = (bf16[6144,512]{1,0:T(8,128)(2,1)}, bf16[6144,512]{1,0:T(8,128)(2,1)}, u32[]{:S(2)}, u32[]{:S(2)}) collective-permute-start(bf16[6144,512]{1,0:T(8,128)(2,1)} %get-tuple-element.73.dy_ref), channel_id=1, source_target_pairs={{0,4},{4,0},{1,5},{5,1},{2,6},{6,2},{3,7},{7,3},{8,12},{12,8},{9,1... | collective-permute-start | bytes 18874376 | tf_op jit(solution)/shard_map/ppermute | solution.py:284
  721.6 207.4 %collective-permute-start.130 = (bf16[1024,128]{1,0:T(8,128)(2,1)}, bf16[1024,128]{1,0:T(8,128)(2,1)}, u32[]{:S(2)}, u32[]{:S(2)}) collective-permute-start(bf16[1024,128]{1,0:T(8,128)(2,1)} %fusion.66.x_ref), channel_id=1, source_target_pairs={{0,4},{4,0},{1,5},{5,1},{2,6},{6,2},{3,7},{7,3},{8,12},{12,8},{9,1... | collective-permute-start | bytes 786440 | tf_op jit(solution)/shard_map/ppermute | solution.py:284
  746.8 479.7 %collective-permute-start.96 = (bf16[2816,512]{1,0:T(8,128)(2,1)}, bf16[2816,512]{1,0:T(8,128)(2,1)}, u32[]{:S(2)}, u32[]{:S(2)}) collective-permute-start(bf16[2816,512]{1,0:T(8,128)(2,1)} %copy-done.83), channel_id=1, source_target_pairs={{0,4},{4,0},{1,5},{5,1},{2,6},{6,2},{3,7},{7,3},{8,12},{12,8},{9,1... | collective-permute-start | bytes 8650760 | tf_op jit(solution)/shard_map/ppermute | solution.py:284
  930.4 69.8 %collective-permute-start.120 = (bf16[1408,512]{1,0:T(8,128)(2,1)}, bf16[1408,512]{1,0:T(8,128)(2,1)}, u32[]{:S(2)}, u32[]{:S(2)}) collective-permute-start(bf16[1408,512]{1,0:T(8,128)(2,1)} %convert_element_type.279.refs_2_.x_ref), channel_id=1, source_target_pairs={{0,4},{4,0},{1,5},{5,1},{2,6},{6,2},{3,7},{7,3},{8,12},{12,8},{9,1... | collective-permute-start | bytes 4325384 | tf_op jit(solution)/shard_map/ppermute | solution.py:284
  957.8 60.5 %collective-permute-start.124 = (bf16[1408,512]{1,0:T(8,128)(2,1)}, bf16[1408,512]{1,0:T(8,128)(2,1)}, u32[]{:S(2)}, u32[]{:S(2)}) collective-permute-start(bf16[1408,512]{1,0:T(8,128)(2,1)} %convert_element_type.275.refs_2_.x_ref), channel_id=1, source_target_pairs={{0,4},{4,0},{1,5},{5,1},{2,6},{6,2},{3,7},{7,3},{8,12},{12,8},{9,1... | collective-permute-start | bytes 4325384 | tf_op jit(solution)/shard_map/ppermute | solution.py:284
  1000.2 207.5 %collective-permute-start.143 = (bf16[176,6144]{1,0:T(8,128)(2,1)}, bf16[176,6144]{1,0:T(8,128)(2,1)}, u32[]{:S(2)}, u32[]{:S(2)}) collective-permute-start(bf16[176,6144]{1,0:T(8,128)(2,1)} %pad_maximum_fusion.6), channel_id=1, source_target_pairs={{0,16},{16,0},{1,17},{17,1},{2,18},{18,2},{3,19},{19,3},{4,20},{20... | collective-permute-start | bytes 6488072 | tf_op jit(solution)/shard_map/ppermute | solution.py:284
  1039.8 164.0 %collective-permute-start.140 = (bf16[384,1408]{1,0:T(8,128)(2,1)}, bf16[384,1408]{1,0:T(8,128)(2,1)}, u32[]{:S(2)}, u32[]{:S(2)}) collective-permute-start(bf16[384,1408]{1,0:T(8,128)(2,1)} %get-tuple-element.140), channel_id=1, source_target_pairs={{0,16},{16,0},{1,17},{17,1},{2,18},{18,2},{3,19},{19,3},{4,20},{20... | collective-permute-start | bytes 3244040 | tf_op jit(solution)/shard_map/ppermute | solution.py:284
  1142.3 66.0 %collective-permute-start.145 = (bf16[176,6144]{1,0:T(8,128)(2,1)}, bf16[176,6144]{1,0:T(8,128)(2,1)}, u32[]{:S(2)}, u32[]{:S(2)}) collective-permute-start(bf16[176,6144]{1,0:T(8,128)(2,1)} %pad_maximum_fusion.7), channel_id=1, source_target_pairs={{0,8},{8,0},{1,9},{9,1},{2,10},{10,2},{3,11},{11,3},{4,12},{12,4},... | collective-permute-start | bytes 6488072 | tf_op jit(solution)/shard_map/ppermute | solution.py:284
  1172.6 275.8 %reduce-scatter.11.cloned.1.call-start = ((), (), s32[]{:S(2)}) async-start(), calls=%async_computation.7 | async-start | bytes 2703360 | tf_op jit(solution)/shard_map/reduce_scatter | solution.py:472
  1217.8 232.7 %reduce-scatter.9.cloned.1.call-start = ((), (), s32[]{:S(2)}) async-start(), calls=%async_computation.6 | async-start | bytes 2703360 | tf_op jit(solution)/shard_map/reduce_scatter | solution.py:472
  1243.3 137.3 %collective-permute-start.132 = (bf16[352,1024]{1,0:T(8,128)(2,1)}, bf16[352,1024]{1,0:T(8,128)(2,1)}, u32[]{:S(2)}, u32[]{:S(2)}) collective-permute-start(bf16[352,1024]{1,0:T(8,128)(2,1)} %pad_maximum_fusion.21), channel_id=1, source_target_pairs={{0,16},{16,0},{1,17},{17,1},{2,18},{18,2},{3,19},{19,3},{4,20},{20... | collective-permute-start | bytes 2162696 | tf_op jit(solution)/shard_map/ppermute | solution.py:284
  1244.5 136.1 %collective-permute-start.134 = (bf16[352,1024]{1,0:T(8,128)(2,1)}, bf16[352,1024]{1,0:T(8,128)(2,1)}, u32[]{:S(2)}, u32[]{:S(2)}) collective-permute-start(bf16[352,1024]{1,0:T(8,128)(2,1)} %pad_maximum_fusion.22), channel_id=1, source_target_pairs={{0,8},{8,0},{1,9},{9,1},{2,10},{10,2},{3,11},{11,3},{4,12},{12,4},... | collective-permute-start | bytes 2162696 | tf_op jit(solution)/shard_map/ppermute | solution.py:284
  1258.2 82.3 %collective-permute-start.99 = (bf16[96,2816]{1,0:T(8,128)(2,1)}, bf16[96,2816]{1,0:T(8,128)(2,1)}, u32[]{:S(2)}, u32[]{:S(2)}) collective-permute-start(bf16[96,2816]{1,0:T(8,128)(2,1)} %get-tuple-element.156), channel_id=1, source_target_pairs={{0,16},{16,0},{1,17},{17,1},{2,18},{18,2},{3,19},{19,3},{4,20},{20... | collective-permute-start | bytes 1622024 | tf_op jit(solution)/shard_map/ppermute | solution.py:284
  1276.6 60.6 %collective-permute-start.97 = (bf16[80,2816]{1,0:T(8,128)(2,1)}, bf16[80,2816]{1,0:T(8,128)(2,1)}, u32[]{:S(2)}, u32[]{:S(2)}) collective-permute-start(bf16[80,2816]{1,0:T(8,128)(2,1)} %slice.545), channel_id=1, source_target_pairs={{0,8},{8,0},{1,9},{9,1},{2,10},{10,2},{3,11},{11,3},{4,12},{12,4},... | collective-permute-start | bytes 1351688 | tf_op jit(solution)/shard_map/ppermute | solution.py:284
  1285.0 167.6 %reduce-scatter.5.cloned.1.call-start = ((), (), s32[]{:S(2)}) async-start(), calls=%async_computation.4 | async-start | bytes 2027520 | tf_op jit(solution)/shard_map/reduce_scatter | solution.py:472
  (309 other events, 5833.5 us)
Sparse Core Ops, SparseCore 0:
  109.9 46.7 all-gather.6
  246.2 68.0 all-gather.8
  372.2 46.3 all-gather.10
  1172.7 32.6 reduce-scatter.6
  1218.0 41.5 reduce-scatter.10
  1285.1 42.1 reduce-scatter.8
  1374.5 57.2 reduce-scatter.4

commit v2 on v1

v2 whole, which is shorter than its diff:
```python
import functools
import math

import jax
import jax.numpy as jnp
from jax import lax
from jax.experimental import pallas as pl
from jax.experimental.pallas import tpu as pltpu
from jax.sharding import Mesh
from jax.sharding import PartitionSpec as P

H = 16
HD = 88
GRID = 32
PAIR = 2 * HD

epsilon = 1e-06
SCALE = HD ** (-0.5)
SCALE_LOG2 = SCALE * math.log2(math.e)

f32 = jnp.float32
bf16 = jnp.bfloat16


def normalize(values, axis):
    center = values - jnp.mean(values, axis=axis, keepdims=True)
    spread = jnp.mean(center * center, axis=axis, keepdims=True)
    return center * lax.rsqrt(spread + epsilon)


def norm_gain(values, gain_vec):
    return normalize(values, 0) * gain_vec[:, None]


def shifted_norm(values, gain_vec, offset):
    return normalize(values, 0) * gain_vec[:, None] + offset[:, None]


def norm_gain_rows(values, gain_vec):
    return normalize(values, -1) * gain_vec


def gelu_tanh(values):
    return jax.nn.gelu(values, approximate=True)


def head_norm(flat):
    return normalize(flat.reshape(H, HD, flat.shape[-1]), 1).reshape(flat.shape)


def rotate(per_head, tables):
    row_cos, row_sin, col_cos, col_sin = tables
    quarter = per_head.shape[1] // 4
    part_one = per_head[:, :quarter]
    part_two = per_head[:, quarter : 2 * quarter]
    part_three = per_head[:, 2 * quarter : 3 * quarter]
    part_four = per_head[:, 3 * quarter :]
    return jnp.concatenate(
        [
            part_one * row_cos - part_two * row_sin,
            part_two * row_cos + part_one * row_sin,
            part_three * col_cos - part_four * col_sin,
            part_four * col_cos + part_three * col_sin,
        ],
        axis=1,
    )


def dot(a, b, dims=((1,), (0,))):
    return lax.dot_general(a, b, (dims, ((), ())), preferred_element_type=f32)


NN = ((1,), (0,))
TN = ((0,), (0,))
NT = ((1,), (1,))


def heads_of(ref):
    pair = ref[...].astype(f32)
    return pair[:HD].astype(bf16), pair[HD:].astype(bf16)


def attend_kernel(blocks, *refs):
    q_ref = refs[0]
    k_refs = refs[1 : 1 + blocks]
    v_refs = refs[1 + blocks : 1 + 2 * blocks]
    o_ref, inv_ref = refs[1 + 2 * blocks :]
    q_heads = heads_of(q_ref)
    k_heads = [heads_of(r) for r in k_refs]
    v_heads = [heads_of(r) for r in v_refs]
    outs = []
    for i in range(2):
        total = None
        summed = None
        for k_pair, v_pair in zip(k_heads, v_heads):
            scores = dot(k_pair[i], q_heads[i], TN)
            probs = jnp.exp2(scores * SCALE_LOG2)
            part_sum = jnp.sum(probs, axis=0, keepdims=True)
            part = dot(v_pair[i], probs.astype(bf16), NN)
            total = part if total is None else total + part
            summed = part_sum if summed is None else summed + part_sum
        inverse = 1.0 / summed
        outs.append(total * inverse)
        inv_ref[0, i : i + 1, :] = inverse
    o_ref[...] = jnp.concatenate(outs, axis=0).astype(bf16)


def attend(query, keys, values):
    blocks = len(keys)
    tokens = query.shape[1]
    per_key = keys[0].shape[1]
    spec_q = pl.BlockSpec((PAIR, tokens), lambda h: (h, 0))
    spec_k = pl.BlockSpec((PAIR, per_key), lambda h: (h, 0))
    return pl.pallas_call(
        functools.partial(attend_kernel, blocks),
        grid=(H // 2,),
        in_specs=[spec_q] + [spec_k] * (2 * blocks),
        out_specs=[spec_q, pl.BlockSpec((1, 2, tokens), lambda h: (h, 0, 0))],
        out_shape=[
            jax.ShapeDtypeStruct((H * HD, tokens), bf16),
            jax.ShapeDtypeStruct((H // 2, 2, tokens), f32),
        ],
        compiler_params=pltpu.CompilerParams(vmem_limit_bytes=48 * 2**20),
        cost_estimate=pl.CostEstimate(
            flops=2 * 2 * H * 128 * tokens * per_key * blocks,
            bytes_accessed=2 * H * HD * (3 * tokens + 2 * per_key * blocks),
            transcendentals=H * tokens * per_key * blocks,
        ),
        name="attend",
    )(query, *keys, *values)


def attend_back_kernel(blocks, *refs):
    q_ref, g_ref, o_ref, inv_ref = refs[:4]
    k_refs = refs[4 : 4 + blocks]
    v_refs = refs[4 + blocks : 4 + 2 * blocks]
    dq_ref = refs[4 + 2 * blocks]
    dk_refs = refs[5 + 2 * blocks : 5 + 3 * blocks]
    dv_refs = refs[5 + 3 * blocks : 5 + 4 * blocks]
    q_heads = heads_of(q_ref)
    g_heads = heads_of(g_ref)
    gated = g_ref[...].astype(f32) * o_ref[...].astype(f32)
    k_heads = [heads_of(r) for r in k_refs]
    v_heads = [heads_of(r) for r in v_refs]
    grad_queries = []
    grad_keys = [[] for _ in range(blocks)]
    grad_values = [[] for _ in range(blocks)]
    for i in range(2):
        row_dot = jnp.sum(gated[i * HD : (i + 1) * HD], axis=0, keepdims=True)
        inverse = inv_ref[0, i : i + 1, :]
        grad_q = None
        for b in range(blocks):
            k_one, v_one = k_heads[b][i], v_heads[b][i]
            scores = dot(k_one, q_heads[i], TN)
            exact = jnp.exp2(scores * SCALE_LOG2) * inverse
            grad_probs = dot(v_one, g_heads[i], TN)
            grad_scores = (exact * (grad_probs - row_dot)).astype(bf16)
            part = dot(k_one, grad_scores, NN)
            grad_q = part if grad_q is None else grad_q + part
            grad_keys[b].append(dot(q_heads[i], grad_scores, NT) * SCALE)
            grad_values[b].append(dot(g_heads[i], exact.astype(bf16), NT))
        grad_queries.append(grad_q * SCALE)
    dq_ref[...] = jnp.concatenate(grad_queries, axis=0)
    for b in range(blocks):
        dk_refs[b][...] = jnp.concatenate(grad_keys[b], axis=0).astype(dk_refs[b].dtype)
        dv_refs[b][...] = jnp.concatenate(grad_values[b], axis=0).astype(dv_refs[b].dtype)


def attend_back(query, grad, out, inverse, keys, values):
    blocks = len(keys)
    tokens = query.shape[1]
    per_key = keys[0].shape[1]
    spec_q = pl.BlockSpec((PAIR, tokens), lambda h: (h, 0))
    spec_k = pl.BlockSpec((PAIR, per_key), lambda h: (h, 0))
    shapes_k = [jax.ShapeDtypeStruct((H * HD, per_key), kind) for kind in (f32, bf16)]
    outs = pl.pallas_call(
        functools.partial(attend_back_kernel, blocks),
        grid=(H // 2,),
        in_specs=[spec_q] * 3
        + [pl.BlockSpec((1, 2, tokens), lambda h: (h, 0, 0))]
        + [spec_k] * (2 * blocks),
        out_specs=[spec_q] + [spec_k] * (2 * blocks),
        out_shape=[jax.ShapeDtypeStruct((H * HD, tokens), f32)] + shapes_k * 2,
        compiler_params=pltpu.CompilerParams(vmem_limit_bytes=56 * 2**20),
        cost_estimate=pl.CostEstimate(
            flops=5 * 2 * H * 128 * tokens * per_key * blocks,
            bytes_accessed=2 * H * HD * (6 * tokens + 6 * per_key * blocks),
            transcendentals=H * tokens * per_key * blocks,
        ),
        name="attend_back",
    )(query, grad, out, inverse, *keys, *values)
    return outs[0], outs[1 : 1 + blocks], outs[1 + blocks :]


def assemble_kernel(heights, layout, *refs):
    count = len(layout)
    place_ref = refs[0]
    pieces = refs[1 : 1 + count]
    wholes = refs[1 + count : 1 + count + len(heights)]
    held = refs[1 + count + len(heights) : -2]
    sem_in, sem_out = refs[-2:]
    loads = [
        pltpu.make_async_copy(piece, room, sem_in.at[i])
        for i, (piece, room) in enumerate(zip(pieces, held))
    ]
    for load in loads:
        load.start()
    stores = []
    for load, room, (rank, low, high) in zip(loads, held, layout):
        load.wait()
        top = 0
        for height, whole in zip(heights, wholes):
            begin, end = max(low, top), min(high, top + height)
            if begin < end:
                row = pl.multiple_of(place_ref[rank] * height, 16) + (begin - top)
                store = pltpu.make_async_copy(
                    room.at[pl.ds(begin - low, end - begin)],
                    whole.at[pl.ds(row, end - begin)],
                    sem_out.at[len(stores)],
                )
                store.start()
                stores.append(store)
            top += height
    for store in stores:
        store.wait()


def assemble(pieces, layout, heights, places):
    width = pieces[0].shape[1]
    total = sum(heights)
    return pl.pallas_call(
        functools.partial(assemble_kernel, heights, layout),
        in_specs=[pl.BlockSpec(memory_space=pltpu.SMEM)]
        + [pl.BlockSpec(memory_space=pl.ANY)] * len(pieces),
        out_specs=[pl.BlockSpec(memory_space=pl.ANY)] * len(heights),
        out_shape=[jax.ShapeDtypeStruct((8 * height, width), bf16) for height in heights],
        scratch_shapes=[pltpu.VMEM(piece.shape, bf16) for piece in pieces]
        + [
            pltpu.SemaphoreType.DMA((len(pieces),)),
            pltpu.SemaphoreType.DMA((len(pieces) * len(heights),)),
        ],
        compiler_params=pltpu.CompilerParams(vmem_limit_bytes=24 * 2**20),
        cost_estimate=pl.CostEstimate(
            flops=0, bytes_accessed=2 * 2 * 8 * total * width, transcendentals=0
        ),
        name="assemble",
    )(places, *pieces)


def outer_kernel(heights, sharing, half, place_ref, *refs):
    count = len(heights)
    outs = 5 if half else 1
    dy_refs = refs[: 2 * count]
    x_refs = refs[2 * count : -outs]
    if half:
        low_ref, high_ref, over_a_ref, over_b_ref, own_ref = refs[-outs:]

    def put(rank, top, block):
        if not half:
            refs[-1][rank, top : top + block.shape[0], :] = block
            return
        if rank < 3:
            (own_ref, over_b_ref, over_a_ref)[rank][top : top + block.shape[0], :] = block
            return
        end = top + block.shape[0]
        if top < half:
            low_ref[top : min(end, half), :] = block[: min(end, half) - top]
        if end > half:
            high_ref[max(top, half) - half : end - half, :] = block[max(top, half) - top :]

    top = 0
    for i, (height, x_index) in enumerate(zip(heights, sharing)):
        step = 4 if height <= 176 else 2 if height <= 352 else 1
        for start in range(0, 4, step):
            total = None
            for core in range(2):
                chosen = [
                    dy_refs[2 * i + core][
                        pl.ds(pl.multiple_of(place_ref[rank] * height, 16), height), :
                    ]
                    for rank in range(start, start + step)
                ]
                lhs = chosen[0] if step == 1 else jnp.concatenate(chosen, axis=0)
                part = dot(lhs, x_refs[2 * x_index + core][...], NT)
                total = part if total is None else total + part
            total = total.astype(bf16)
            for n in range(step):
                put(start + n, top, total[n * height : (n + 1) * height])
        top += height


def outer_blocks(places, groups, blocks, split):
    x_pairs = [x_pair for x_pair, _ in groups]
    dy_pairs = [dy for _, group in groups for dy in group]
    sharing = [i for i, (_, group) in enumerate(groups) for _ in group]
    heights = [dy[0].shape[0] // blocks for dy in dy_pairs]
    rows = sum(heights)
    half = rows // 32 * 16 if split else 0
    tokens = dy_pairs[0][0].shape[1]
    width = x_pairs[0][0].shape[0]
    cut = next(c for c in (1408, 1536, 512, 128) if width % c == 0)
    once = pl.Buffered(1)
    dy_specs = [
        pl.BlockSpec(dy.shape, lambda i, place: (0, 0), pipeline_mode=once)
        for pair in dy_pairs
        for dy in pair
    ]
    x_buffers = {"pipeline_mode": once} if cut == width else {}
    x_specs = [pl.BlockSpec((cut, tokens), lambda i, place: (i, 0), **x_buffers)] * (
        2 * len(x_pairs)
    )
    sizes = (half, rows - half, rows, rows, rows)
    if split:
        out_specs = [pl.BlockSpec((size, cut), lambda i, place: (0, i)) for size in sizes]
        out_shape = [jax.ShapeDtypeStruct((size, width), bf16) for size in sizes]
    else:
        out_specs = [pl.BlockSpec((4, rows, cut), lambda i, place: (0, 0, i))]
        out_shape = [jax.ShapeDtypeStruct((4, rows, width), bf16)]
    return pl.pallas_call(
        functools.partial(outer_kernel, heights, sharing, half),
        grid_spec=pltpu.PrefetchScalarGridSpec(
            num_scalar_prefetch=1,
            grid=(width // cut,),
            in_specs=dy_specs + x_specs,
            out_specs=out_specs,
        ),
        out_shape=out_shape,
        compiler_params=pltpu.CompilerParams(vmem_limit_bytes=56 * 2**20),
        cost_estimate=pl.CostEstimate(
            flops=2 * 2 * 4 * rows * width * tokens,
            bytes_accessed=2 * (2 * tokens * (8 * rows + width) + 4 * rows * width),
            transcendentals=0,
        ),
        name="outer_blocks",
    )(places, *[dy for pair in dy_pairs for dy in pair], *[x for pair in x_pairs for x in pair])


def cut_kernel(seq, z_ref, *refs):
    term_refs, out_refs, held = refs[: -seq - 1], refs[-seq - 1 : -1], refs[-1]
    at_z = z_ref[0]
    rows, width = term_refs[0].shape
    part = width // seq

    def chunk(i, _):
        at = pl.ds(pl.multiple_of(i * 16, 16), 16)
        total = term_refs[0][at, :]
        if len(term_refs) > 1:
            total = sum(ref[at, :].astype(f32) for ref in term_refs).astype(bf16)
        for j in range(seq):
            held[j, at, :] = total[:, j * part : (j + 1) * part]
        return 0

    lax.fori_loop(0, rows // 16, chunk, 0)
    for step in range(seq):
        out_refs[step][...] = held[lax.rem(at_z + step, seq)]


def cut_sum(at_z, seq, *terms):
    rows, width = terms[0].shape
    return pl.pallas_call(
        functools.partial(cut_kernel, seq),
        in_specs=[pl.BlockSpec(memory_space=pltpu.SMEM)]
        + [pl.BlockSpec(memory_space=pltpu.VMEM)] * len(terms),
        out_specs=[pl.BlockSpec(memory_space=pltpu.VMEM)] * seq,
        out_shape=[jax.ShapeDtypeStruct((rows, width // seq), bf16)] * seq,
        scratch_shapes=[pltpu.VMEM((seq, rows, width // seq), bf16)],
        compiler_params=pltpu.CompilerParams(vmem_limit_bytes=32 * 2**20),
        cost_estimate=pl.CostEstimate(
            flops=2 * rows * width, bytes_accessed=8 * rows * width, transcendentals=0
        ),
        name="cut_sum",
    )(at_z.reshape(1), *terms)


def join_kernel(seq, z_ref, *refs):
    part_refs, out_ref, held = refs[:seq], refs[seq], refs[seq + 1]
    at_z = z_ref[0]
    rows, width = out_ref.shape
    for step in range(seq):
        held[lax.rem(at_z + seq - step, seq)] = part_refs[step][...]

    def chunk(i, _):
        at = pl.ds(pl.multiple_of(i * 16, 16), 16)
        out_ref[at, :] = jnp.concatenate([held[j, at, :] for j in range(seq)], axis=1)
        return 0

    lax.fori_loop(0, rows // 16, chunk, 0)


def join_parts(at_z, parts):
    seq = len(parts)
    rows, part = parts[0].shape
    return pl.pallas_call(
        functools.partial(join_kernel, seq),
        in_specs=[pl.BlockSpec(memory_space=pltpu.SMEM)]
        + [pl.BlockSpec(memory_space=pltpu.VMEM)] * seq,
        out_specs=pl.BlockSpec(memory_space=pltpu.VMEM),
        out_shape=jax.ShapeDtypeStruct((rows, seq * part), bf16),
        scratch_shapes=[pltpu.VMEM((seq, rows, part), bf16)],
        compiler_params=pltpu.CompilerParams(vmem_limit_bytes=32 * 2**20),
        cost_estimate=pl.CostEstimate(
            flops=0, bytes_accessed=4 * seq * rows * part, transcendentals=0
        ),
        name="join_parts",
    )(at_z.reshape(1), *parts)


def join_gathered_kernel(gathered_ref, out_ref):
    seq = gathered_ref.shape[0]

    def chunk(i, _):
        at = pl.ds(pl.multiple_of(i * 16, 16), 16)
        out_ref[at, :] = jnp.concatenate([gathered_ref[j, at, :] for j in range(seq)], axis=1)
        return 0

    lax.fori_loop(0, out_ref.shape[0] // 16, chunk, 0)


def join_gathered(gathered):
    seq, rows, part = gathered.shape
    return pl.pallas_call(
        join_gathered_kernel,
        in_specs=[pl.BlockSpec(memory_space=pltpu.VMEM)],
        out_specs=pl.BlockSpec(memory_space=pltpu.VMEM),
        out_shape=jax.ShapeDtypeStruct((rows, seq * part), bf16),
        compiler_params=pltpu.CompilerParams(vmem_limit_bytes=32 * 2**20),
        cost_estimate=pl.CostEstimate(
            flops=0, bytes_accessed=4 * seq * rows * part, transcendentals=0
        ),
        name="join_gathered",
    )(gathered)


def stack_kernel(*refs):
    term_refs, out_ref = refs[:-1], refs[-1]
    seq, _, part = out_ref.shape

    def chunk(i, _):
        at = pl.ds(pl.multiple_of(i * 16, 16), 16)
        total = sum(ref[at, :].astype(f32) for ref in term_refs).astype(bf16)
        for j in range(seq):
            out_ref[j, at, :] = total[:, j * part : (j + 1) * part]
        return 0

    lax.fori_loop(0, out_ref.shape[1] // 16, chunk, 0)


def stack_sum(seq, *terms):
    rows, width = terms[0].shape
    return pl.pallas_call(
        stack_kernel,
        in_specs=[pl.BlockSpec(memory_space=pltpu.VMEM)] * len(terms),
        out_specs=pl.BlockSpec(memory_space=pltpu.VMEM),
        out_shape=jax.ShapeDtypeStruct((seq, rows, width // seq), bf16),
        compiler_params=pltpu.CompilerParams(vmem_limit_bytes=32 * 2**20),
        cost_estimate=pl.CostEstimate(
            flops=2 * rows * width, bytes_accessed=8 * rows * width, transcendentals=0
        ),
        name="stack_sum",
    )(*terms)


def gelu_slope(x):
    scale = math.sqrt(2.0 / math.pi)
    bend = 0.044715
    curve = jnp.tanh(scale * (x + bend * x * x * x))
    return 0.5 * (1.0 + curve) + 0.5 * x * (1.0 - curve * curve) * scale * (1.0 + 3.0 * bend * x * x)


def mlp_up_kernel(up_ref, u_ref, hidden_ref, act_ref):
    hidden = dot(up_ref[...], u_ref[0], NN)
    hidden_ref[0] = hidden
    act_ref[0] = gelu_tanh(hidden).astype(bf16)


def mlp_down_kernel(down_ref, act_ref, out_ref):
    out_ref[0] = dot(down_ref[...], act_ref[0], NN).astype(bf16)


def mlp_back_kernel(down_flip_ref, up_flip_ref, grad_ref, hidden_ref, dh_ref, du_ref):
    grad_act = dot(down_flip_ref[...], grad_ref[0], NN)
    grad_hidden = (grad_act * gelu_slope(hidden_ref[0])).astype(bf16)
    dh_ref[0] = grad_hidden
    du_ref[0] = dot(up_flip_ref[...], grad_hidden, NN).astype(bf16)


def mlp_outer_kernel(a_ref, b_ref, out_ref, total_ref):
    step = pl.program_id(0)

    @pl.when(step == 0)
    def _():
        total_ref[...] = jnp.zeros_like(total_ref)

    total_ref[...] += dot(a_ref[0], b_ref[0], NT)

    @pl.when(step == pl.num_programs(0) - 1)
    def _():
        out_ref[...] = total_ref[...].astype(bf16)


def by_device(shape):
    return pl.BlockSpec((1,) + shape, lambda i: (i, 0, 0))


def kept(shape):
    return pl.BlockSpec(shape, lambda i: (0, 0))


def mlp_call(kernel, name, held, streams, outs, whole=None):
    count, _, tokens = streams[0].shape
    params = pltpu.CompilerParams(vmem_limit_bytes=48 * 2**20)
    flops = 2 * count * tokens * sum(x.shape[0] * x.shape[1] for x in held)
    moved = sum(x.size * 2 for x in streams) + sum(count * r * tokens * 3 for r, _ in outs)
    if whole:
        flops = 2 * count * tokens * whole[0] * whole[1]
        out_specs, out_shape = kept(whole), jax.ShapeDtypeStruct(whole, bf16)
        scratch = [pltpu.VMEM(whole, f32)]
    else:
        out_specs = [by_device((rows, tokens)) for rows, _ in outs]
        out_shape = [jax.ShapeDtypeStruct((count, rows, tokens), kind) for rows, kind in outs]
        scratch = []
    return pl.pallas_call(
        kernel,
        grid=(count,),
        in_specs=[kept(x.shape) for x in held] + [by_device(x.shape[1:]) for x in streams],
        out_specs=out_specs,
        out_shape=out_shape,
        scratch_shapes=scratch,
        compiler_params=params,
        cost_estimate=pl.CostEstimate(flops=flops, bytes_accessed=moved, transcendentals=0),
        name=name,
    )(*held, *streams)


def after(value, *others):
    return lax.optimization_barrier((value,) + others)[0]


SWAP = ((0, 1), (1, 0))


def swap(values, axis):
    return lax.ppermute(values, axis, SWAP)


def on_device(
    sizes,
    inputs,
    skipped,
    text_rows,
    condition,
    cotangent,
    norm_gains,
    skip_weight,
    shift_weight,
    query_key_weight,
    value_weight,
    self_output,
    cross_query,
    cross_memory,
    cross_output,
    up_weight,
    down_weight,
):
    outer, inner, cores, seq = sizes
    plane = outer * inner
    square = outer == 2 and inner == 2
    lat_count, local_rows, width = inputs.shape
    text_local = text_rows.shape[1]
    at_a = lax.axis_index("a")
    at_b = lax.axis_index("b")
    at_c = lax.axis_index("c")
    at_z = lax.axis_index("z")
    tokens = lat_count * local_rows

    def route(step):
        return [
            (
                core * seq + z,
                (z // lat_count) * seq + core * lat_count + (z % lat_count + step) % lat_count,
            )
            for core in range(cores)
            for z in range(seq)
        ]

    slot = at_z % lat_count

    def to_latent(values):
        parts = []
        for step in range(lat_count):
            chosen = lax.dynamic_index_in_dim(
                values, (slot + step) % lat_count, 0, keepdims=False
            )
            parts.append(lax.ppermute(chosen, ("c", "z"), route(step)))
        return jnp.concatenate(parts, axis=0)

    def from_latent(rows, *others):
        height = rows.shape[0] // lat_count
        parts = []
        for step in range(lat_count):
            back = [(target, source) for source, target in route(step)]
            parts.append(
                lax.ppermute(rows[step * height : (step + 1) * height], ("c", "z"), back)
            )
        parts = [after(part, *others) for part in parts]
        stacked = jnp.stack(parts + parts)
        return lax.dynamic_slice_in_dim(stacked, (lat_count - slot) % lat_count, lat_count, 0)

    places = jnp.stack(
        [
            ((at_a + da) % outer * inner + (at_b + db) % inner) * cores + (at_c + dc) % cores
            for dc in range(2)
            for da in range(2)
            for db in range(2)
        ]
    ).astype(jnp.int32)
    here = {"a": at_a, "b": at_b, "c": at_c}

    def z_shift(values, step):
        return lax.ppermute(values, "z", [(z, (z + step) % seq) for z in range(seq)])

    def z_send(values):
        return [values] + [z_shift(values, step) for step in range(1, seq)]

    def z_order(arrived):
        blocks = []
        for z in range(seq):
            block = arrived[0]
            for step in range(1, seq):
                block = jnp.where(at_z == (z + step) % seq, arrived[step], block)
            blocks.append(block)
        return blocks

    def z_piece(arrived, *others):
        arrived = [after(part, *others) for part in arrived]
        if square:
            return join_parts(at_z, arrived)
        return jnp.concatenate(z_order(arrived), axis=1)

    def flip(shards):
        return jnp.concatenate([shard.T for shard in shards], axis=0)

    def gather_rows(values, axes):
        if not square:
            return lax.all_gather(values, axes[::-1], axis=0, tiled=True)
        for axis in axes:
            other = swap(values, axis)
            lower = here[axis] == 0
            values = jnp.concatenate(
                [jnp.where(lower, values, other), jnp.where(lower, other, values)], axis=0
            )
        return values

    def total_of(values):
        if not square:
            return lax.psum(values, ("a", "b", "c", "z"))
        held = jnp.zeros((8,) + values.shape, values.dtype)
        for rank in range(8):
            arrived = to_rank(values, rank) if rank else values
            held = lax.dynamic_update_slice(held, arrived[None], (places[rank], 0))
        values = sum(held[i] for i in range(8))
        values = sum(z_order(z_send(values)))
        return values

    def to_rank(values, rank):
        axes = tuple(axis for axis, bit in (("c", 4), ("a", 2), ("b", 1)) if rank & bit)
        axes = tuple(axis for axis in ("a", "b", "c") if axis in axes)
        last = 2 ** len(axes) - 1
        return lax.ppermute(values, axes, [(i, last - i) for i in range(last + 1)])

    def exchange(blocks):
        return [blocks[0]] + [to_rank(blocks[rank], rank) for rank in range(1, 8)]

    def stack_by_device(blocks):
        rows = blocks[0].shape[0]
        layout = tuple((rank, 0, rows) for rank in range(8))
        return assemble(tuple(blocks), layout, [rows], places)[0]

    def hop_one(piece):
        return swap(piece, "b"), swap(piece, "a")

    def halves(over_b, over_a):
        half = over_b.shape[0] // 32 * 16
        return over_b[:half], over_a[half:]

    def hop_two(low, high):
        return swap(low, "a"), swap(high, "b")

    def after_all(parts, *others):
        return tuple(lax.optimization_barrier(tuple(parts) + others)[: len(parts)])

    def to_core(parts):
        return tuple(swap(part, "c") for part in parts)

    def whole_of(mine, others, shards):
        rows = mine[0].shape[0]
        half = mine[3].shape[0]
        spans = ((0, 0, rows), (1, 0, rows), (2, 0, rows), (3, 0, half), (3, half, rows))
        layout = spans + tuple((rank + 4, begin, end) for rank, begin, end in spans)
        return assemble(mine + others, layout, [shard.shape[1] for shard in shards], places)

    def gather_plain(piece, shards):
        heights = [shard.shape[1] for shard in shards]
        starts = [sum(heights[:i]) for i in range(len(heights))]
        return [
            lax.all_gather(piece[s : s + h], ("a", "b", "c"), axis=0, tiled=True)
            for s, h in zip(starts, heights)
        ]

    in_order = jnp.arange(4, dtype=jnp.int32) * cores + at_c

    def outer_of(*groups, split=True):
        if square:
            return outer_blocks(
                places[:4] if split else in_order, groups, plane * cores, split
            )
        outs = []
        for x_pair, dy_pairs in groups:
            for dy_pair in dy_pairs:
                total = 0.0
                for dy, x in zip(dy_pair, x_pair):
                    cube = dy.reshape(plane, cores, -1, dy.shape[1])
                    mine = lax.dynamic_index_in_dim(cube, at_c, 1, keepdims=False)
                    total = total + dot(mine.reshape(-1, dy.shape[1]), x, NT)
                cube = total.astype(bf16).reshape(plane, -1, x_pair[0].shape[0])
                outs.append(
                    lax.psum_scatter(cube, ("a", "b"), scatter_dimension=0, tiled=True)[0]
                )
        return (jnp.concatenate(outs, axis=0),)

    def sum_far(state):
        low, high, over_a, over_b, own = state
        return swap(low, "b"), swap(high, "a"), over_a, over_b, own

    def sum_near(state, *others):
        low, high, over_a, over_b, own = state
        half = low.shape[0]
        low = after(low, *others)
        over_a = lax.dynamic_update_slice(over_a, over_a[:half] + low, (0, 0))
        over_b = lax.dynamic_update_slice(over_b, over_b[half:] + high, (half, 0))
        return own, swap(over_a, "a"), swap(over_b, "b"), (over_a, over_b)

    def sum_z(state, *others):
        own, got_a, got_b, _ = state
        parts = cut_sum(at_z, seq, own, after(got_a, *others), got_b)
        return [parts[0]] + [z_shift(parts[step], step) for step in range(1, seq)]

    def sum_z_one(total, *others):
        parts = cut_sum(at_z, seq, after(total, *others))
        return [parts[0]] + [z_shift(parts[step], step) for step in range(1, seq)]

    def sum_z_offloaded(state, *others):
        own, got_a, got_b, _ = state
        stacked = stack_sum(seq, own, after(got_a, *others), got_b)
        return [lax.psum_scatter(stacked, "z", scatter_dimension=0, tiled=True)[0]], stacked

    def sum_plain(state):
        (total,) = state
        cut = total.reshape(total.shape[0], seq, -1).transpose(1, 0, 2)
        return [
            z_shift(lax.dynamic_index_in_dim(cut, (at_z + step) % seq, 0, keepdims=False), step)
            for step in range(seq)
        ]

    def sum_end(parts, shards, *others):
        owned = sum(after(part, *others).astype(f32) for part in parts)
        results = []
        start = 0
        for shard in shards:
            results.append(owned[start : start + shard.shape[1]].T)
            start += shard.shape[1]
        return results

    gain_skip = norm_gains[: 2 * width]
    gain_one = norm_gains[2 * width : 3 * width]
    gain_two = norm_gains[3 * width : 4 * width]
    gain_three = norm_gains[4 * width :]

    both_in = jnp.concatenate([inputs, skipped], axis=-1)
    skip_set = [skip_weight]
    pair_set = [query_key_weight, value_weight, shift_weight]
    self_set = [self_output, cross_query, cross_output]
    memory_set = [cross_memory]
    up_set = [up_weight]
    down_set = [down_weight]
    skip_flip, pair_flip, self_flip, memory_flip, up_flip, down_flip = (
        flip(one) for one in (skip_set, pair_set, self_set, memory_set, up_set, down_set)
    )
    if square:
        skip_sent = z_send(skip_flip)
        self_flip = after(self_flip, pair_flip)
        up_flip = after(up_flip, self_flip)
        down_flip = after(down_flip, up_flip)
        grad_sent = to_latent(after(cotangent, down_flip))
        pair_sent = lax.all_gather(pair_flip, "z", axis=0, tiled=False)
        self_sent = lax.all_gather(self_flip, "z", axis=0, tiled=False)
        up_sent = lax.all_gather(up_flip, "z", axis=0, tiled=False)
        down_sent = lax.all_gather(down_flip, "z", axis=0, tiled=False)
        skip_piece = z_piece(skip_sent)
        skip_near = hop_one(skip_piece)
        skip_half = halves(*skip_near)
        skip_far = hop_two(*skip_half)
        pair_piece = join_gathered(after(pair_sent, *skip_half))
        pair_near = hop_one(pair_piece)
        memory_sent = z_send(after(memory_flip, pair_piece))
        skip_far = after_all(skip_far, pair_piece)
        skip_mine = (skip_piece,) + skip_near + skip_far
        skip_other = to_core(skip_mine)
        (skip_t,) = whole_of(skip_mine, skip_other, skip_set)
        joined = jnp.concatenate(
            [
                inputs.reshape(tokens, width).T,
                skipped.reshape(tokens, width).T,
            ],
            axis=0,
        ).astype(f32)
        start_zero = dot(skip_t, norm_gain(joined, gain_skip).astype(bf16)).astype(bf16)
        zero_sent = to_latent(start_zero.T.reshape(inputs.shape))
        pair_near = after_all(pair_near, start_zero)
        pair_half = halves(*pair_near)
        pair_far = hop_two(*pair_half)
        memory_piece = z_piece(memory_sent, *pair_half)
        self_piece = join_gathered(after(self_sent, memory_piece))
        pair_far = after_all(pair_far, self_piece)
        pair_mine = (pair_piece,) + pair_near + pair_far
        pair_other = to_core(pair_mine)
        self_near = hop_one(self_piece)
        memory_near = hop_one(memory_piece)
        stream_zero = after(zero_sent, *pair_far).T.astype(f32)
        pair_t, value_t, shift_t = whole_of(pair_mine, pair_other, pair_set)
    else:
        chip_both = to_latent(both_in)
        joined = chip_both.T.astype(f32)
        level_zero = norm_gain(joined, gain_skip).astype(bf16)
        chip_text = to_latent(text_rows).T
        chip_grad = to_latent(cotangent).T
        (skip_t,) = gather_plain(z_piece(z_send(skip_flip)), skip_set)
        pair_t, value_t, shift_t = gather_plain(z_piece(z_send(pair_flip)), pair_set)
        self_t, cq_t, cout_t = gather_plain(z_piece(z_send(self_flip)), self_set)
        (memory_t,) = gather_plain(z_piece(z_send(memory_flip)), memory_set)
        (up_t,) = gather_plain(z_piece(z_send(up_flip)), up_set)
        (down_t,) = gather_plain(z_piece(z_send(down_flip)), down_set)
        stream_zero = dot(skip_t, level_zero)

    quarter = HD // 4
    frequency = jnp.power(10000.0, -jnp.arange(quarter, dtype=f32) / quarter)
    position = jnp.concatenate(
        [
            (at_c * lat_count + (slot - step) % lat_count) * local_rows
            + jnp.arange(local_rows, dtype=jnp.int32)
            for step in range(lat_count)
        ]
    )
    row_angle = (position // GRID).astype(f32)[None, :] * frequency[:, None]
    col_angle = (position % GRID).astype(f32)[None, :] * frequency[:, None]
    tables = (jnp.cos(row_angle), jnp.sin(row_angle), jnp.cos(col_angle), jnp.sin(col_angle))

    def prepare(flat):
        cube = flat.reshape(H, HD, flat.shape[-1])
        return rotate(normalize(cube, 1), tables).reshape(flat.shape)

    cond_pair = (condition, swap(condition, "c"))
    same_core = at_z // lat_count == at_c
    cond_two = jnp.where(same_core, cond_pair[0], cond_pair[1])
    chip_cond = lax.dynamic_index_in_dim(cond_two, slot, 0, keepdims=False)
    shift = dot(shift_t, jax.nn.silu(chip_cond.astype(f32)).astype(bf16)[:, None], NN)[:, 0]

    level_one = shifted_norm(stream_zero, gain_one, shift).astype(bf16)
    pair_proj = dot(pair_t, level_one)
    value_proj = dot(value_t, level_one).astype(bf16)
    query_flat = pair_proj[:width]
    key_flat = pair_proj[width:]
    query = prepare(query_flat).astype(bf16)
    key = prepare(key_flat).astype(bf16)
    keys = [key, swap(key, "c")]
    values = [value_proj, swap(value_proj, "c")]
    query_next = query
    if square:
        self_near = after_all(self_near, query)
        self_half = halves(*self_near)
        self_far = hop_two(*self_half)
        memory_near = after_all(memory_near, *self_half)
        memory_half = halves(*memory_near)
        memory_far = hop_two(*memory_half)
        query_next = after(query, *memory_half)
    attended, self_inverse = attend(query_next, keys, values)
    attended_next = attended
    if square:
        all_plane = ("a", "b", "c")
        up_piece = join_gathered(after(up_sent, attended))
        down_piece = join_gathered(after(down_sent, attended))
        slice_rows = up_weight.shape[1]
        down_blocks = [
            lax.dynamic_slice_in_dim(down_piece, places[rank] * slice_rows, slice_rows, 1)
            for rank in range(8)
        ]
        chip_grad = after(grad_sent, attended).T
        grad_all = lax.all_gather(chip_grad, all_plane, axis=0, tiled=False)
        text_sent = to_latent(after(text_rows, query))
        down_sent = exchange(down_blocks)
        self_far = after_all(self_far, attended)
        self_mine = (self_piece,) + self_near + self_far
        self_other = to_core(self_mine)
        memory_far = after_all(memory_far, *self_far)
        memory_mine = (memory_piece,) + memory_near + memory_far
        memory_other = to_core(memory_mine)
        self_t, cq_t, cout_t = whole_of(self_mine, self_other, self_set)
        (memory_t,) = whole_of(memory_mine, memory_other, memory_set)
        chip_text = after(text_sent, *memory_far).T
    stream_one = stream_zero + dot(self_t, attended_next)
    level_two = norm_gain(stream_one, gain_two).astype(bf16)
    cross_proj = dot(cq_t, level_two)
    cross = head_norm(cross_proj).astype(bf16)
    memory_proj = dot(memory_t, chip_text)
    memory_key_flat = memory_proj[:width]
    memory_key = head_norm(memory_key_flat).astype(bf16)
    memory_value = memory_proj[width:].astype(bf16)
    text_keys = [memory_key, swap(memory_key, "c")]
    text_values = [memory_value, swap(memory_value, "c")]
    crossed, cross_inverse = attend(cross, text_keys, text_values)
    stream_two = stream_one + dot(cout_t, crossed)
    level_three = norm_gain(stream_two, gain_three).astype(bf16)
    if square:
        up_slice = up_piece
        three_all = lax.all_gather(
            after(level_three, grad_all), all_plane, axis=0, tiled=False
        )
        down_slice = stack_by_device([after(part, level_three) for part in down_sent])
        hidden, activated = mlp_call(
            mlp_up_kernel,
            "mlp_up",
            [up_slice],
            [three_all],
            [(slice_rows, f32), (slice_rows, bf16)],
        )
    else:
        hidden = dot(up_t, level_three)
        activated = gelu_tanh(hidden).astype(bf16)

    def with_other(values):
        return values, swap(values, "c")

    one_pair = with_other(level_one)
    attended_pair = with_other(attended)
    two_pair = with_other(level_two)
    text_pair = with_other(chip_text)
    crossed_pair = with_other(crossed)

    if square:
        grad_hidden, part = mlp_call(
            mlp_back_kernel,
            "mlp_back",
            [down_slice.T, up_slice.T],
            [grad_all, hidden],
            [(slice_rows, bf16), (width, bf16)],
        )
        grad_level_three = lax.psum_scatter(part, all_plane, scatter_dimension=0, tiled=True)[0]
        both_sent = to_latent(after(both_in, part))
        down_grad = mlp_call(
            mlp_outer_kernel,
            "mlp_outer",
            [],
            [after(grad_all, part), activated],
            [],
            (width, slice_rows),
        )
        down_parts = exchange(
            [
                lax.dynamic_slice_in_dim(
                    down_grad, places[rank] * (width // 8), width // 8, 0
                )
                for rank in range(8)
            ]
        )
        up_grad = mlp_call(
            mlp_outer_kernel,
            "mlp_outer",
            [],
            [after(grad_hidden, down_grad), three_all],
            [],
            (slice_rows, width),
        )
        up_sum = sum_z_one(up_grad)
        (out_part,) = mlp_call(
            mlp_down_kernel,
            "mlp_down",
            [down_slice],
            [after(activated, up_grad)],
            [(width, bf16)],
        )
        down_whole = stack_by_device([after(part, out_part) for part in down_parts])
        down_cube = down_whole.reshape(seq, -1, slice_rows)
        down_sum = [
            z_shift(
                lax.dynamic_index_in_dim(down_cube, (at_z + step) % seq, 0, keepdims=False), step
            )
            if step
            else lax.dynamic_index_in_dim(down_cube, at_z, 0, keepdims=False)
            for step in range(seq)
        ]
        level_zero = norm_gain(after(both_sent, out_part).T.astype(f32), gain_skip).astype(bf16)
        grad_level_three = after(grad_level_three, level_zero, down_cube).astype(f32)
    else:
        grad_act = dot(down_t, chip_grad, TN)
        _, gelu_pull = jax.vjp(gelu_tanh, hidden)
        grad_hidden = gelu_pull(grad_act)[0].astype(bf16)
        down_outer = outer_of((with_other(activated), [with_other(chip_grad)]))
        up_outer = outer_of((with_other(level_three), [with_other(grad_hidden)]))
        grad_level_three = dot(up_t, grad_hidden, TN)
    zero_pair = with_other(level_zero)
    _, pull_three = jax.vjp(norm_gain, stream_two, gain_three)
    grad_from_three, grad_gain_three = pull_three(grad_level_three)
    grad_stream_two = chip_grad.astype(f32) + grad_from_three
    cross_back = grad_stream_two.astype(bf16)
    grad_crossed = dot(cout_t, cross_back, TN).astype(bf16)
    grad_cross, grad_tk, grad_tv = attend_back(
        cross, grad_crossed, crossed, cross_inverse, text_keys, text_values
    )
    grad_memory_key = grad_tk[0] + swap(grad_tk[1], "c").astype(f32)
    grad_memory_value = grad_tv[0] + swap(grad_tv[1], "c").astype(f32)
    _, pull_memory = jax.vjp(head_norm, memory_key_flat)
    grad_memory_proj = jnp.concatenate(
        [pull_memory(grad_memory_key)[0], grad_memory_value], axis=0
    ).astype(bf16)
    _, pull_cq = jax.vjp(head_norm, cross_proj)
    grad_cq_flat = pull_cq(grad_cross)[0].astype(bf16)
    early = up_sum + down_sum if square else []
    grad_level_two = dot(cq_t, grad_cq_flat, TN)
    _, pull_two = jax.vjp(norm_gain, stream_one, gain_two)
    grad_from_two, grad_gain_two = pull_two(grad_level_two)
    grad_stream_one = grad_stream_two + grad_from_two
    self_back = grad_stream_one.astype(bf16)
    cross_outer = outer_of(
        (crossed_pair, [with_other(cross_back)]),
        (two_pair, [with_other(grad_cq_flat)]),
        (attended_pair, [with_other(self_back)]),
    )
    memory_outer = outer_of((text_pair, [with_other(grad_memory_proj)]))
    if square:
        cross_sum = sum_far(cross_outer)
        memory_sum = sum_far(memory_outer)
    grad_attended = dot(
        self_t, after(self_back, cross_outer[0], memory_outer[0]), TN
    ).astype(bf16)
    grad_q, grad_k, grad_v = attend_back(
        query, grad_attended, attended, self_inverse, keys, values
    )
    if square:
        cross_sum = sum_near(cross_sum, grad_q)
        memory_sum = sum_near(memory_sum, grad_q)
        out_sum = lax.psum_scatter(
            after(out_part, grad_level_three), all_plane, scatter_dimension=0, tiled=True
        )[0]
        blended = (stream_two + after(out_sum, grad_q).astype(f32)).astype(bf16)
        grad_q = after(grad_q, blended, *early, *cross_sum[3], *memory_sum[3])
    grad_key = grad_k[0] + swap(grad_k[1], "c").astype(f32)
    grad_value_proj = (grad_v[0] + swap(grad_v[1], "c").astype(f32)).astype(bf16)
    _, pull_query = jax.vjp(prepare, query_flat)
    _, pull_key = jax.vjp(prepare, key_flat)
    grad_pair_proj = jnp.concatenate([pull_query(grad_q)[0], pull_key(grad_key)[0]], axis=0).astype(
        bf16
    )
    first_outer = outer_of(
        (one_pair, [with_other(grad_value_proj), with_other(grad_pair_proj)]),
    )
    if square:
        first_sum = sum_far(first_outer)
        cross_sum, stacked = sum_z_offloaded(cross_sum, first_outer[0])
        memory_sum = sum_z(memory_sum, first_outer[0])
    else:
        stacked = first_outer[0]
        blended = (stream_two + dot(down_t, activated)).astype(bf16)
    blended_out = from_latent(blended.T, first_outer[0])
    grad_text_rows = dot(grad_memory_proj, memory_t, TN).astype(bf16)
    grad_text = from_latent(grad_text_rows, first_outer[0]).astype(f32)
    grad_pair_next = after(grad_pair_proj, first_outer[0], stacked, blended_out, grad_text)
    grad_level_one = dot(pair_t, grad_pair_next, TN) + dot(value_t, grad_value_proj, TN)
    _, pull_one = jax.vjp(shifted_norm, stream_zero, gain_one, shift)
    grad_from_one, grad_gain_one, grad_shift_part = pull_one(grad_level_one)
    skip_back = (grad_stream_one + grad_from_one).astype(bf16)
    skip_outer = outer_of((zero_pair, [with_other(skip_back)]))
    late = skip_outer[0]
    if square:
        skip_sum = sum_far(skip_outer)
        first_sum = sum_near(first_sum, skip_outer[0])
        late = first_sum[3][0]
    skip_rows = from_latent(skip_back.T, late)
    skip_back_rows = skip_rows.reshape(tokens, width)
    grad_level_zero = dot(skip_back_rows, skip_t, NN)
    if square:
        skip_sum = sum_near(skip_sum, grad_level_zero)
        first_sum = sum_z(first_sum, *skip_sum[3])
        stacked = first_sum[0]
        grad_level_zero = after(grad_level_zero, stacked)
        (grad_up,) = sum_end(up_sum, up_set, stacked)
        down_total = sum(after(part, stacked).astype(f32) for part in down_sum)
        grad_down = (
            down_total.reshape(cores, -1, slice_rows)
            .transpose(0, 2, 1)
            .reshape(cores * slice_rows, -1)
        )
        skip_sum = sum_z(skip_sum, grad_level_zero)
        late = skip_sum[0]
        grad_cout, grad_cq, grad_self = sum_end(
            cross_sum, [cross_output, cross_query, self_output], late
        )
        (grad_memory,) = sum_end(memory_sum, memory_set, late)
        (grad_skip_w,) = sum_end(skip_sum, skip_set, grad_memory)
        grad_value, grad_pair = sum_end(
            first_sum, [value_weight, query_key_weight], grad_skip_w
        )
    else:
        (grad_down,) = sum_end(sum_plain(down_outer), down_set)
        (grad_up,) = sum_end(sum_plain(up_outer), up_set)
        grad_cout, grad_cq, grad_self = sum_end(
            sum_plain(cross_outer), [cross_output, cross_query, self_output]
        )
        (grad_memory,) = sum_end(sum_plain(memory_outer), memory_set)
        grad_value, grad_pair = sum_end(sum_plain(first_outer), [value_weight, query_key_weight])
        (grad_skip_w,) = sum_end(sum_plain(skip_outer), skip_set)

    cond_act = jax.nn.silu(gather_rows(condition, ("c", "b", "a")).astype(f32)).astype(bf16)
    block_in, block_out = shift_weight.shape
    cond_block = lax.dynamic_slice_in_dim(cond_act, at_z * block_in, block_in, 1).astype(f32)
    small = jnp.stack([grad_shift_part, grad_gain_one, grad_gain_two, grad_gain_three])
    small = after(small, late)
    if square:
        small = small + swap(small, "c")
        columns = z_order(z_send(small))
        shift_grads = jnp.concatenate([column[:1] for column in columns], axis=0)
        gain_part = sum(column[1:] for column in columns)
        for axis in ("b", "a"):
            carried = jnp.concatenate([gain_part, shift_grads], axis=0)
            other = swap(carried, axis)
            gain_part = gain_part + other[:3]
            lower = here[axis] == 0
            shift_grads = jnp.concatenate(
                [
                    jnp.where(lower, shift_grads, other[3:]),
                    jnp.where(lower, other[3:], shift_grads),
                ],
                axis=0,
            )
    else:
        gain_part = lax.psum(small[1:], ("a", "b", "c", "z"))
        shift_grads = lax.all_gather(lax.psum(small[:1], "c"), ("a", "b", "z"), axis=0, tiled=True)
    own_columns = ((at_a * inner + at_b) * cores + at_c) * block_out
    grad_shift = jnp.dot(
        cond_block.T,
        lax.dynamic_slice_in_dim(shift_grads, own_columns, block_out, 1),
        precision=lax.Precision.HIGHEST,
    )

    joined_rows = jnp.concatenate([inputs, skipped], axis=-1).astype(f32).reshape(tokens, -1)
    _, pull_zero = jax.vjp(norm_gain_rows, joined_rows, gain_skip)
    grad_joined, grad_gain_skip = pull_zero(grad_level_zero)
    grad_input = grad_joined[:, :width].reshape(inputs.shape)
    grad_skipped = grad_joined[:, width:].reshape(inputs.shape)
    grad_gains = jnp.concatenate([total_of(grad_gain_skip), gain_part.reshape(-1)])
    return (
        blended_out,
        grad_input,
        grad_skipped,
        grad_text,
        grad_gains,
        grad_skip_w,
        grad_shift,
        grad_pair,
        grad_value,
        grad_self,
        grad_cq,
        grad_memory,
        grad_cout,
        grad_up,
        grad_down,
    )


def solution(mesh):
    dp, seq = mesh.shape["dp"], mesh.shape["seq"]
    inner, cores = 2, 2
    sizes = (dp // (inner * cores), inner, cores, seq)
    split = Mesh(mesh.devices.reshape(sizes), ("a", "b", "c", "z"))
    rows = P(("a", "b", "c"), "z", None)
    blocks = P("z", ("a", "b", "c"))
    return jax.shard_map(
        functools.partial(on_device, sizes),
        mesh=split,
        in_specs=(rows, rows, rows, P(("a", "b", "c"), None), rows, P()) + (blocks,) * 10,
        out_specs=(rows, rows, rows, rows, P()) + (blocks,) * 10,
        check_vma=False,
    )
```

time: 1480 us -> 1290 us (0.87)
  waiting for transfers between devices: 555 us -> 352 us
  starting transfers between devices: 175 us -> 287 us
  matrix products: 148 us -> 68.7 us
  Pallas kernels: 208 us -> 253 us
  other arithmetic: 173 us -> 142 us
  local copies, waits for them, and re-layouts: 185 us -> 155 us
    ppermute x112 -> x79, waiting for transfers between devices: 322 us -> 111 us  [swap(): return lax.ppermute(values, axis, SWAP)]
    all_gather x3 -> x6, waiting for transfers between devices: 0.02 us -> 98.1 us  [the longest x1 51.3 us: on_device(): lax.all_gather(after(level_three, grad_all), all_plane, axis=0, tiled=False)]
    ppermute x8, waiting for transfers between devices: 95.3 us -> 7.5 us  [to_latent(): parts.append(lax.ppermute(chosen, ('c', 'z'), route(step)))]
    dot_general x19 -> x15, matrix products: 146 us -> 67.6 us  [dot(): return lax.dot_general(a, b, (dims, ((), ())), preferred_element_type=f32)]
    pallas_call x9 -> x20, Pallas kernels: 98.8 us -> 162 us  [the longest x5 90.1 us: mlp_call(): pl.pallas_call(kernel, grid=(count,), in_specs=[kept(x.shape) for x in he...]
    ppermute x18 -> x27, starting transfers between devices: 33.9 us -> 83.3 us  [z_shift(): lax.ppermute(values, 'z', [(z, (z + step) % seq) for z in range(seq)])]
    ppermute x18 -> x27, waiting for transfers between devices: 114 us -> 71.2 us  [z_shift(): lax.ppermute(values, 'z', [(z, (z + step) % seq) for z in range(seq)])]
    ppermute x112 -> x79, starting transfers between devices: 89.5 us -> 129 us  [swap(): return lax.ppermute(values, axis, SWAP)]
  transfers between devices with their start and end apart: 153 -> 150, of which waited for: 43 -> 35; matrix products, arithmetic and copies ran while one was open for 28% -> 24% of each run, Pallas kernels for 14% -> 15%
where the time goes in v2:
time: 1290 us; the launch traced here: 1270 us
  waiting for transfers between devices  352 us (27%)
  starting transfers between devices  287 us (22%)
  Pallas kernels  253 us (20%)
  local copies, waits for them, and re-layouts  155 us (12%)
  other arithmetic  142 us (11%)
  matrix products  68.7 us (5%)
  between operations  17.4 us (1%)
    ppermute x79, starting transfers between devices, swap(): return lax.ppermute(values, axis, SWAP)  129 us
    ppermute x79, waiting for transfers between devices, swap(): return lax.ppermute(values, axis, SWAP)  111 us
    pallas_call x5, Pallas kernels, mlp_call(): pl.pallas_call(kernel, grid=(count,), in_specs=[kept(x.shape) for x in he...  90.1 us
    ppermute x27, starting transfers between devices, z_shift(): lax.ppermute(values, 'z', [(z, (z + step) % seq) for z in range(seq)])  83.3 us
    ppermute x27, waiting for transfers between devices, z_shift(): lax.ppermute(values, 'z', [(z, (z + step) % seq) for z in range(seq)])  71.2 us
    dot_general x15, matrix products, dot(): return lax.dot_general(a, b, (dims, ((), ())), preferred_element_type=f32)  67.6 us
    unnamed x450, local copies, waits for them, and re-layouts  66.3 us
    all_gather x1, waiting for transfers between devices, on_device(): lax.all_gather(after(level_three, grad_all), all_plane, axis=0, tiled=False)  51.3 us
  transfers between devices with their start and end apart: 150, of which 35 were waited for; matrix products, arithmetic and copies ran while one was open for 24% of the time, Pallas kernels for 15%

profile of v2, /device:TPU:0, one launch (start us, length us, event | category | flops | bytes accessed | tf_op | source)
XLA Modules:
  0.0 1274.3 jit_solution(11116374027641352415)
XLA Ops:
  23.1 22.4 %collective-permute-done.1.refs_2_ = bf16[176,704]{1,0:T(8,128)(2,1)S(1)} collective-permute-done((bf16[176,704]{1,0:T(8,128)(2,1)}, bf16[176,704]{1,0:T(8,128)(2,1)S(1)}, u32[]{:S(2)}, u32[]{:S(2)}) %collective-permute-start.1) | collective-permute-done | bytes 247840 | tf_op jit(solution)/shard_map/ppermute | solution.py:620
  50.4 20.7 %collective-permute-done.4.refs_3_ = bf16[176,2816]{1,0:T(8,128)(2,1)S(1)} collective-permute-done((bf16[176,2816]{1,0:T(8,128)(2,1)S(1)}, bf16[176,2816]{1,0:T(8,128)(2,1)S(1)}, u32[]{:S(2)}, u32[]{:S(2)}) %collective-permute-start.4) | collective-permute-done | bytes 991264 | tf_op jit(solution)/shard_map/ppermute | solution.py:543
  101.1 18.7 %collective-permute-start.59 = (bf16[256,1408]{0,1:T(8,128)(2,1)}, bf16[256,1408]{0,1:T(8,128)(2,1)}, u32[]{:S(2)}, u32[]{:S(2)}) collective-permute-start(bf16[256,1408]{0,1:T(8,128)(2,1)} %bitcast.281), channel_id=1, source_target_pairs={{0,1},{1,0},{2,5},{3,4},{4,3},{5,2},{6,7},{7,6},{8,9},{9,8},{10,13... | collective-permute-start | bytes 2162696 | tf_op jit(solution)/shard_map/ppermute | solution.py:594
  170.2 17.4 %collective-permute-start.23 = (bf16[704,1408]{1,0:T(8,128)(2,1)S(1)}, bf16[704,1408]{1,0:T(8,128)(2,1)}, u32[]{:S(2)}, u32[]{:S(2)}) collective-permute-start(bf16[704,1408]{1,0:T(8,128)(2,1)S(1)} %join_gathered.4.refs_1_), channel_id=1, source_target_pairs={{0,4},{4,0},{1,5},{5,1},{2,6},{6,2},{3,7},{7,3},{8,12},{12,8},{9,1... | collective-permute-start | bytes 5947400 | tf_op jit(solution)/shard_map/ppermute | solution.py:543
  214.7 12.0 collective-permute-start.27
  279.0 10.1 collective-permute-done.32.refs_3_
  292.7 11.2 attend.2
  333.2 15.6 %collective-permute-done.41.refs_5_ = bf16[176,1024]{1,0:T(8,128)(2,1)} collective-permute-done((bf16[176,1024]{1,0:T(8,128)(2,1)}, bf16[176,1024]{1,0:T(8,128)(2,1)}, u32[]{:S(2)}, u32[]{:S(2)}) %collective-permute-start.41) | collective-permute-done | bytes 360480 | tf_op jit(solution)/shard_map/ppermute | solution.py:543
  417.8 17.6 %all-gather.17.cloned.1.call-done = bf16[704,1536]{1,0:T(8,128)(2,1)} async-done(((bf16[176,1536]{1,0:T(8,128)(2,1)}), bf16[704,1536]{1,0:T(8,128)(2,1)}) %all-gather.17.cloned.1.call-update) | async-done | bytes 2162704 | tf_op jit(solution)/shard_map/all_gather | solution.py:798
  453.6 29.2 %all-gather.19.cloned.1.call-done = bf16[3072,352]{0,1:T(8,128)(2,1)} async-done(((bf16[768,352]{0,1:T(8,128)(2,1)}), bf16[3072,352]{0,1:T(8,128)(2,1)}) %all-gather.19.cloned.1.call-update) | async-done | bytes 2162704 | tf_op jit(solution)/shard_map/all_gather | solution.py:797
  499.8 51.3 %all-gather.23.cloned.1.call-done = bf16[11264,512]{1,0:T(8,128)(2,1)} async-done(((bf16[1408,512]{1,0:T(8,128)(2,1)}), bf16[11264,512]{1,0:T(8,128)(2,1)}) %all-gather.23.cloned.1.call-update) | async-done | bytes 11534352 | tf_op jit(solution)/shard_map/all_gather | solution.py:925
  552.7 18.0 %mlp_up.1 = (f32[8,768,512]{2,1,0:T(8,128)}, bf16[8,768,512]{2,1,0:T(8,128)(2,1)}) custom-call(bf16[768,1408]{1,0:T(8,128)(2,1)S(1)} %copy-done.2, bf16[8,1408,512]{2,1,0:T(8,128)(2,1)} %bitcast.301), custom_call_target="tpu_custom_call" | custom-call | flops 8858370048 | bytes 30408704 | tf_op jit(solution)/shard_map/mlp_up/pallas_call | solution.py:522
  570.6 28.4 %mlp_back.1 = (bf16[8,768,512]{2,1,0:T(8,128)(2,1)}, bf16[8,1408,512]{2,1,0:T(8,128)(2,1)}) custom-call(bf16[768,1408]{1,0:T(8,128)(2,1)S(1)} %bitcast.210, bf16[1408,768]{1,0:T(8,128)(2,1)S(1)} %bitcast.209, bf16[8,1408,512]{2,1,0:T(8,128)(2,1)} %bitcast.299, f32[8,768,512]{2,1,0:T(8,128)} %get-tuple-element.222.hidden_ref), custom_call_target="tpu_custom_call" | custom-call | flops 17716740096 | bytes 44564480 | tf_op jit(solution)/shard_map/mlp_back/pallas_call | solution.py:522
  599.1 15.2 %mlp_outer.2 = bf16[1408,768]{1,0:T(8,128)(2,1)S(1)} custom-call(bf16[8,1408,512]{2,1,0:T(8,128)(2,1)} %bitcast.300, bf16[8,768,512]{2,1,0:T(8,128)(2,1)} %get-tuple-element.227.b_ref.act_ref), custom_call_target="tpu_custom_call" | custom-call | flops 8858370048 | bytes 17825792 | tf_op jit(solution)/shard_map/mlp_outer/pallas_call | solution.py:522
  615.7 14.6 %mlp_outer.3.refs_0_ = bf16[768,1408]{1,0:T(8,128)(2,1)S(1)} custom-call(bf16[8,768,512]{2,1,0:T(8,128)(2,1)} %get-tuple-element.226.a_ref, bf16[8,1408,512]{2,1,0:T(8,128)(2,1)} %bitcast.302), custom_call_target="tpu_custom_call" | custom-call | flops 8858370048 | bytes 17825792 | tf_op jit(solution)/shard_map/mlp_outer/pallas_call | solution.py:522
  631.7 14.0 %mlp_down.1 = bf16[8,1408,512]{2,1,0:T(8,128)(2,1)} custom-call(bf16[1408,768]{1,0:T(8,128)(2,1)S(1)} %assemble.10.down_ref, bf16[8,768,512]{2,1,0:T(8,128)(2,1)} %get-tuple-element.227.b_ref.act_ref), custom_call_target="tpu_custom_call" | custom-call | flops 8858370048 | bytes 23592960 | tf_op jit(solution)/shard_map/mlp_down/pallas_call | solution.py:522
  656.5 12.4 collective-permute-start.60
  730.1 13.5 %attend_back.2 = (f32[1408,512]{1,0:T(8,128)}, f32[1408,128]{1,0:T(8,128)}, bf16[1408,128]{1,0:T(8,128)(2,1)}, f32[1408,128]{1,0:T(8,128)}, bf16[1408,128]{1,0:T(8,128)(2,1)}) custom-call(bf16[1408,512]{1,0:T(8,128)(2,1)} %copy-done.21, bf16[1408,512]{1,0:T(8,128)(2,1)} %convolution_convert_fusion.1.refs_1_, bf16[1408,512]{1,0:T(8,128)(2,1)} %copy-done.57, ...), custom_call_target="tpu_custom_call" | custom-call | flops 2684354560 | bytes 12976128 | tf_op jit(solution)/shard_map/attend_back/pallas_call | solution.py:176
  781.5 12.9 %collective-permute-done.91 = bf16[176,1024]{1,0:T(8,128)(2,1)} collective-permute-done((bf16[176,1024]{1,0:T(8,128)(2,1)}, bf16[176,1024]{1,0:T(8,128)(2,1)}, u32[]{:S(2)}, u32[]{:S(2)}) %collective-permute-start.91) | collective-permute-done | bytes 360480 | tf_op jit(solution)/shard_map/ppermute | solution.py:543
  817.2 16.0 %outer_blocks.4 = (bf16[256,1408]{1,0:T(8,128)(2,1)}, bf16[272,1408]{1,0:T(8,128)(2,1)}, bf16[528,1408]{1,0:T(8,128)(2,1)}, bf16[528,1408]{1,0:T(8,128)(2,1)}, bf16[528,1408]{1,0:T(8,128)(2,1)}) custom-call(s32[4]{0:T(128)} %pad_add_fusion.3.place_ref, bf16[1408,512]{1,0:T(8,128)(2,1)} %fusion.40.refs_0_, bf16[1408,512]{1,0:T(8,128)(2,1)} %collective-permute-done.69.refs_1_, ...), custom_call_target="tpu_custom_call" | custom-call | flops 6090129408 | bytes 17481728 | tf_op jit(solution)/shard_map/outer_blocks/pallas_call | solution.py:319
  838.7 27.4 %attend_back.3 = (f32[1408,512]{1,0:T(8,128)}, f32[1408,512]{1,0:T(8,128)}, bf16[1408,512]{1,0:T(8,128)(2,1)}, f32[1408,512]{1,0:T(8,128)}, bf16[1408,512]{1,0:T(8,128)(2,1)}) custom-call(bf16[1408,512]{1,0:T(8,128)(2,1)} %bitcast.216, bf16[1408,512]{1,0:T(8,128)(2,1)} %convolution_convert_fusion.refs_1_, bf16[1408,512]{1,0:T(8,128)(2,1)} %copy-done.55, ...), custom_call_target="tpu_custom_call" | custom-call | flops 10737418240 | bytes 25952256 | tf_op jit(solution)/shard_map/attend_back/pallas_call | solution.py:176
  889.7 20.7 %collective-permute-done.86 = bf16[352,768]{1,0:T(8,128)(2,1)S(1)} collective-permute-done((bf16[352,768]{1,0:T(8,128)(2,1)S(1)}, bf16[352,768]{1,0:T(8,128)(2,1)S(1)}, u32[]{:S(2)}, u32[]{:S(2)}) %collective-permute-start.86) | collective-permute-done | bytes 540704 | tf_op jit(solution)/shard_map/ppermute | solution.py:620
  928.6 12.2 collective-permute-start.81
  954.7 13.5 %outer_blocks.6 = (bf16[256,1408]{1,0:T(8,128)(2,1)}, bf16[272,1408]{1,0:T(8,128)(2,1)}, bf16[528,1408]{1,0:T(8,128)(2,1)}, bf16[528,1408]{1,0:T(8,128)(2,1)}, bf16[528,1408]{1,0:T(8,128)(2,1)}) custom-call(s32[4]{0:T(128)} %pad_add_fusion.3.place_ref, bf16[1408,512]{1,0:T(8,128)(2,1)} %copy-done.117, bf16[1408,512]{1,0:T(8,128)(2,1)} %copy-done.213, ...), custom_call_target="tpu_custom_call" | custom-call | flops 6090129408 | bytes 17481728 | tf_op jit(solution)/shard_map/outer_blocks/pallas_call | solution.py:319
  968.2 21.3 %collective-permute-start.103 = (bf16[2816,512]{1,0:T(8,128)(2,1)}, bf16[2816,512]{1,0:T(8,128)(2,1)}, u32[]{:S(2)}, u32[]{:S(2)}) collective-permute-start(bf16[2816,512]{1,0:T(8,128)(2,1)} %fusion.36.refs_2_), channel_id=1, source_target_pairs={{0,4},{4,0},{1,5},{5,1},{2,6},{6,2},{3,7},{7,3},{8,12},{12,8},{9,1... | collective-permute-start | bytes 8650760 | tf_op jit(solution)/shard_map/ppermute | solution.py:543
  1000.0 10.4 fusion.83
  1025.7 10.1 collective-permute-done.108
  1053.7 25.0 %collective-permute-done.104 = bf16[256,1408]{0,1:T(8,128)(2,1)S(1)} collective-permute-done((bf16[256,1408]{0,1:T(8,128)(2,1)S(1)}, bf16[256,1408]{0,1:T(8,128)(2,1)S(1)}, u32[]{:S(2)}, u32[]{:S(2)}) %collective-permute-start.104) | collective-permute-done | bytes 720928 | tf_op jit(solution)/shard_map/ppermute | solution.py:603
  1083.3 10.9 fusion.97
  1098.1 11.3 collective-permute-done.107
  1216.9 12.7 %collective-permute-done.135 = bf16[176,704]{1,0:T(8,128)(2,1)S(1)} collective-permute-done((bf16[176,704]{1,0:T(8,128)(2,1)S(1)}, bf16[176,704]{1,0:T(8,128)(2,1)S(1)}, u32[]{:S(2)}, u32[]{:S(2)}) %collective-permute-start.135) | collective-permute-done | bytes 247840 | tf_op jit(solution)/shard_map/ppermute | solution.py:620
  1229.7 27.6 %collective-permute-start.138 = (bf16[528,352]{1,0:T(8,128)(2,1)S(1)}, bf16[528,352]{1,0:T(8,128)(2,1)S(1)}, u32[]{:S(2)}, u32[]{:S(2)}) collective-permute-start(bf16[528,352]{1,0:T(8,128)(2,1)S(1)} %copy-done.59), channel_id=1, source_target_pairs={{0,1},{1,2},{2,3},{3,0},{4,5},{5,6},{6,7},{7,4},{8,9},{9,10},{10,1... | collective-permute-start | bytes 1115144 | tf_op jit(solution)/shard_map/ppermute | solution.py:620
  (994 shorter events, 682.5 us)
Async XLA Ops:
  7.2 68.7 %all-gather.13.cloned.1.call-start = ((), (), s32[]{:S(2)}) async-start(), calls=%async_computation.6 | async-start | bytes 2703360 | tf_op jit(solution)/shard_map/all_gather | solution.py:795
  10.2 195.9 %all-gather.15.cloned.1.call-start = ((), (), s32[]{:S(2)}) async-start(), calls=%async_computation.7 | async-start | bytes 2027520 | tf_op jit(solution)/shard_map/all_gather | solution.py:796
  80.9 57.6 %collective-permute-start.14 = (bf16[704,1408]{1,0:T(8,128)(2,1)S(1)}, bf16[704,1408]{1,0:T(8,128)(2,1)}, u32[]{:S(2)}, u32[]{:S(2)}) collective-permute-start(bf16[704,1408]{1,0:T(8,128)(2,1)S(1)} %join_gathered.4.refs_1_), channel_id=1, source_target_pairs={{0,8},{8,0},{1,9},{9,1},{2,10},{10,2},{3,11},{11,3},{4,12},{12,4},... | collective-permute-start | bytes 5947400 | tf_op jit(solution)/shard_map/ppermute | solution.py:543
  81.5 65.7 %collective-permute-start.15 = (bf16[704,1408]{1,0:T(8,128)(2,1)S(1)}, bf16[704,1408]{1,0:T(8,128)(2,1)}, u32[]{:S(2)}, u32[]{:S(2)}) collective-permute-start(bf16[704,1408]{1,0:T(8,128)(2,1)S(1)} %join_gathered.4.refs_1_), channel_id=1, source_target_pairs={{0,16},{16,0},{1,17},{17,1},{2,18},{18,2},{3,19},{19,3},{4,20},{20... | collective-permute-start | bytes 5947400 | tf_op jit(solution)/shard_map/ppermute | solution.py:543
  84.6 333.1 %all-gather.21.cloned.1.call-start = ((), (), s32[]{:S(2)}) async-start(), calls=%async_computation.10 | async-start | bytes 12976128 | tf_op jit(solution)/shard_map/all_gather | solution.py:898
  101.1 54.8 %collective-permute-start.59 = (bf16[256,1408]{0,1:T(8,128)(2,1)}, bf16[256,1408]{0,1:T(8,128)(2,1)}, u32[]{:S(2)}, u32[]{:S(2)}) collective-permute-start(bf16[256,1408]{0,1:T(8,128)(2,1)} %bitcast.281), channel_id=1, source_target_pairs={{0,1},{1,0},{2,5},{3,4},{4,3},{5,2},{6,7},{7,6},{8,9},{9,8},{10,13... | collective-permute-start | bytes 2162696 | tf_op jit(solution)/shard_map/ppermute | solution.py:594
  170.2 58.7 %collective-permute-start.23 = (bf16[704,1408]{1,0:T(8,128)(2,1)S(1)}, bf16[704,1408]{1,0:T(8,128)(2,1)}, u32[]{:S(2)}, u32[]{:S(2)}) collective-permute-start(bf16[704,1408]{1,0:T(8,128)(2,1)S(1)} %join_gathered.4.refs_1_), channel_id=1, source_target_pairs={{0,4},{4,0},{1,5},{5,1},{2,6},{6,2},{3,7},{7,3},{8,12},{12,8},{9,1... | collective-permute-start | bytes 5947400 | tf_op jit(solution)/shard_map/ppermute | solution.py:543
  305.1 130.3 %all-gather.17.cloned.1.call-start = ((), (), s32[]{:S(2)}) async-start(), calls=%async_computation.8 | async-start | bytes 2703360 | tf_op jit(solution)/shard_map/all_gather | solution.py:798
  305.7 177.2 %all-gather.19.cloned.1.call-start = ((), (), s32[]{:S(2)}) async-start(), calls=%async_computation.9 | async-start | bytes 2703360 | tf_op jit(solution)/shard_map/all_gather | solution.py:797
  356.5 194.6 %all-gather.23.cloned.1.call-start = ((), (), s32[]{:S(2)}) async-start(), calls=%async_computation.11 | async-start | bytes 12976128 | tf_op jit(solution)/shard_map/all_gather | solution.py:925
  417.7 297.7 %reduce-scatter.4.cloned.1.call-start = ((), (), s32[]{:S(2)}) async-start(), calls=%async_computation.3 | async-start | bytes 12976128 | tf_op jit(solution)/shard_map/reduce_scatter | solution.py:957
  441.4 53.9 %collective-permute-start.53 = (bf16[176,768]{1,0:T(8,128)(2,1)}, bf16[176,768]{1,0:T(8,128)(2,1)S(1)}, u32[]{:S(2)}, u32[]{:S(2)}) collective-permute-start(bf16[176,768]{1,0:T(8,128)(2,1)} %get-tuple-element.449), channel_id=1, source_target_pairs={{0,24},{8,16},{16,8},{24,0},{1,25},{9,17},{17,9},{25,1},{2,26},{10... | collective-permute-start | bytes 811016 | tf_op jit(solution)/shard_map/ppermute | solution.py:669
  442.0 53.4 %collective-permute-start.54 = (bf16[176,768]{1,0:T(8,128)(2,1)}, bf16[176,768]{1,0:T(8,128)(2,1)}, u32[]{:S(2)}, u32[]{:S(2)}) collective-permute-start(bf16[176,768]{1,0:T(8,128)(2,1)} %get-tuple-element.448), channel_id=1, source_target_pairs={{0,4},{4,0},{1,5},{5,1},{2,6},{6,2},{3,7},{7,3},{8,12},{12,8},{9,1... | collective-permute-start | bytes 811016 | tf_op jit(solution)/shard_map/ppermute | solution.py:669
  442.0 53.4 %collective-permute-start.55 = (bf16[176,768]{1,0:T(8,128)(2,1)}, bf16[176,768]{1,0:T(8,128)(2,1)}, u32[]{:S(2)}, u32[]{:S(2)}) collective-permute-start(bf16[176,768]{1,0:T(8,128)(2,1)} %get-tuple-element.447), channel_id=1, source_target_pairs={{0,12},{4,8},{8,4},{12,0},{1,13},{5,9},{9,5},{13,1},{2,14},{6,10},... | collective-permute-start | bytes 811016 | tf_op jit(solution)/shard_map/ppermute | solution.py:669
  599.1 267.0 %reduce-scatter.6.cloned.1.call-start = ((), (), s32[]{:S(2)}) async-start(), calls=%async_computation.4 | async-start | bytes 12976128 | tf_op jit(solution)/shard_map/reduce_scatter | solution.py:1051
  645.7 543.8 %reduce-scatter.8.cloned.1.call-start = ((), (), s32[]{:S(2)}) async-start(), calls=%async_computation.5 | async-start | bytes 2027520 | tf_op jit(solution)/shard_map/reduce_scatter | solution.py:755
  652.3 56.6 %collective-permute-start.61 = (bf16[256,2816]{0,1:T(8,128)(2,1)}, bf16[256,2816]{0,1:T(8,128)(2,1)}, u32[]{:S(2)}, u32[]{:S(2)}) collective-permute-start(bf16[256,2816]{0,1:T(8,128)(2,1)} %bitcast.272), channel_id=1, source_target_pairs={{0,1},{1,0},{2,5},{3,4},{4,3},{5,2},{6,7},{7,6},{8,9},{9,8},{10,13... | collective-permute-start | bytes 4325384 | tf_op jit(solution)/shard_map/ppermute | solution.py:594
  696.4 78.7 %collective-permute-start.136 = (bf16[4,1408]{1,0:T(4,128)(2,1)}, bf16[4,1408]{1,0:T(4,128)(2,1)}, u32[]{:S(2)}, u32[]{:S(2)}) collective-permute-start(bf16[4,1408]{1,0:T(4,128)(2,1)} %pad_maximum_fusion.20), channel_id=1, source_target_pairs={{0,8},{8,0},{1,9},{9,1},{2,10},{10,2},{3,11},{11,3},{4,12},{12,4},... | collective-permute-start | bytes 33800 | tf_op jit(solution)/shard_map/ppermute | solution.py:543
  706.9 68.4 %collective-permute-start.74 = (bf16[1408,512]{1,0:T(8,128)(2,1)}, bf16[1408,512]{1,0:T(8,128)(2,1)}, u32[]{:S(2)}, u32[]{:S(2)}) collective-permute-start(bf16[1408,512]{1,0:T(8,128)(2,1)} %copy-done.55), channel_id=1, source_target_pairs={{0,4},{4,0},{1,5},{5,1},{2,6},{6,2},{3,7},{7,3},{8,12},{12,8},{9,1... | collective-permute-start | bytes 4325384 | tf_op jit(solution)/shard_map/ppermute | solution.py:543
  706.9 61.8 %collective-permute-start.78 = (bf16[1024,128]{1,0:T(8,128)(2,1)}, bf16[1024,128]{1,0:T(8,128)(2,1)}, u32[]{:S(2)}, u32[]{:S(2)}) collective-permute-start(bf16[1024,128]{1,0:T(8,128)(2,1)} %bitcast.278), channel_id=1, source_target_pairs={{0,4},{4,0},{1,5},{5,1},{2,6},{6,2},{3,7},{7,3},{8,12},{12,8},{9,1... | collective-permute-start | bytes 786440 | tf_op jit(solution)/shard_map/ppermute | solution.py:543
  708.9 102.5 %collective-permute-start.72 = (bf16[1408,512]{1,0:T(8,128)(2,1)}, bf16[1408,512]{1,0:T(8,128)(2,1)}, u32[]{:S(2)}, u32[]{:S(2)}) collective-permute-start(bf16[1408,512]{1,0:T(8,128)(2,1)} %copy-done.57), channel_id=1, source_target_pairs={{0,4},{4,0},{1,5},{5,1},{2,6},{6,2},{3,7},{7,3},{8,12},{12,8},{9,1... | collective-permute-start | bytes 4325384 | tf_op jit(solution)/shard_map/ppermute | solution.py:543
  811.5 62.1 %collective-permute-start.82 = (bf16[768,352]{0,1:T(8,128)(2,1)}, bf16[768,352]{0,1:T(8,128)(2,1)S(1)}, u32[]{:S(2)}, u32[]{:S(2)}) collective-permute-start(bf16[768,352]{0,1:T(8,128)(2,1)} %copy.117), channel_id=1, source_target_pairs={{0,1},{1,2},{2,3},{3,0},{4,5},{5,6},{6,7},{7,4},{8,9},{9,10},{10,1... | collective-permute-start | bytes 1622024 | tf_op jit(solution)/shard_map/ppermute | solution.py:620
  812.4 61.2 %collective-permute-start.83 = (bf16[768,352]{0,1:T(8,128)(2,1)}, bf16[768,352]{0,1:T(8,128)(2,1)}, u32[]{:S(2)}, u32[]{:S(2)}) collective-permute-start(bf16[768,352]{0,1:T(8,128)(2,1)} %copy.118), channel_id=1, source_target_pairs={{0,2},{1,3},{2,0},{3,1},{4,6},{5,7},{6,4},{7,5},{8,10},{9,11},{10,... | collective-permute-start | bytes 1622024 | tf_op jit(solution)/shard_map/ppermute | solution.py:620
  815.3 73.8 %collective-permute-start.84 = (bf16[768,352]{0,1:T(8,128)(2,1)}, bf16[768,352]{0,1:T(8,128)(2,1)}, u32[]{:S(2)}, u32[]{:S(2)}) collective-permute-start(bf16[768,352]{0,1:T(8,128)(2,1)} %copy.119), channel_id=1, source_target_pairs={{0,3},{1,0},{2,1},{3,2},{4,7},{5,4},{6,5},{7,6},{8,11},{9,8},{10,9... | collective-permute-start | bytes 1622024 | tf_op jit(solution)/shard_map/ppermute | solution.py:620
  815.5 52.7 %collective-permute-start.90 = (bf16[176,1024]{1,0:T(8,128)(2,1)}, bf16[176,1024]{1,0:T(8,128)(2,1)}, u32[]{:S(2)}, u32[]{:S(2)}) collective-permute-start(bf16[176,1024]{1,0:T(8,128)(2,1)} %get-tuple-element.247), channel_id=1, source_target_pairs={{0,8},{8,0},{1,9},{9,1},{2,10},{10,2},{3,11},{11,3},{4,12},{12,4},... | collective-permute-start | bytes 1081352 | tf_op jit(solution)/shard_map/ppermute | solution.py:543
  968.2 70.4 %collective-permute-start.103 = (bf16[2816,512]{1,0:T(8,128)(2,1)}, bf16[2816,512]{1,0:T(8,128)(2,1)}, u32[]{:S(2)}, u32[]{:S(2)}) collective-permute-start(bf16[2816,512]{1,0:T(8,128)(2,1)} %fusion.36.refs_2_), channel_id=1, source_target_pairs={{0,4},{4,0},{1,5},{5,1},{2,6},{6,2},{3,7},{7,3},{8,12},{12,8},{9,1... | collective-permute-start | bytes 8650760 | tf_op jit(solution)/shard_map/ppermute | solution.py:543
  1038.6 74.4 %collective-permute-start.109 = (bf16[528,1408]{1,0:T(8,128)(2,1)}, bf16[528,1408]{1,0:T(8,128)(2,1)S(1)}, u32[]{:S(2)}, u32[]{:S(2)}) collective-permute-start(bf16[528,1408]{1,0:T(8,128)(2,1)} %add_dynamic-update-slice_fusion), channel_id=1, source_target_pairs={{0,8},{8,0},{1,9},{9,1},{2,10},{10,2},{3,11},{11,3},{4,12},{12,4},... | collective-permute-start | bytes 4460552 | tf_op jit(solution)/shard_map/ppermute | solution.py:543
  1052.4 60.6 %collective-permute-start.105 = (bf16[528,1408]{1,0:T(8,128)(2,1)}, bf16[528,1408]{1,0:T(8,128)(2,1)S(1)}, u32[]{:S(2)}, u32[]{:S(2)}) collective-permute-start(bf16[528,1408]{1,0:T(8,128)(2,1)} %add_dynamic-update-slice_fusion.2), channel_id=1, source_target_pairs={{0,16},{16,0},{1,17},{17,1},{2,18},{18,2},{3,19},{19,3},{4,20},{20... | collective-permute-start | bytes 4460552 | tf_op jit(solution)/shard_map/ppermute | solution.py:543
  1097.6 54.1 %collective-permute-start.120 = (bf16[176,2816]{1,0:T(8,128)(2,1)}, bf16[176,2816]{1,0:T(8,128)(2,1)}, u32[]{:S(2)}, u32[]{:S(2)}) collective-permute-start(bf16[176,2816]{1,0:T(8,128)(2,1)} %add_dynamic-update-slice_fusion.5), channel_id=1, source_target_pairs={{0,16},{16,0},{1,17},{17,1},{2,18},{18,2},{3,19},{19,3},{4,20},{20... | collective-permute-start | bytes 2973704 | tf_op jit(solution)/shard_map/ppermute | solution.py:543
  1111.4 57.0 %collective-permute-start.121 = (bf16[176,2816]{1,0:T(8,128)(2,1)}, bf16[176,2816]{1,0:T(8,128)(2,1)}, u32[]{:S(2)}, u32[]{:S(2)}) collective-permute-start(bf16[176,2816]{1,0:T(8,128)(2,1)} %add_dynamic-update-slice_fusion.4), channel_id=1, source_target_pairs={{0,8},{8,0},{1,9},{9,1},{2,10},{10,2},{3,11},{11,3},{4,12},{12,4},... | collective-permute-start | bytes 2973704 | tf_op jit(solution)/shard_map/ppermute | solution.py:543
  1201.5 62.2 %collective-permute-start.140 = (bf16[528,352]{1,0:T(8,128)(2,1)S(1)}, bf16[528,352]{1,0:T(8,128)(2,1)}, u32[]{:S(2)}, u32[]{:S(2)}) collective-permute-start(bf16[528,352]{1,0:T(8,128)(2,1)S(1)} %copy-done.63), channel_id=1, source_target_pairs={{0,3},{1,0},{2,1},{3,2},{4,7},{5,4},{6,5},{7,6},{8,11},{9,8},{10,9... | collective-permute-start | bytes 1115144 | tf_op jit(solution)/shard_map/ppermute | solution.py:620
  1206.0 57.7 %collective-permute-start.139 = (bf16[528,352]{1,0:T(8,128)(2,1)S(1)}, bf16[528,352]{1,0:T(8,128)(2,1)}, u32[]{:S(2)}, u32[]{:S(2)}) collective-permute-start(bf16[528,352]{1,0:T(8,128)(2,1)S(1)} %copy-done.61), channel_id=1, source_target_pairs={{0,2},{1,3},{2,0},{3,1},{4,6},{5,7},{6,4},{7,5},{8,10},{9,11},{10,... | collective-permute-start | bytes 1115144 | tf_op jit(solution)/shard_map/ppermute | solution.py:620
  (339 other events, 5308.5 us)
Sparse Core Ops, SparseCore 0:
  10.4 64.2 all-gather.12
  84.7 68.7 all-gather.14
  305.2 81.5 all-gather.20
  388.2 47.1 all-gather.16
  436.8 45.9 all-gather.18
  484.6 66.4 all-gather.22
  599.2 95.1 reduce-scatter.3
  697.9 98.7 reduce-scatter.5
  1020.3 55.4 reduce-scatter.7

commit v3 on v2

--- a/solution.py
+++ b/solution.py
@@ -306,9 +306,11 @@
         for dy in pair
     ]
     x_buffers = {"pipeline_mode": once} if cut == width else {}
-    x_specs = [pl.BlockSpec((cut, tokens), lambda i, place: (i, 0), **x_buffers)] * (
-        2 * len(x_pairs)
-    )
+    x_specs = [
+        pl.BlockSpec((cut, x.shape[1]), lambda i, place: (i, 0), **x_buffers)
+        for pair in x_pairs
+        for x in pair
+    ]
     sizes = (half, rows - half, rows, rows, rows)
     if split:
         out_specs = [pl.BlockSpec((size, cut), lambda i, place: (0, i)) for size in sizes]
@@ -530,6 +532,125 @@
         cost_estimate=pl.CostEstimate(flops=flops, bytes_accessed=moved, transcendentals=0),
         name=name,
     )(*held, *streams)
+
+
+def join_two_kernel(gathered_ref, first_ref, second_ref):
+    seq = gathered_ref.shape[0]
+    top = 0
+    for out_ref in (first_ref, second_ref):
+        rows, part = out_ref.shape[0], out_ref.shape[1] // seq
+
+        def chunk(i, _, top=top, part=part, out_ref=out_ref):
+            at = pl.ds(pl.multiple_of(i * 16, 16), 16)
+            source = pl.ds(pl.multiple_of(top + i * 16, 16), 16)
+            out_ref[at, :] = jnp.concatenate(
+                [gathered_ref[j, source, :part] for j in range(seq)], axis=1
+            )
+            return 0
+
+        lax.fori_loop(0, rows // 16, chunk, 0)
+        top += rows
+
+
+def join_two(gathered, first, second):
+    seq = gathered.shape[0]
+    shapes = [(rows, seq * part) for rows, part in (first, second)]
+    return pl.pallas_call(
+        join_two_kernel,
+        in_specs=[pl.BlockSpec(memory_space=pltpu.VMEM)],
+        out_specs=[pl.BlockSpec(memory_space=pltpu.VMEM)] * 2,
+        out_shape=[jax.ShapeDtypeStruct(shape, bf16) for shape in shapes],
+        compiler_params=pltpu.CompilerParams(vmem_limit_bytes=32 * 2**20),
+        cost_estimate=pl.CostEstimate(
+            flops=0, bytes_accessed=4 * gathered.size, transcendentals=0
+        ),
+        name="join_two",
+    )(gathered)
+
+
+def unpack_kernel(wide, tall, packed_ref, up_ref, down_ref):
+    seq = packed_ref.shape[0]
+    up_rows, down_rows = tall
+    slabs = (packed_ref.shape[1] - up_rows) // down_rows
+
+    def chunk(i, _):
+        at = pl.ds(pl.multiple_of(i * 16, 16), 16)
+        up_ref[at, :] = jnp.concatenate([packed_ref[z, at, :wide] for z in range(seq)], axis=1)
+        return 0
+
+    lax.fori_loop(0, up_rows // 16, chunk, 0)
+    lanes = packed_ref.shape[2]
+    for z in range(seq):
+        for slab in range(slabs):
+            left = (z * slabs + slab) * lanes
+            top = up_rows + slab * down_rows
+            down_ref[:, left : left + lanes] = packed_ref[z, top : top + down_rows, :]
+
+
+def unpack(packed, seq, wide, tall):
+    devices, rows, lanes = packed.shape
+    blocks = devices // seq
+    up_rows, down_rows = tall
+    down_width = seq * lanes * ((rows - up_rows) // down_rows)
+    return pl.pallas_call(
+        functools.partial(unpack_kernel, wide, tall),
+        grid=(blocks,),
+        in_specs=[pl.BlockSpec((seq, rows, lanes), lambda p: (p, 0, 0))],
+        out_specs=[
+            pl.BlockSpec((up_rows, seq * wide), lambda p: (p, 0)),
+            pl.BlockSpec((down_rows, down_width), lambda p: (p, 0)),
+        ],
+        out_shape=[
+            jax.ShapeDtypeStruct((blocks * up_rows, seq * wide), bf16),
+            jax.ShapeDtypeStruct((blocks * down_rows, down_width), bf16),
+        ],
+        compiler_params=pltpu.CompilerParams(vmem_limit_bytes=40 * 2**20),
+        cost_estimate=pl.CostEstimate(
+            flops=0, bytes_accessed=4 * devices * rows * lanes, transcendentals=0
+        ),
+        name="unpack",
+    )(packed)
+
+
+def pack_kernel(up_ref, down_ref, out_ref):
+    seq, _, lanes = out_ref.shape
+    up_rows, up_width = up_ref.shape
+    part = up_width // seq
+    down_rows, down_width = down_ref.shape
+    block = down_rows // seq
+
+    def chunk(i, _):
+        at = pl.ds(pl.multiple_of(i * 16, 16), 16)
+        rows = up_ref[at, :]
+        fill = jnp.zeros((16, lanes - part), rows.dtype)
+        for z in range(seq):
+            out_ref[z, at, :] = jnp.concatenate(
+                [rows[:, z * part : (z + 1) * part], fill], axis=1
+            )
+        return 0
+
+    lax.fori_loop(0, up_rows // 16, chunk, 0)
+    for z in range(seq):
+        for slab in range(down_width // lanes):
+            top = up_rows + slab * block
+            out_ref[z, top : top + block, :] = down_ref[
+                z * block : (z + 1) * block, slab * lanes : (slab + 1) * lanes
+            ]
+
+
+def pack(up_grad, down_grad, seq, lanes):
+    rows = up_grad.shape[0] + down_grad.shape[0] // seq * (down_grad.shape[1] // lanes)
+    return pl.pallas_call(
+        pack_kernel,
+        in_specs=[pl.BlockSpec(memory_space=pltpu.VMEM)] * 2,
+        out_specs=pl.BlockSpec(memory_space=pltpu.VMEM),
+        out_shape=jax.ShapeDtypeStruct((seq, rows, lanes), bf16),
+        compiler_params=pltpu.CompilerParams(vmem_limit_bytes=32 * 2**20),
+        cost_estimate=pl.CostEstimate(
+            flops=0, bytes_accessed=4 * seq * rows * lanes, transcendentals=0
+        ),
+        name="pack",
+    )(up_grad, down_grad)
 
 
 def after(value, *others):
@@ -651,17 +772,6 @@
             )
         return values
 
-    def total_of(values):
-        if not square:
-            return lax.psum(values, ("a", "b", "c", "z"))
-        held = jnp.zeros((8,) + values.shape, values.dtype)
-        for rank in range(8):
-            arrived = to_rank(values, rank) if rank else values
-            held = lax.dynamic_update_slice(held, arrived[None], (places[rank], 0))
-        values = sum(held[i] for i in range(8))
-        values = sum(z_order(z_send(values)))
-        return values
-
     def to_rank(values, rank):
         axes = tuple(axis for axis, bit in (("c", 4), ("a", 2), ("b", 1)) if rank & bit)
         axes = tuple(axis for axis in ("a", "b", "c") if axis in axes)
@@ -745,10 +855,6 @@
         parts = cut_sum(at_z, seq, own, after(got_a, *others), got_b)
         return [parts[0]] + [z_shift(parts[step], step) for step in range(1, seq)]
 
-    def sum_z_one(total, *others):
-        parts = cut_sum(at_z, seq, after(total, *others))
-        return [parts[0]] + [z_shift(parts[step], step) for step in range(1, seq)]
-
     def sum_z_offloaded(state, *others):
         own, got_a, got_b, _ = state
         stacked = stack_sum(seq, own, after(got_a, *others), got_b)
@@ -776,7 +882,6 @@
     gain_two = norm_gains[3 * width : 4 * width]
     gain_three = norm_gains[4 * width :]
 
-    both_in = jnp.concatenate([inputs, skipped], axis=-1)
     skip_set = [skip_weight]
     pair_set = [query_key_weight, value_weight, shift_weight]
     self_set = [self_output, cross_query, cross_output]
@@ -788,21 +893,26 @@
     )
     if square:
         skip_sent = z_send(skip_flip)
-        self_flip = after(self_flip, pair_flip)
-        up_flip = after(up_flip, self_flip)
-        down_flip = after(down_flip, up_flip)
-        grad_sent = to_latent(after(cotangent, down_flip))
+        lanes = down_weight.shape[0] // seq
+        cross_flip = jnp.concatenate(
+            [
+                jnp.pad(one, ((0, 0), (0, lanes - one.shape[1])))
+                for one in (self_flip, memory_flip)
+            ],
+            axis=0,
+        )
+        cross_flip = after(cross_flip, pair_flip)
+        up_padded = jnp.pad(up_flip, ((0, 0), (0, lanes - up_flip.shape[1])))
+        slabs = [down_flip[:, i * lanes : (i + 1) * lanes] for i in range(seq)]
+        mlp_flip = jnp.concatenate([up_padded] + slabs, axis=0)
         pair_sent = lax.all_gather(pair_flip, "z", axis=0, tiled=False)
-        self_sent = lax.all_gather(self_flip, "z", axis=0, tiled=False)
-        up_sent = lax.all_gather(up_flip, "z", axis=0, tiled=False)
-        down_sent = lax.all_gather(down_flip, "z", axis=0, tiled=False)
+        cross_sent = lax.all_gather(cross_flip, "z", axis=0, tiled=False)
         skip_piece = z_piece(skip_sent)
         skip_near = hop_one(skip_piece)
         skip_half = halves(*skip_near)
         skip_far = hop_two(*skip_half)
         pair_piece = join_gathered(after(pair_sent, *skip_half))
         pair_near = hop_one(pair_piece)
-        memory_sent = z_send(after(memory_flip, pair_piece))
         skip_far = after_all(skip_far, pair_piece)
         skip_mine = (skip_piece,) + skip_near + skip_far
         skip_other = to_core(skip_mine)
@@ -814,22 +924,25 @@
             ],
             axis=0,
         ).astype(f32)
-        start_zero = dot(skip_t, norm_gain(joined, gain_skip).astype(bf16)).astype(bf16)
+        level_zero = norm_gain(joined, gain_skip).astype(bf16)
+        start_zero = dot(skip_t, level_zero).astype(bf16)
         zero_sent = to_latent(start_zero.T.reshape(inputs.shape))
         pair_near = after_all(pair_near, start_zero)
         pair_half = halves(*pair_near)
         pair_far = hop_two(*pair_half)
-        memory_piece = z_piece(memory_sent, *pair_half)
-        self_piece = join_gathered(after(self_sent, memory_piece))
+        self_piece, memory_piece = join_two(
+            after(cross_sent, *pair_half), self_flip.shape, memory_flip.shape
+        )
         pair_far = after_all(pair_far, self_piece)
         pair_mine = (pair_piece,) + pair_near + pair_far
         pair_other = to_core(pair_mine)
         self_near = hop_one(self_piece)
         memory_near = hop_one(memory_piece)
         stream_zero = after(zero_sent, *pair_far).T.astype(f32)
+        mlp_sent = lax.all_gather(after(mlp_flip, zero_sent), "z", axis=0, tiled=False)
         pair_t, value_t, shift_t = whole_of(pair_mine, pair_other, pair_set)
     else:
-        chip_both = to_latent(both_in)
+        chip_both = to_latent(jnp.concatenate([inputs, skipped], axis=-1))
         joined = chip_both.T.astype(f32)
         level_zero = norm_gain(joined, gain_skip).astype(bf16)
         chip_text = to_latent(text_rows).T
@@ -879,26 +992,31 @@
         self_near = after_all(self_near, query)
         self_half = halves(*self_near)
         self_far = hop_two(*self_half)
-        memory_near = after_all(memory_near, *self_half)
-        memory_half = halves(*memory_near)
-        memory_far = hop_two(*memory_half)
-        query_next = after(query, *memory_half)
+        query_next = after(query, *self_half)
     attended, self_inverse = attend(query_next, keys, values)
     attended_next = attended
     if square:
         all_plane = ("a", "b", "c")
-        up_piece = join_gathered(after(up_sent, attended))
-        down_piece = join_gathered(after(down_sent, attended))
+        up_piece, down_piece = unpack(
+            after(mlp_sent, attended),
+            seq,
+            up_flip.shape[1],
+            (up_flip.shape[0], down_flip.shape[0]),
+        )
         slice_rows = up_weight.shape[1]
         down_blocks = [
             lax.dynamic_slice_in_dim(down_piece, places[rank] * slice_rows, slice_rows, 1)
             for rank in range(8)
         ]
-        chip_grad = after(grad_sent, attended).T
-        grad_all = lax.all_gather(chip_grad, all_plane, axis=0, tiled=False)
-        text_sent = to_latent(after(text_rows, query))
+        text_padded = jnp.pad(text_rows, ((0, 0), (0, 0), (0, width - text_rows.shape[2])))
+        mixed = to_latent(after(jnp.concatenate([cotangent, text_padded], axis=1), query))
+        mixed = mixed.reshape(lat_count, -1, width)
+        attended_next = after(attended, up_piece)
         down_sent = exchange(down_blocks)
-        self_far = after_all(self_far, attended)
+        memory_near = after_all(memory_near, attended)
+        memory_half = halves(*memory_near)
+        memory_far = hop_two(*memory_half)
+        self_far = after_all(self_far, *memory_half)
         self_mine = (self_piece,) + self_near + self_far
         self_other = to_core(self_mine)
         memory_far = after_all(memory_far, *self_far)
@@ -906,7 +1024,8 @@
         memory_other = to_core(memory_mine)
         self_t, cq_t, cout_t = whole_of(self_mine, self_other, self_set)
         (memory_t,) = whole_of(memory_mine, memory_other, memory_set)
-        chip_text = after(text_sent, *memory_far).T
+        mixed = after(mixed, *memory_far)
+        chip_text = mixed[:, local_rows:, : text_rows.shape[2]].reshape(-1, text_rows.shape[2]).T
     stream_one = stream_zero + dot(self_t, attended_next)
     level_two = norm_gain(stream_one, gain_two).astype(bf16)
     cross_proj = dot(cq_t, level_two)
@@ -917,11 +1036,29 @@
     memory_value = memory_proj[width:].astype(bf16)
     text_keys = [memory_key, swap(memory_key, "c")]
     text_values = [memory_value, swap(memory_value, "c")]
-    crossed, cross_inverse = attend(cross, text_keys, text_values)
+    cross_next = cross
+    if square:
+        chip_grad = mixed[:, :local_rows].reshape(-1, width).T
+        grad_all = lax.all_gather(chip_grad, all_plane, axis=0, tiled=False)
+        cross_next = after(cross, chip_grad)
+    crossed, cross_inverse = attend(cross_next, text_keys, text_values)
     stream_two = stream_one + dot(cout_t, crossed)
     level_three = norm_gain(stream_two, gain_three).astype(bf16)
+    def with_other(values):
+        return values, swap(values, "c")
+
+    one_pair = with_other(level_one)
+    attended_pair = with_other(attended)
+    two_pair = with_other(level_two)
+    text_pair = with_other(chip_text)
+    crossed_pair = with_other(crossed)
     if square:
-        up_slice = up_piece
+        zero_pair = with_other(level_zero)
+        swapped = [
+            pair[1]
+            for pair in (one_pair, attended_pair, two_pair, text_pair, crossed_pair, zero_pair)
+        ]
+        up_slice = after(up_piece, *swapped)
         three_all = lax.all_gather(
             after(level_three, grad_all), all_plane, axis=0, tiled=False
         )
@@ -937,15 +1074,6 @@
         hidden = dot(up_t, level_three)
         activated = gelu_tanh(hidden).astype(bf16)
 
-    def with_other(values):
-        return values, swap(values, "c")
-
-    one_pair = with_other(level_one)
-    attended_pair = with_other(attended)
-    two_pair = with_other(level_two)
-    text_pair = with_other(chip_text)
-    crossed_pair = with_other(crossed)
-
     if square:
         grad_hidden, part = mlp_call(
             mlp_back_kernel,
@@ -955,7 +1083,6 @@
             [(slice_rows, bf16), (width, bf16)],
         )
         grad_level_three = lax.psum_scatter(part, all_plane, scatter_dimension=0, tiled=True)[0]
-        both_sent = to_latent(after(both_in, part))
         down_grad = mlp_call(
             mlp_outer_kernel,
             "mlp_outer",
@@ -980,7 +1107,6 @@
             [],
             (slice_rows, width),
         )
-        up_sum = sum_z_one(up_grad)
         (out_part,) = mlp_call(
             mlp_down_kernel,
             "mlp_down",
@@ -989,17 +1115,8 @@
             [(width, bf16)],
         )
         down_whole = stack_by_device([after(part, out_part) for part in down_parts])
-        down_cube = down_whole.reshape(seq, -1, slice_rows)
-        down_sum = [
-            z_shift(
-                lax.dynamic_index_in_dim(down_cube, (at_z + step) % seq, 0, keepdims=False), step
-            )
-            if step
-            else lax.dynamic_index_in_dim(down_cube, at_z, 0, keepdims=False)
-            for step in range(seq)
-        ]
-        level_zero = norm_gain(after(both_sent, out_part).T.astype(f32), gain_skip).astype(bf16)
-        grad_level_three = after(grad_level_three, level_zero, down_cube).astype(f32)
+        mlp_cut = pack(up_grad, down_whole, seq, lanes)
+        grad_level_three = after(grad_level_three, mlp_cut).astype(f32)
     else:
         grad_act = dot(down_t, chip_grad, TN)
         _, gelu_pull = jax.vjp(gelu_tanh, hidden)
@@ -1007,7 +1124,7 @@
         down_outer = outer_of((with_other(activated), [with_other(chip_grad)]))
         up_outer = outer_of((with_other(level_three), [with_other(grad_hidden)]))
         grad_level_three = dot(up_t, grad_hidden, TN)
-    zero_pair = with_other(level_zero)
+        zero_pair = with_other(level_zero)
     _, pull_three = jax.vjp(norm_gain, stream_two, gain_three)
     grad_from_three, grad_gain_three = pull_three(grad_level_three)
     grad_stream_two = chip_grad.astype(f32) + grad_from_three
@@ -1024,35 +1141,44 @@
     ).astype(bf16)
     _, pull_cq = jax.vjp(head_norm, cross_proj)
     grad_cq_flat = pull_cq(grad_cross)[0].astype(bf16)
-    early = up_sum + down_sum if square else []
+    if square:
+        def spread(values):
+            cube = values.reshape(seq, -1, values.shape[1])
+            cube = jnp.pad(cube, ((0, 0), (0, width // seq - cube.shape[1]), (0, 0)))
+            return cube.reshape(width, -1)
+
+        cross_outer = outer_of(
+            (crossed_pair, [with_other(cross_back)]),
+            (two_pair, [with_other(grad_cq_flat)]),
+            (tuple(spread(text) for text in text_pair), [with_other(grad_memory_proj)]),
+        )
+        cross_sum = sum_far(cross_outer)
+    else:
+        cross_outer = outer_of(
+            (crossed_pair, [with_other(cross_back)]), (two_pair, [with_other(grad_cq_flat)])
+        )
+        memory_outer = outer_of((text_pair, [with_other(grad_memory_proj)]))
     grad_level_two = dot(cq_t, grad_cq_flat, TN)
     _, pull_two = jax.vjp(norm_gain, stream_one, gain_two)
     grad_from_two, grad_gain_two = pull_two(grad_level_two)
     grad_stream_one = grad_stream_two + grad_from_two
     self_back = grad_stream_one.astype(bf16)
-    cross_outer = outer_of(
-        (crossed_pair, [with_other(cross_back)]),
-        (two_pair, [with_other(grad_cq_flat)]),
-        (attended_pair, [with_other(self_back)]),
-    )
-    memory_outer = outer_of((text_pair, [with_other(grad_memory_proj)]))
-    if square:
-        cross_sum = sum_far(cross_outer)
-        memory_sum = sum_far(memory_outer)
     grad_attended = dot(
-        self_t, after(self_back, cross_outer[0], memory_outer[0]), TN
+        self_t, after(self_back, cross_outer[0]), TN
     ).astype(bf16)
     grad_q, grad_k, grad_v = attend_back(
         query, grad_attended, attended, self_inverse, keys, values
     )
     if square:
         cross_sum = sum_near(cross_sum, grad_q)
-        memory_sum = sum_near(memory_sum, grad_q)
         out_sum = lax.psum_scatter(
             after(out_part, grad_level_three), all_plane, scatter_dimension=0, tiled=True
         )[0]
         blended = (stream_two + after(out_sum, grad_q).astype(f32)).astype(bf16)
-        grad_q = after(grad_q, blended, *early, *cross_sum[3], *memory_sum[3])
+        mlp_sum = lax.psum_scatter(
+            after(mlp_cut, grad_level_three), "z", scatter_dimension=0, tiled=True
+        )[0]
+        grad_q = after(grad_q, blended, *cross_sum[3])
     grad_key = grad_k[0] + swap(grad_k[1], "c").astype(f32)
     grad_value_proj = (grad_v[0] + swap(grad_v[1], "c").astype(f32)).astype(bf16)
     _, pull_query = jax.vjp(prepare, query_flat)
@@ -1061,89 +1187,107 @@
         bf16
     )
     first_outer = outer_of(
+        (attended_pair, [with_other(self_back)]),
         (one_pair, [with_other(grad_value_proj), with_other(grad_pair_proj)]),
     )
     if square:
         first_sum = sum_far(first_outer)
         cross_sum, stacked = sum_z_offloaded(cross_sum, first_outer[0])
-        memory_sum = sum_z(memory_sum, first_outer[0])
+        early = [stacked, mlp_sum]
     else:
-        stacked = first_outer[0]
+        early = []
         blended = (stream_two + dot(down_t, activated)).astype(bf16)
-    blended_out = from_latent(blended.T, first_outer[0])
     grad_text_rows = dot(grad_memory_proj, memory_t, TN).astype(bf16)
-    grad_text = from_latent(grad_text_rows, first_outer[0]).astype(f32)
-    grad_pair_next = after(grad_pair_proj, first_outer[0], stacked, blended_out, grad_text)
+    text_width = text_rows.shape[2]
+    back = jnp.concatenate(
+        [
+            blended.T.reshape(lat_count, -1, width),
+            jnp.pad(grad_text_rows, ((0, 0), (0, width - text_width))).reshape(
+                lat_count, -1, width
+            ),
+        ],
+        axis=1,
+    )
+    back = from_latent(back.reshape(-1, width), first_outer[0])
+    blended_out = back[:, :local_rows]
+    grad_text = back[:, local_rows:, :text_width].astype(f32)
+    grad_pair_next = after(grad_pair_proj, first_outer[0], back, *early)
     grad_level_one = dot(pair_t, grad_pair_next, TN) + dot(value_t, grad_value_proj, TN)
     _, pull_one = jax.vjp(shifted_norm, stream_zero, gain_one, shift)
     grad_from_one, grad_gain_one, grad_shift_part = pull_one(grad_level_one)
     skip_back = (grad_stream_one + grad_from_one).astype(bf16)
-    skip_outer = outer_of((zero_pair, [with_other(skip_back)]))
-    late = skip_outer[0]
     if square:
+        first_sum = sum_near(first_sum, skip_back)
+        skip_back_rows = from_latent(skip_back.T, *first_sum[3]).reshape(tokens, width)
+        skip_outer = outer_of((zero_pair, [with_other(skip_back_rows.T)]))
         skip_sum = sum_far(skip_outer)
-        first_sum = sum_near(first_sum, skip_outer[0])
-        late = first_sum[3][0]
-    skip_rows = from_latent(skip_back.T, late)
-    skip_back_rows = skip_rows.reshape(tokens, width)
+        skip_back_rows = after(skip_back_rows, skip_outer[0])
+    else:
+        skip_outer = outer_of((zero_pair, [with_other(skip_back)]))
+        skip_back_rows = from_latent(skip_back.T).reshape(tokens, width)
     grad_level_zero = dot(skip_back_rows, skip_t, NN)
     if square:
         skip_sum = sum_near(skip_sum, grad_level_zero)
-        first_sum = sum_z(first_sum, *skip_sum[3])
-        stacked = first_sum[0]
-        grad_level_zero = after(grad_level_zero, stacked)
-        (grad_up,) = sum_end(up_sum, up_set, stacked)
-        down_total = sum(after(part, stacked).astype(f32) for part in down_sum)
+        first_sum, stacked = sum_z_offloaded(first_sum, *skip_sum[3])
+        late = stacked
+        up_rows, up_part = up_weight.shape[1], up_weight.shape[0]
+        mlp_sum = after(mlp_sum, late).astype(f32)
+        grad_up = mlp_sum[:up_rows, :up_part].T
         grad_down = (
-            down_total.reshape(cores, -1, slice_rows)
-            .transpose(0, 2, 1)
+            mlp_sum[up_rows:]
+            .reshape(slice_rows // lanes, cores, -1, lanes)
+            .transpose(1, 0, 3, 2)
             .reshape(cores * slice_rows, -1)
         )
-        skip_sum = sum_z(skip_sum, grad_level_zero)
+        skip_sum = sum_z(skip_sum, stacked)
         late = skip_sum[0]
-        grad_cout, grad_cq, grad_self = sum_end(
-            cross_sum, [cross_output, cross_query, self_output], late
-        )
-        (grad_memory,) = sum_end(memory_sum, memory_set, late)
-        (grad_skip_w,) = sum_end(skip_sum, skip_set, grad_memory)
-        grad_value, grad_pair = sum_end(
-            first_sum, [value_weight, query_key_weight], grad_skip_w
-        )
+        grad_cout, grad_cq, grad_memory = sum_end(
+            cross_sum, [cross_output, cross_query, cross_memory], late
+        )
+        grad_memory = grad_memory[: cross_memory.shape[0]]
+        grad_self, grad_value, grad_pair = sum_end(
+            first_sum, [self_output, value_weight, query_key_weight], late
+        )
+        (grad_skip_w,) = sum_end(skip_sum, skip_set, grad_pair)
     else:
         (grad_down,) = sum_end(sum_plain(down_outer), down_set)
         (grad_up,) = sum_end(sum_plain(up_outer), up_set)
-        grad_cout, grad_cq, grad_self = sum_end(
-            sum_plain(cross_outer), [cross_output, cross_query, self_output]
-        )
+        grad_cout, grad_cq = sum_end(sum_plain(cross_outer), [cross_output, cross_query])
         (grad_memory,) = sum_end(sum_plain(memory_outer), memory_set)
-        grad_value, grad_pair = sum_end(sum_plain(first_outer), [value_weight, query_key_weight])
+        grad_self, grad_value, grad_pair = sum_end(
+            sum_plain(first_outer), [self_output, value_weight, query_key_weight]
+        )
         (grad_skip_w,) = sum_end(sum_plain(skip_outer), skip_set)
 
-    cond_act = jax.nn.silu(gather_rows(condition, ("c", "b", "a")).astype(f32)).astype(bf16)
+    joined_rows = jnp.concatenate([inputs, skipped], axis=-1).astype(f32).reshape(tokens, -1)
+    _, pull_zero = jax.vjp(norm_gain_rows, joined_rows, gain_skip)
+    grad_joined, grad_gain_skip = pull_zero(grad_level_zero)
+    grad_input = grad_joined[:, :width].reshape(inputs.shape)
+    grad_skipped = grad_joined[:, width:].reshape(inputs.shape)
+    small = jnp.concatenate(
+        [grad_shift_part, grad_gain_skip, grad_gain_one, grad_gain_two, grad_gain_three]
+    ).reshape(-1, width)
+    if square:
+        small = jnp.concatenate([after(small, stacked), condition.astype(f32)], axis=0)
+        held = jnp.zeros((8,) + small.shape, f32)
+        for rank in range(8):
+            arrived = to_rank(small, rank) if rank else small
+            held = lax.dynamic_update_slice(held, arrived[None], (places[rank], 0, 0))
+        shift_plane = held[:, 0].reshape(plane, cores, width).sum(axis=1)
+        gain_plane = sum(held[i, 1:-lat_count] for i in range(8))
+        cond_rows = held[:, -lat_count:].reshape(-1, width)
+        columns = z_order(z_send(jnp.concatenate([gain_plane, shift_plane], axis=0)))
+        gain_rows = len(gain_plane)
+        grad_gains = sum(column[:gain_rows] for column in columns).reshape(-1)
+        shift_grads = jnp.stack([column[gain_rows:] for column in columns], axis=1)
+        shift_grads = shift_grads.reshape(-1, width)
+    else:
+        cond_rows = gather_rows(condition, ("c", "b", "a")).astype(f32)
+        grad_gains = lax.psum(small[1:], ("a", "b", "c", "z")).reshape(-1)
+        shift_grads = lax.all_gather(lax.psum(small[:1], "c"), ("a", "b", "z"), axis=0, tiled=True)
+    cond_act = jax.nn.silu(cond_rows).astype(bf16)
     block_in, block_out = shift_weight.shape
     cond_block = lax.dynamic_slice_in_dim(cond_act, at_z * block_in, block_in, 1).astype(f32)
-    small = jnp.stack([grad_shift_part, grad_gain_one, grad_gain_two, grad_gain_three])
-    small = after(small, late)
-    if square:
-        small = small + swap(small, "c")
-        columns = z_order(z_send(small))
-        shift_grads = jnp.concatenate([column[:1] for column in columns], axis=0)
-        gain_part = sum(column[1:] for column in columns)
-        for axis in ("b", "a"):
-            carried = jnp.concatenate([gain_part, shift_grads], axis=0)
-            other = swap(carried, axis)
-            gain_part = gain_part + other[:3]
-            lower = here[axis] == 0
-            shift_grads = jnp.concatenate(
-                [
-                    jnp.where(lower, shift_grads, other[3:]),
-                    jnp.where(lower, other[3:], shift_grads),
-                ],
-                axis=0,
-            )
-    else:
-        gain_part = lax.psum(small[1:], ("a", "b", "c", "z"))
-        shift_grads = lax.all_gather(lax.psum(small[:1], "c"), ("a", "b", "z"), axis=0, tiled=True)
     own_columns = ((at_a * inner + at_b) * cores + at_c) * block_out
     grad_shift = jnp.dot(
         cond_block.T,
@@ -1151,12 +1295,6 @@
         precision=lax.Precision.HIGHEST,
     )
 
-    joined_rows = jnp.concatenate([inputs, skipped], axis=-1).astype(f32).reshape(tokens, -1)
-    _, pull_zero = jax.vjp(norm_gain_rows, joined_rows, gain_skip)
-    grad_joined, grad_gain_skip = pull_zero(grad_level_zero)
-    grad_input = grad_joined[:, :width].reshape(inputs.shape)
-    grad_skipped = grad_joined[:, width:].reshape(inputs.shape)
-    grad_gains = jnp.concatenate([total_of(grad_gain_skip), gain_part.reshape(-1)])
     return (
         blended_out,
         grad_input,

time: 1290 us -> 1130 us (0.88)
  starting transfers between devices: 287 us -> 176 us
  waiting for transfers between devices: 352 us -> 301 us
  local copies, waits for them, and re-layouts: 155 us -> 141 us
    ppermute x27 -> x9, starting transfers between devices: 83.3 us -> 18.6 us  [z_shift(): lax.ppermute(values, 'z', [(z, (z + step) % seq) for z in range(seq)])]
    ppermute x21, waiting for transfers between devices: 37.9 us -> 89.5 us  [to_rank(): return lax.ppermute(values, axes, [(i, last - i) for i in range(last + 1)])]
    all_gather x3 -> x2, waiting for transfers between devices: 46.8 us -> 0.01 us  [the longest x1 0.01 us: on_device(): cross_sent = lax.all_gather(cross_flip, 'z', axis=0, tiled=False)]
    ppermute x79 -> x70, waiting for transfers between devices: 111 us -> 70.6 us  [swap(): return lax.ppermute(values, axis, SWAP)]
    ppermute x8 -> x4, starting transfers between devices: 50.2 us -> 15.6 us  [to_latent(): parts.append(lax.ppermute(chosen, ('c', 'z'), route(step)))]
    all_gather x1, waiting for transfers between devices: 51.3 us -> 22.2 us  [on_device(): lax.all_gather(after(level_three, grad_all), all_plane, axis=0, tiled=False)]
    ppermute x27 -> x9, waiting for transfers between devices: 71.2 us -> 42.8 us  [z_shift(): lax.ppermute(values, 'z', [(z, (z + step) % seq) for z in range(seq)])]
    reduce_scatter x1, waiting for transfers between devices: 0.01 us -> 27.5 us  [on_device(): lax.psum_scatter(part, all_plane, scatter_dimension=0, tiled=True)[0]]
  transfers between devices with their start and end apart: 150 -> 118, of which waited for: 35 -> 37; matrix products, arithmetic and copies ran while one was open for 24% -> 28% of each run, Pallas kernels for 15% -> 19%
where the time goes in v3:
time: 1130 us; the launch traced here: 1110 us
  waiting for transfers between devices  301 us (27%)
  Pallas kernels  258 us (23%)
  starting transfers between devices  176 us (16%)
  local copies, waits for them, and re-layouts  141 us (12%)
  other arithmetic  140 us (12%)
  matrix products  80.4 us (7%)
  between operations  17.1 us (2%)
    ppermute x70, starting transfers between devices, swap(): return lax.ppermute(values, axis, SWAP)  113 us
    ppermute x21, waiting for transfers between devices, to_rank(): return lax.ppermute(values, axes, [(i, last - i) for i in range(last + 1)])  89.5 us
    pallas_call x5, Pallas kernels, mlp_call(): pl.pallas_call(kernel, grid=(count,), in_specs=[kept(x.shape) for x in he...  88.7 us
    dot_general x15, matrix products, dot(): return lax.dot_general(a, b, (dims, ((), ())), preferred_element_type=f32)  78.5 us
    unnamed x369, local copies, waits for them, and re-layouts  70.6 us
    ppermute x70, waiting for transfers between devices, swap(): return lax.ppermute(values, axis, SWAP)  70.6 us
    pallas_call x3, Pallas kernels, outer_blocks(): pl.pallas_call(functools.partial(outer_kernel, heights, sharing, half), g...  43 us
    ppermute x9, waiting for transfers between devices, z_shift(): lax.ppermute(values, 'z', [(z, (z + step) % seq) for z in range(seq)])  42.8 us
  transfers between devices with their start and end apart: 118, of which 37 were waited for; matrix products, arithmetic and copies ran while one was open for 28% of the time, Pallas kernels for 19%

profile of v3, /device:TPU:0, one launch (start us, length us, event | category | flops | bytes accessed | tf_op | source)
XLA Modules:
  0.0 1113.6 jit_solution(8062774037438154903)
XLA Ops:
  23.1 22.4 %collective-permute-done.1.refs_2_ = bf16[176,704]{1,0:T(8,128)(2,1)S(1)} collective-permute-done((bf16[176,704]{1,0:T(8,128)(2,1)}, bf16[176,704]{1,0:T(8,128)(2,1)S(1)}, u32[]{:S(2)}, u32[]{:S(2)}) %collective-permute-start.1) | collective-permute-done | bytes 247840 | tf_op jit(solution)/shard_map/ppermute | solution.py:741
  58.9 11.4 %collective-permute-done.4.refs_3_ = bf16[176,2816]{1,0:T(8,128)(2,1)} collective-permute-done((bf16[176,2816]{1,0:T(8,128)(2,1)S(1)}, bf16[176,2816]{1,0:T(8,128)(2,1)}, u32[]{:S(2)}, u32[]{:S(2)}) %collective-permute-start.4) | collective-permute-done | bytes 991264 | tf_op jit(solution)/shard_map/ppermute | solution.py:664
  112.8 25.7 %collective-permute-done.14.refs_2_ = bf16[704,1408]{1,0:T(8,128)(2,1)S(1)} collective-permute-done((bf16[704,1408]{1,0:T(8,128)(2,1)S(1)}, bf16[704,1408]{1,0:T(8,128)(2,1)S(1)}, u32[]{:S(2)}, u32[]{:S(2)}) %collective-permute-start.14) | collective-permute-done | bytes 1982496 | tf_op jit(solution)/shard_map/ppermute | solution.py:664
  159.8 13.3 %collective-permute-start.20 = (bf16[704,1408]{1,0:T(8,128)(2,1)S(1)}, bf16[704,1408]{1,0:T(8,128)(2,1)}, u32[]{:S(2)}, u32[]{:S(2)}) collective-permute-start(bf16[704,1408]{1,0:T(8,128)(2,1)S(1)} %join_gathered.1.refs_1_), channel_id=1, source_target_pairs={{0,4},{4,0},{1,5},{5,1},{2,6},{6,2},{3,7},{7,3},{8,12},{12,8},{9,1... | collective-permute-start | bytes 5947400 | tf_op jit(solution)/shard_map/ppermute | solution.py:664
  250.0 11.6 %pad_maximum_fusion.4 = bf16[16,88,512]{2,1,0:T(8,128)(2,1)S(1)} fusion(bf16[16,22,512]{2,1,0:T(8,128)(2,1)S(1)} %get-tuple-element.339, bf16[16,22,512]{2,1,0:T(8,128)(2,1)S(1)} %get-tuple-element.340, bf16[16,22,512]{2,1,0:T(8,128)(2,1)S(1)} %get-tuple-element.330, bf16[16,22,512]{2,1,0:T(8,128)(2,1)S(1)} %get-tuple-element.329), kind=kLoop, calls=%fused_computation.106 | loop fusion | flops 5767168 | bytes 2883584 | tf_op jit(solution)/shard_map/concatenate | solution.py:58
  267.7 11.9 %attend.2 = (bf16[1408,512]{1,0:T(8,128)(2,1)}, f32[8,2,512]{2,1,0:T(2,128)S(1)}) custom-call(bf16[1408,512]{1,0:T(8,128)(2,1)S(1)} %bitcast.242, bf16[1408,512]{1,0:T(8,128)(2,1)S(1)} %bitcast.240, bf16[1408,512]{1,0:T(8,128)(2,1)S(1)} %collective-permute-done.30.refs_2_.refs_5_, bf16[1408,512]{1,0:T(8,128)(2,1)} %convolution_convert_fusion.2.refs_3_.refs_6_, ...), custom_call_target="tpu_custom_call" | custom-call | flops 4294967296 | bytes 10092544 | tf_op jit(solution)/shard_map/attend/pallas_call | solution.py:114
  284.2 19.5 %collective-permute-done.38 = bf16[320,1408]{1,0:T(8,128)(2,1)S(1)} collective-permute-done((bf16[320,1408]{1,0:T(8,128)(2,1)S(1)}, bf16[320,1408]{1,0:T(8,128)(2,1)S(1)}, u32[]{:S(2)}, u32[]{:S(2)}) %collective-permute-start.38) | collective-permute-done | bytes 901152 | tf_op jit(solution)/shard_map/ppermute | solution.py:715
  309.3 13.3 %collective-permute-start.41 = (bf16[352,1024]{1,0:T(8,128)(2,1)}, bf16[352,1024]{1,0:T(8,128)(2,1)S(1)}, u32[]{:S(2)}, u32[]{:S(2)}) collective-permute-start(bf16[352,1024]{1,0:T(8,128)(2,1)} %get-tuple-element.149.refs_1_), channel_id=1, source_target_pairs={{0,4},{4,0},{1,5},{5,1},{2,6},{6,2},{3,7},{7,3},{8,12},{12,8},{9,1... | collective-permute-start | bytes 2162696 | tf_op jit(solution)/shard_map/ppermute | solution.py:664
  343.2 10.1 assemble.8
  385.0 8.9 attend.3
  422.5 14.2 %collective-permute-done.50.refs_4_ = bf16[176,768]{1,0:T(8,128)(2,1)S(1)} collective-permute-done((bf16[176,768]{1,0:T(8,128)(2,1)S(1)}, bf16[176,768]{1,0:T(8,128)(2,1)S(1)}, u32[]{:S(2)}, u32[]{:S(2)}) %collective-permute-start.50) | collective-permute-done | bytes 270368 | tf_op jit(solution)/shard_map/ppermute | solution.py:779
  438.2 9.6 collective-permute-done.49.refs_3_
  449.3 9.0 collective-permute-done.48.refs_2_
  466.2 22.2 %all-gather.19.cloned.1.call-done = bf16[11264,512]{1,0:T(8,128)(2,1)} async-done(((bf16[1408,512]{1,0:T(8,128)(2,1)}), bf16[11264,512]{1,0:T(8,128)(2,1)}) %all-gather.19.cloned.1.call-update) | async-done | bytes 11534352 | tf_op jit(solution)/shard_map/all_gather | solution.py:1062
  490.1 18.0 %mlp_up.1 = (f32[8,768,512]{2,1,0:T(8,128)}, bf16[8,768,512]{2,1,0:T(8,128)(2,1)}) custom-call(bf16[768,1408]{1,0:T(8,128)(2,1)S(1)} %copy-done.12, bf16[8,1408,512]{2,1,0:T(8,128)(2,1)} %bitcast.332), custom_call_target="tpu_custom_call" | custom-call | flops 8858370048 | bytes 30408704 | tf_op jit(solution)/shard_map/mlp_up/pallas_call | solution.py:524
  508.0 28.4 %mlp_back.1 = (bf16[8,768,512]{2,1,0:T(8,128)(2,1)}, bf16[8,1408,512]{2,1,0:T(8,128)(2,1)}) custom-call(bf16[768,1408]{1,0:T(8,128)(2,1)S(1)} %bitcast.237, bf16[1408,768]{1,0:T(8,128)(2,1)S(1)} %bitcast.238, bf16[8,1408,512]{2,1,0:T(8,128)(2,1)} %bitcast.330, f32[8,768,512]{2,1,0:T(8,128)} %get-tuple-element.182.hidden_ref), custom_call_target="tpu_custom_call" | custom-call | flops 17716740096 | bytes 44564480 | tf_op jit(solution)/shard_map/mlp_back/pallas_call | solution.py:524
  536.6 13.7 %mlp_outer.2 = bf16[1408,768]{1,0:T(8,128)(2,1)S(1)} custom-call(bf16[8,1408,512]{2,1,0:T(8,128)(2,1)} %bitcast.331, bf16[8,768,512]{2,1,0:T(8,128)(2,1)} %get-tuple-element.187.b_ref.act_ref), custom_call_target="tpu_custom_call" | custom-call | flops 8858370048 | bytes 17825792 | tf_op jit(solution)/shard_map/mlp_outer/pallas_call | solution.py:524
  554.5 14.7 %mlp_outer.3.up_ref = bf16[768,1408]{1,0:T(8,128)(2,1)S(1)} custom-call(bf16[8,768,512]{2,1,0:T(8,128)(2,1)} %get-tuple-element.186.a_ref, bf16[8,1408,512]{2,1,0:T(8,128)(2,1)} %bitcast.333), custom_call_target="tpu_custom_call" | custom-call | flops 8858370048 | bytes 17825792 | tf_op jit(solution)/shard_map/mlp_outer/pallas_call | solution.py:524
  574.5 13.8 %mlp_down.1 = bf16[8,1408,512]{2,1,0:T(8,128)(2,1)} custom-call(bf16[1408,768]{1,0:T(8,128)(2,1)S(1)} %assemble.10.down_ref, bf16[8,768,512]{2,1,0:T(8,128)(2,1)} %get-tuple-element.187.b_ref.act_ref), custom_call_target="tpu_custom_call" | custom-call | flops 8858370048 | bytes 23592960 | tf_op jit(solution)/shard_map/mlp_down/pallas_call | solution.py:524
  597.2 11.6 %collective-permute-done.61.refs_2_ = bf16[176,768]{1,0:T(8,128)(2,1)} collective-permute-done((bf16[176,768]{1,0:T(8,128)(2,1)}, bf16[176,768]{1,0:T(8,128)(2,1)}, u32[]{:S(2)}, u32[]{:S(2)}) %collective-permute-start.61) | collective-permute-done | bytes 270368 | tf_op jit(solution)/shard_map/ppermute | solution.py:779
  617.0 27.5 %reduce-scatter.6.cloned.1.call-done = bf16[1,1408,512]{2,1,0:T(8,128)(2,1)} async-done(((bf16[8,1408,512]{2,1,0:T(8,128)(2,1)}), bf16[1,1408,512]{2,1,0:T(8,128)(2,1)}) %reduce-scatter.6.cloned.1.call-update) | async-done | bytes 1441808 | tf_op jit(solution)/shard_map/reduce_scatter | solution.py:1085
  661.1 13.5 %attend_back.2 = (f32[1408,512]{1,0:T(8,128)}, f32[1408,128]{1,0:T(8,128)}, bf16[1408,128]{1,0:T(8,128)(2,1)}, f32[1408,128]{1,0:T(8,128)}, bf16[1408,128]{1,0:T(8,128)(2,1)}) custom-call(bf16[1408,512]{1,0:T(8,128)(2,1)} %copy-done.21, bf16[1408,512]{1,0:T(8,128)(2,1)} %convolution_convert_fusion.1.refs_1_, ...), custom_call_target="tpu_custom_call" | custom-call | flops 2684354560 | bytes 12976128 | tf_op jit(solution)/shard_map/attend_back/pallas_call | solution.py:176
  694.4 15.4 %outer_blocks.3 = (bf16[352,1408]{1,0:T(8,128)(2,1)}, bf16[352,1408]{1,0:T(8,128)(2,1)}, bf16[704,1408]{1,0:T(8,128)(2,1)}, bf16[704,1408]{1,0:T(8,128)(2,1)}, bf16[704,1408]{1,0:T(8,128)(2,1)}) custom-call(s32[4]{0:T(128)} %pad_add_fusion.3.place_ref, bf16[1408,512]{1,0:T(8,128)(2,1)} %fusion.31.refs_0_, bf16[1408,512]{1,0:T(8,128)(2,1)} %collective-permute-done.68.refs_1_, ...), custom_call_target="tpu_custom_call" | custom-call | flops 8120172544 | bytes 22347776 | tf_op jit(solution)/shard_map/outer_blocks/pallas_call | solution.py:321
  716.1 27.7 %attend_back.3 = (f32[1408,512]{1,0:T(8,128)}, f32[1408,512]{1,0:T(8,128)}, bf16[1408,512]{1,0:T(8,128)(2,1)}, f32[1408,512]{1,0:T(8,128)}, bf16[1408,512]{1,0:T(8,128)(2,1)}) custom-call(bf16[1408,512]{1,0:T(8,128)(2,1)} %bitcast.243, bf16[1408,512]{1,0:T(8,128)(2,1)} %convolution_convert_fusion.refs_1_, ...), custom_call_target="tpu_custom_call" | custom-call | flops 10737418240 | bytes 25952256 | tf_op jit(solution)/shard_map/attend_back/pallas_call | solution.py:176
  798.4 17.7 %outer_blocks.4 = (bf16[352,1408]{1,0:T(8,128)(2,1)}, bf16[352,1408]{1,0:T(8,128)(2,1)}, bf16[704,1408]{1,0:T(8,128)(2,1)}, bf16[704,1408]{1,0:T(8,128)(2,1)}, bf16[704,1408]{1,0:T(8,128)(2,1)}) custom-call(s32[4]{0:T(128)} %pad_add_fusion.3.place_ref, bf16[1408,512]{1,0:T(8,128)(2,1)} %fusion.57.refs_0_, bf16[1408,512]{1,0:T(8,128)(2,1)} %collective-permute-done.74.refs_1_, ...), custom_call_target="tpu_custom_call" | custom-call | flops 8120172544 | bytes 22347776 | tf_op jit(solution)/shard_map/outer_blocks/pallas_call | solution.py:321
  827.0 19.2 %collective-permute-done.81 = bf16[320,1408]{1,0:T(8,128)(2,1)S(1)} collective-permute-done((bf16[320,1408]{1,0:T(8,128)(2,1)S(1)}, bf16[320,1408]{1,0:T(8,128)(2,1)S(1)}, u32[]{:S(2)}, u32[]{:S(2)}) %collective-permute-start.81) | collective-permute-done | bytes 901152 | tf_op jit(solution)/shard_map/ppermute | solution.py:724
  863.8 9.9 fusion.26
  893.2 41.3 %collective-permute-start.88 = (bf16[1408,512]{1,0:T(8,128)(2,1)}, bf16[1408,512]{1,0:T(8,128)(2,1)}, u32[]{:S(2)}, u32[]{:S(2)}) collective-permute-start(bf16[1408,512]{1,0:T(8,128)(2,1)} %bitcast.79.refs_0_), channel_id=1, source_target_pairs={{0,4},{4,0},{1,5},{5,1},{2,6},{6,2},{3,7},{7,3},{8,12},{12,8},{9,1... | collective-permute-start | bytes 4325384 | tf_op jit(solution)/shard_map/ppermute | solution.py:664
  941.6 9.9 outer_blocks.5
  984.7 10.2 collective-permute-done.90
  1026.8 15.5 %collective-permute-done.94 = f32[8,1408]{1,0:T(8,128)S(1)} collective-permute-done((f32[8,1408]{1,0:T(8,128)S(1)}, f32[8,1408]{1,0:T(8,128)S(1)}, u32[]{:S(2)}, u32[]{:S(2)}) %collective-permute-start.94) | collective-permute-done | bytes 45088 | tf_op jit(solution)/shard_map/ppermute | solution.py:779
  1094.2 10.7 collective-permute-done.106
  (825 shorter events, 574.8 us)
Async XLA Ops:
  7.2 76.1 %all-gather.11.cloned.1.call-start = ((), (), s32[]{:S(2)}) async-start(), calls=%async_computation.10 | async-start | bytes 2703360 | tf_op jit(solution)/shard_map/all_gather | solution.py:908
  10.3 181.8 %all-gather.13.cloned.1.call-start = ((), (), s32[]{:S(2)}) async-start(), calls=%async_computation.11 | async-start | bytes 3379200 | tf_op jit(solution)/shard_map/all_gather | solution.py:909
  50.5 308.5 %all-gather.15.cloned.1.call-start = ((), (), s32[]{:S(2)}) async-start(), calls=%async_computation.12 | async-start | bytes 5652480 | tf_op jit(solution)/shard_map/all_gather | solution.py:942
  93.7 44.8 %collective-permute-start.14 = (bf16[704,1408]{1,0:T(8,128)(2,1)S(1)}, bf16[704,1408]{1,0:T(8,128)(2,1)S(1)}, u32[]{:S(2)}, u32[]{:S(2)}) collective-permute-start(bf16[704,1408]{1,0:T(8,128)(2,1)S(1)} %join_gathered.1.refs_1_), channel_id=1, source_target_pairs={{0,8},{8,0},{1,9},{9,1},{2,10},{10,2},{3,11},{11,3},{4,12},{12,4},... | collective-permute-start | bytes 5947400 | tf_op jit(solution)/shard_map/ppermute | solution.py:664
  99.6 75.8 %collective-permute-start.25 = (bf16[2,1408]{1,0:T(2,128)(2,1)S(1)}, bf16[2,1408]{1,0:T(2,128)(2,1)S(1)}, u32[]{:S(2)}, u32[]{:S(2)}) collective-permute-start(bf16[2,1408]{1,0:T(2,128)(2,1)S(1)} %copy-done.160), channel_id=1, source_target_pairs={{0,4},{4,0},{1,5},{5,1},{2,6},{6,2},{3,7},{7,3},{8,12},{12,8},{9,1... | collective-permute-start | bytes 16904 | tf_op jit(solution)/shard_map/ppermute | solution.py:664
  141.4 46.4 %collective-permute-start.16 = (bf16[352,1408]{1,0:T(8,128)(2,1)}, bf16[352,1408]{1,0:T(8,128)(2,1)S(1)}, u32[]{:S(2)}, u32[]{:S(2)}) collective-permute-start(bf16[352,1408]{1,0:T(8,128)(2,1)} %slice.227), channel_id=1, source_target_pairs={{0,16},{16,0},{1,17},{17,1},{2,18},{18,2},{3,19},{19,3},{4,20},{20... | collective-permute-start | bytes 2973704 | tf_op jit(solution)/shard_map/ppermute | solution.py:664
  159.8 45.5 %collective-permute-start.20 = (bf16[704,1408]{1,0:T(8,128)(2,1)S(1)}, bf16[704,1408]{1,0:T(8,128)(2,1)}, u32[]{:S(2)}, u32[]{:S(2)}) collective-permute-start(bf16[704,1408]{1,0:T(8,128)(2,1)S(1)} %join_gathered.1.refs_1_), channel_id=1, source_target_pairs={{0,4},{4,0},{1,5},{5,1},{2,6},{6,2},{3,7},{7,3},{8,12},{12,8},{9,1... | collective-permute-start | bytes 5947400 | tf_op jit(solution)/shard_map/ppermute | solution.py:664
  201.6 199.3 %all-gather.17.cloned.1.call-start = ((), (), s32[]{:S(2)}) async-start(), calls=%async_computation.13 | async-start | bytes 12976128 | tf_op jit(solution)/shard_map/all_gather | solution.py:1042
  205.3 57.3 %collective-permute-start.18 = (bf16[528,1408]{1,0:T(8,128)(2,1)}, bf16[528,1408]{1,0:T(8,128)(2,1)}, u32[]{:S(2)}, u32[]{:S(2)}) collective-permute-start(bf16[528,1408]{1,0:T(8,128)(2,1)} %get-tuple-element.141.refs_1_), channel_id=1, source_target_pairs={{0,8},{8,0},{1,9},{9,1},{2,10},{10,2},{3,11},{11,3},{4,12},{12,4},... | collective-permute-start | bytes 4460552 | tf_op jit(solution)/shard_map/ppermute | solution.py:664
  205.9 58.3 %collective-permute-start.19 = (bf16[528,1408]{1,0:T(8,128)(2,1)}, bf16[528,1408]{1,0:T(8,128)(2,1)S(1)}, u32[]{:S(2)}, u32[]{:S(2)}) collective-permute-start(bf16[528,1408]{1,0:T(8,128)(2,1)} %get-tuple-element.141.refs_1_), channel_id=1, source_target_pairs={{0,16},{16,0},{1,17},{17,1},{2,18},{18,2},{3,19},{19,3},{4,20},{20... | collective-permute-start | bytes 4460552 | tf_op jit(solution)/shard_map/ppermute | solution.py:664
  206.4 55.4 %collective-permute-start.28 = (bf16[352,1024]{1,0:T(8,128)(2,1)}, bf16[352,1024]{1,0:T(8,128)(2,1)}, u32[]{:S(2)}, u32[]{:S(2)}) collective-permute-start(bf16[352,1024]{1,0:T(8,128)(2,1)} %get-tuple-element.149.refs_1_), channel_id=1, source_target_pairs={{0,8},{8,0},{1,9},{9,1},{2,10},{10,2},{3,11},{11,3},{4,12},{12,4},... | collective-permute-start | bytes 2162696 | tf_op jit(solution)/shard_map/ppermute | solution.py:664
  309.2 179.2 %all-gather.19.cloned.1.call-start = ((), (), s32[]{:S(2)}) async-start(), calls=%async_computation.14 | async-start | bytes 12976128 | tf_op jit(solution)/shard_map/all_gather | solution.py:1062
  400.9 243.6 %reduce-scatter.6.cloned.1.call-start = ((), (), s32[]{:S(2)}) async-start(), calls=%async_computation.5 | async-start | bytes 12976128 | tf_op jit(solution)/shard_map/reduce_scatter | solution.py:1085
  405.0 56.8 %collective-permute-start.55 = (bf16[1408,512]{1,0:T(8,128)(2,1)}, bf16[1408,512]{1,0:T(8,128)(2,1)}, u32[]{:S(2)}, u32[]{:S(2)}) collective-permute-start(bf16[1408,512]{1,0:T(8,128)(2,1)} %fusion.23.refs_8_), channel_id=1, source_target_pairs={{0,4},{4,0},{1,5},{5,1},{2,6},{6,2},{3,7},{7,3},{8,12},{12,8},{9,1... | collective-permute-start | bytes 4325384 | tf_op jit(solution)/shard_map/ppermute | solution.py:664
  407.0 54.8 %collective-permute-start.56 = (bf16[1408,512]{1,0:T(8,128)(2,1)}, bf16[1408,512]{1,0:T(8,128)(2,1)}, u32[]{:S(2)}, u32[]{:S(2)}) collective-permute-start(bf16[1408,512]{1,0:T(8,128)(2,1)} %get-tuple-element.161.refs_2_.refs_6_), channel_id=1, source_target_pairs={{0,4},{4,0},{1,5},{5,1},{2,6},{6,2},{3,7},{7,3},{8,12},{12,8},{9,1... | collective-permute-start | bytes 4325384 | tf_op jit(solution)/shard_map/ppermute | solution.py:664
  411.6 50.3 %collective-permute-start.59 = (bf16[1408,512]{1,0:T(8,128)(2,1)}, bf16[1408,512]{1,0:T(8,128)(2,1)}, u32[]{:S(2)}, u32[]{:S(2)}) collective-permute-start(bf16[1408,512]{1,0:T(8,128)(2,1)} %get-tuple-element.169.refs_2_.refs_6_), channel_id=1, source_target_pairs={{0,4},{4,0},{1,5},{5,1},{2,6},{6,2},{3,7},{7,3},{8,12},{12,8},{9,1... | collective-permute-start | bytes 4325384 | tf_op jit(solution)/shard_map/ppermute | solution.py:664
  536.5 224.4 %reduce-scatter.8.cloned.1.call-start = ((), (), s32[]{:S(2)}) async-start(), calls=%async_computation.6 | async-start | bytes 12976128 | tf_op jit(solution)/shard_map/reduce_scatter | solution.py:1174
  644.6 219.2 %reduce-scatter.10.cloned.1.call-start = ((), (), s32[]{:S(2)}) async-start(), calls=%async_computation.7 | async-start | bytes 5652480 | tf_op jit(solution)/shard_map/reduce_scatter | solution.py:1178
  743.9 337.0 %reduce-scatter.14.cloned.1.call-start = ((), (), s32[]{:S(2)}) async-start(), calls=%async_computation.9 | async-start | bytes 2703360 | tf_op jit(solution)/shard_map/reduce_scatter | solution.py:861
  779.6 46.2 %collective-permute-start.82 = (bf16[704,1408]{1,0:T(8,128)(2,1)}, bf16[704,1408]{1,0:T(8,128)(2,1)S(1)}, u32[]{:S(2)}, u32[]{:S(2)}) collective-permute-start(bf16[704,1408]{1,0:T(8,128)(2,1)} %add_dynamic-update-slice_fusion.3), channel_id=1, source_target_pairs={{0,16},{16,0},{1,17},{17,1},{2,18},{18,2},{3,19},{19,3},{4,20},{20... | collective-permute-start | bytes 5947400 | tf_op jit(solution)/shard_map/ppermute | solution.py:664
  780.9 65.3 %collective-permute-start.83 = (bf16[704,1408]{1,0:T(8,128)(2,1)}, bf16[704,1408]{1,0:T(8,128)(2,1)}, u32[]{:S(2)}, u32[]{:S(2)}) collective-permute-start(bf16[704,1408]{1,0:T(8,128)(2,1)} %copy-done.124), channel_id=1, source_target_pairs={{0,8},{8,0},{1,9},{9,1},{2,10},{10,2},{3,11},{11,3},{4,12},{12,4},... | collective-permute-start | bytes 5947400 | tf_op jit(solution)/shard_map/ppermute | solution.py:664
  788.6 57.6 %collective-permute-start.81 = (bf16[320,1408]{1,0:T(8,128)(2,1)S(1)}, bf16[320,1408]{1,0:T(8,128)(2,1)S(1)}, u32[]{:S(2)}, u32[]{:S(2)}) collective-permute-start(bf16[320,1408]{1,0:T(8,128)(2,1)S(1)} %get-tuple-element.357), channel_id=1, source_target_pairs={{1,0},{0,1},{5,2},{4,3},{3,4},{2,5},{7,6},{6,7},{9,8},{8,9},{13,10... | collective-permute-start | bytes 2703368 | tf_op jit(solution)/shard_map/ppermute | solution.py:724
  790.1 56.1 %collective-permute-start.73 = (bf16[320,1408]{1,0:T(8,128)(2,1)S(1)}, bf16[320,1408]{1,0:T(8,128)(2,1)}, u32[]{:S(2)}, u32[]{:S(2)}) collective-permute-start(bf16[320,1408]{1,0:T(8,128)(2,1)S(1)} %get-tuple-element.358), channel_id=1, source_target_pairs={{0,0},{1,1},{4,2},{5,3},{2,4},{3,5},{6,6},{7,7},{8,8},{9,9},{12,10... | collective-permute-start | bytes 2703368 | tf_op jit(solution)/shard_map/ppermute | solution.py:724
  816.1 69.1 %collective-permute-start.86 = (bf16[352,1408]{1,0:T(8,128)(2,1)}, bf16[352,1408]{1,0:T(8,128)(2,1)S(1)}, u32[]{:S(2)}, u32[]{:S(2)}) collective-permute-start(bf16[352,1408]{1,0:T(8,128)(2,1)} %get-tuple-element.228), channel_id=1, source_target_pairs={{0,16},{16,0},{1,17},{17,1},{2,18},{18,2},{3,19},{19,3},{4,20},{20... | collective-permute-start | bytes 2973704 | tf_op jit(solution)/shard_map/ppermute | solution.py:664
  825.8 56.7 %collective-permute-start.85 = (bf16[352,1408]{1,0:T(8,128)(2,1)}, bf16[352,1408]{1,0:T(8,128)(2,1)}, u32[]{:S(2)}, u32[]{:S(2)}) collective-permute-start(bf16[352,1408]{1,0:T(8,128)(2,1)} %get-tuple-element.218), channel_id=1, source_target_pairs={{0,8},{8,0},{1,9},{9,1},{2,10},{10,2},{3,11},{11,3},{4,12},{12,4},... | collective-permute-start | bytes 2973704 | tf_op jit(solution)/shard_map/ppermute | solution.py:664
  893.2 48.3 %collective-permute-start.88 = (bf16[1408,512]{1,0:T(8,128)(2,1)}, bf16[1408,512]{1,0:T(8,128)(2,1)}, u32[]{:S(2)}, u32[]{:S(2)}) collective-permute-start(bf16[1408,512]{1,0:T(8,128)(2,1)} %bitcast.79.refs_0_), channel_id=1, source_target_pairs={{0,4},{4,0},{1,5},{5,1},{2,6},{6,2},{3,7},{7,3},{8,12},{12,8},{9,1... | collective-permute-start | bytes 4325384 | tf_op jit(solution)/shard_map/ppermute | solution.py:664
  935.1 156.1 %reduce-scatter.12.cloned.1.call-start = ((), (), s32[]{:S(2)}) async-start(), calls=%async_computation.8 | async-start | bytes 2703360 | tf_op jit(solution)/shard_map/reduce_scatter | solution.py:861
  938.6 60.5 %collective-permute-start.89 = (bf16[704,1408]{1,0:T(8,128)(2,1)}, bf16[704,1408]{1,0:T(8,128)(2,1)}, u32[]{:S(2)}, u32[]{:S(2)}) collective-permute-start(bf16[704,1408]{1,0:T(8,128)(2,1)} %add_dynamic-update-slice_fusion.1), channel_id=1, source_target_pairs={{0,16},{16,0},{1,17},{17,1},{2,18},{18,2},{3,19},{19,3},{4,20},{20... | collective-permute-start | bytes 5947400 | tf_op jit(solution)/shard_map/ppermute | solution.py:664
  940.1 59.0 %collective-permute-start.92 = (bf16[704,1408]{1,0:T(8,128)(2,1)}, bf16[704,1408]{1,0:T(8,128)(2,1)}, u32[]{:S(2)}, u32[]{:S(2)}) collective-permute-start(bf16[704,1408]{1,0:T(8,128)(2,1)} %add_dynamic-update-slice_fusion), channel_id=1, source_target_pairs={{0,8},{8,0},{1,9},{9,1},{2,10},{10,2},{3,11},{11,3},{4,12},{12,4},... | collective-permute-start | bytes 5947400 | tf_op jit(solution)/shard_map/ppermute | solution.py:664
  951.5 45.5 %collective-permute-start.91 = (bf16[96,2816]{1,0:T(8,128)(2,1)}, bf16[96,2816]{1,0:T(8,128)(2,1)}, u32[]{:S(2)}, u32[]{:S(2)}) collective-permute-start(bf16[96,2816]{1,0:T(8,128)(2,1)} %get-tuple-element.237), channel_id=1, source_target_pairs={{0,16},{16,0},{1,17},{17,1},{2,18},{18,2},{3,19},{19,3},{4,20},{20... | collective-permute-start | bytes 1622024 | tf_op jit(solution)/shard_map/ppermute | solution.py:664
  1018.8 59.5 %collective-permute-start.103 = (bf16[176,2816]{1,0:T(8,128)(2,1)}, bf16[176,2816]{1,0:T(8,128)(2,1)S(1)}, u32[]{:S(2)}, u32[]{:S(2)}) collective-permute-start(bf16[176,2816]{1,0:T(8,128)(2,1)} %add_dynamic-update-slice_fusion.5), channel_id=1, source_target_pairs={{0,16},{16,0},{1,17},{17,1},{2,18},{18,2},{3,19},{19,3},{4,20},{20... | collective-permute-start | bytes 2973704 | tf_op jit(solution)/shard_map/ppermute | solution.py:664
  1023.2 55.0 %collective-permute-start.104 = (bf16[176,2816]{1,0:T(8,128)(2,1)}, bf16[176,2816]{1,0:T(8,128)(2,1)S(1)}, u32[]{:S(2)}, u32[]{:S(2)}) collective-permute-start(bf16[176,2816]{1,0:T(8,128)(2,1)} %add_dynamic-update-slice_fusion.4), channel_id=1, source_target_pairs={{0,8},{8,0},{1,9},{9,1},{2,10},{10,2},{3,11},{11,3},{4,12},{12,4},... | collective-permute-start | bytes 2973704 | tf_op jit(solution)/shard_map/ppermute | solution.py:664
  (262 other events, 3290.2 us)
Sparse Core Ops, SparseCore 0:
  10.4 64.2 all-gather.10
  76.3 55.6 all-gather.12
  201.7 102.0 all-gather.14
  309.4 88.0 all-gather.16
  401.0 87.3 all-gather.18
  536.6 107.8 reduce-scatter.5
  648.0 103.0 reduce-scatter.7
  753.4 110.2 reduce-scatter.9
  935.2 45.1 reduce-scatter.13
  1026.8 50.3 reduce-scatter.11

commit v4 on v3

--- a/solution.py
+++ b/solution.py
@@ -433,24 +433,35 @@
     )(gathered)
 
 
-def stack_kernel(*refs):
+def stack_kernel(counts, *refs):
     term_refs, out_ref = refs[:-1], refs[-1]
     seq, _, part = out_ref.shape
-
-    def chunk(i, _):
-        at = pl.ds(pl.multiple_of(i * 16, 16), 16)
-        total = sum(ref[at, :].astype(f32) for ref in term_refs).astype(bf16)
-        for j in range(seq):
-            out_ref[j, at, :] = total[:, j * part : (j + 1) * part]
-        return 0
-
-    lax.fori_loop(0, out_ref.shape[1] // 16, chunk, 0)
-
-
-def stack_sum(seq, *terms):
-    rows, width = terms[0].shape
+    top = 0
+    first = 0
+    for count in counts:
+        group = term_refs[first : first + count]
+        rows = group[0].shape[0]
+
+        def chunk(i, _, group=group, top=top):
+            at = pl.ds(pl.multiple_of(i * 16, 16), 16)
+            total = group[0][at, :]
+            if len(group) > 1:
+                total = sum(ref[at, :].astype(f32) for ref in group).astype(bf16)
+            to = pl.ds(pl.multiple_of(top + i * 16, 16), 16)
+            for j in range(seq):
+                out_ref[j, to, :] = total[:, j * part : (j + 1) * part]
+            return 0
+
+        lax.fori_loop(0, rows // 16, chunk, 0)
+        top += rows
+        first += count
+
+
+def stack_sum(seq, *groups):
+    terms = [term for group in groups for term in group]
+    rows, width = sum(group[0].shape[0] for group in groups), terms[0].shape[1]
     return pl.pallas_call(
-        stack_kernel,
+        functools.partial(stack_kernel, [len(group) for group in groups]),
         in_specs=[pl.BlockSpec(memory_space=pltpu.VMEM)] * len(terms),
         out_specs=pl.BlockSpec(memory_space=pltpu.VMEM),
         out_shape=jax.ShapeDtypeStruct((seq, rows, width // seq), bf16),
@@ -855,10 +866,9 @@
         parts = cut_sum(at_z, seq, own, after(got_a, *others), got_b)
         return [parts[0]] + [z_shift(parts[step], step) for step in range(1, seq)]
 
-    def sum_z_offloaded(state, *others):
+    def sum_three(state, *others):
         own, got_a, got_b, _ = state
-        stacked = stack_sum(seq, own, after(got_a, *others), got_b)
-        return [lax.psum_scatter(stacked, "z", scatter_dimension=0, tiled=True)[0]], stacked
+        return (own.astype(f32) + after(got_a, *others).astype(f32) + got_b.astype(f32)).astype(bf16)
 
     def sum_plain(state):
         (total,) = state
@@ -1192,8 +1202,8 @@
     )
     if square:
         first_sum = sum_far(first_outer)
-        cross_sum, stacked = sum_z_offloaded(cross_sum, first_outer[0])
-        early = [stacked, mlp_sum]
+        cross_total = sum_three(cross_sum, first_outer[0])
+        early = [cross_total, mlp_sum]
     else:
         early = []
         blended = (stream_two + dot(down_t, activated)).astype(bf16)
@@ -1211,15 +1221,22 @@
     back = from_latent(back.reshape(-1, width), first_outer[0])
     blended_out = back[:, :local_rows]
     grad_text = back[:, local_rows:, :text_width].astype(f32)
-    grad_pair_next = after(grad_pair_proj, first_outer[0], back, *early)
+    grad_pair_next = after(grad_pair_proj, first_outer[0])
     grad_level_one = dot(pair_t, grad_pair_next, TN) + dot(value_t, grad_value_proj, TN)
     _, pull_one = jax.vjp(shifted_norm, stream_zero, gain_one, shift)
     grad_from_one, grad_gain_one, grad_shift_part = pull_one(grad_level_one)
     skip_back = (grad_stream_one + grad_from_one).astype(bf16)
     if square:
         first_sum = sum_near(first_sum, skip_back)
-        skip_back_rows = from_latent(skip_back.T, *first_sum[3]).reshape(tokens, width)
-        skip_outer = outer_of((zero_pair, [with_other(skip_back_rows.T)]))
+        skip_sent = after(skip_back, back, *early).T
+        skip_back_rows = from_latent(skip_sent, *first_sum[3]).reshape(tokens, width)
+        own_back, other_back = with_other(skip_back_rows.T)
+        own_sum, got_a, got_b, _ = first_sum
+        stacked = stack_sum(
+            seq, (cross_total,), (own_sum, after(got_a, skip_back_rows), got_b)
+        )
+        both_sum = [lax.psum_scatter(stacked, "z", scatter_dimension=0, tiled=True)[0]]
+        skip_outer = outer_of((zero_pair, [(after(own_back, stacked), other_back)]))
         skip_sum = sum_far(skip_outer)
         skip_back_rows = after(skip_back_rows, skip_outer[0])
     else:
@@ -1228,8 +1245,7 @@
     grad_level_zero = dot(skip_back_rows, skip_t, NN)
     if square:
         skip_sum = sum_near(skip_sum, grad_level_zero)
-        first_sum, stacked = sum_z_offloaded(first_sum, *skip_sum[3])
-        late = stacked
+        late = skip_sum[3][0]
         up_rows, up_part = up_weight.shape[1], up_weight.shape[0]
         mlp_sum = after(mlp_sum, late).astype(f32)
         grad_up = mlp_sum[:up_rows, :up_part].T
@@ -1239,15 +1255,21 @@
             .transpose(1, 0, 3, 2)
             .reshape(cores * slice_rows, -1)
         )
-        skip_sum = sum_z(skip_sum, stacked)
+        skip_sum = sum_z(skip_sum, late)
         late = skip_sum[0]
-        grad_cout, grad_cq, grad_memory = sum_end(
-            cross_sum, [cross_output, cross_query, cross_memory], late
+        grad_cout, grad_cq, grad_memory, grad_self, grad_value, grad_pair = sum_end(
+            both_sum,
+            [
+                cross_output,
+                cross_query,
+                cross_memory,
+                self_output,
+                value_weight,
+                query_key_weight,
+            ],
+            late,
         )
         grad_memory = grad_memory[: cross_memory.shape[0]]
-        grad_self, grad_value, grad_pair = sum_end(
-            first_sum, [self_output, value_weight, query_key_weight], late
-        )
         (grad_skip_w,) = sum_end(skip_sum, skip_set, grad_pair)
     else:
         (grad_down,) = sum_end(sum_plain(down_outer), down_set)
@@ -1268,7 +1290,7 @@
         [grad_shift_part, grad_gain_skip, grad_gain_one, grad_gain_two, grad_gain_three]
     ).reshape(-1, width)
     if square:
-        small = jnp.concatenate([after(small, stacked), condition.astype(f32)], axis=0)
+        small = jnp.concatenate([after(small, late), condition.astype(f32)], axis=0)
         held = jnp.zeros((8,) + small.shape, f32)
         for rank in range(8):
             arrived = to_rank(small, rank) if rank else small

time: 1130 us -> 1090 us (0.965)
  waiting for transfers between devices: 301 us -> 269 us
    ppermute x21, waiting for transfers between devices: 89.5 us -> 68.7 us  [to_rank(): return lax.ppermute(values, axes, [(i, last - i) for i in range(last + 1)])]
    unnamed x369 -> x373, local copies, waits for them, and re-layouts: 70.6 us -> 68.9 us
  transfers between devices with their start and end apart: 118 -> 117, of which waited for: 37 -> 35; matrix products, arithmetic and copies ran while one was open for 28% -> 29% of each run, Pallas kernels for 19% -> 18%
where the time goes in v4:
time: 1090 us; the launch traced here: 1070 us
  waiting for transfers between devices  269 us (25%)
  Pallas kernels  252 us (23%)
  starting transfers between devices  170 us (16%)
  other arithmetic  148 us (14%)
  local copies, waits for them, and re-layouts  137 us (13%)
  matrix products  76.1 us (7%)
  between operations  16.8 us (2%)
    ppermute x70, starting transfers between devices, swap(): return lax.ppermute(values, axis, SWAP)  103 us
    pallas_call x5, Pallas kernels, mlp_call(): pl.pallas_call(kernel, grid=(count,), in_specs=[kept(x.shape) for x in he...  88.7 us
    dot_general x15, matrix products, dot(): return lax.dot_general(a, b, (dims, ((), ())), preferred_element_type=f32)  75 us
    ppermute x70, waiting for transfers between devices, swap(): return lax.ppermute(values, axis, SWAP)  72.9 us
    unnamed x373, local copies, waits for them, and re-layouts  68.9 us
    ppermute x21, waiting for transfers between devices, to_rank(): return lax.ppermute(values, axes, [(i, last - i) for i in range(last + 1)])  68.7 us
    pallas_call x3, Pallas kernels, outer_blocks(): pl.pallas_call(functools.partial(outer_kernel, heights, sharing, half), g...  42.5 us
    pallas_call x2, Pallas kernels, attend_back(): pl.pallas_call(functools.partial(attend_back_kernel, blocks), grid=(H //...  41.2 us
  transfers between devices with their start and end apart: 117, of which 35 were waited for; matrix products, arithmetic and copies ran while one was open for 29% of the time, Pallas kernels for 18%

profile of v4, /device:TPU:0, one launch (start us, length us, event | category | flops | bytes accessed | tf_op | source)
XLA Modules:
  0.0 1068.7 jit_solution(17034518906066544982)
XLA Ops:
  23.1 22.4 %collective-permute-done.1.refs_2_ = bf16[176,704]{1,0:T(8,128)(2,1)S(1)} collective-permute-done((bf16[176,704]{1,0:T(8,128)(2,1)}, bf16[176,704]{1,0:T(8,128)(2,1)S(1)}, u32[]{:S(2)}, u32[]{:S(2)}) %collective-permute-start.1) | collective-permute-done | bytes 247840 | tf_op jit(solution)/shard_map/ppermute | solution.py:752
  58.9 11.4 %collective-permute-done.4.refs_3_ = bf16[176,2816]{1,0:T(8,128)(2,1)} collective-permute-done((bf16[176,2816]{1,0:T(8,128)(2,1)S(1)}, bf16[176,2816]{1,0:T(8,128)(2,1)}, u32[]{:S(2)}, u32[]{:S(2)}) %collective-permute-start.4) | collective-permute-done | bytes 991264 | tf_op jit(solution)/shard_map/ppermute | solution.py:675
  108.9 29.6 %collective-permute-done.14.refs_2_ = bf16[704,1408]{1,0:T(8,128)(2,1)S(1)} collective-permute-done((bf16[704,1408]{1,0:T(8,128)(2,1)S(1)}, bf16[704,1408]{1,0:T(8,128)(2,1)S(1)}, u32[]{:S(2)}, u32[]{:S(2)}) %collective-permute-start.14) | collective-permute-done | bytes 1982496 | tf_op jit(solution)/shard_map/ppermute | solution.py:675
  159.8 13.3 %collective-permute-start.20 = (bf16[704,1408]{1,0:T(8,128)(2,1)S(1)}, bf16[704,1408]{1,0:T(8,128)(2,1)}, u32[]{:S(2)}, u32[]{:S(2)}) collective-permute-start(bf16[704,1408]{1,0:T(8,128)(2,1)S(1)} %join_gathered.1.refs_1_), channel_id=1, source_target_pairs={{0,4},{4,0},{1,5},{5,1},{2,6},{6,2},{3,7},{7,3},{8,12},{12,8},{9,1... | collective-permute-start | bytes 5947400 | tf_op jit(solution)/shard_map/ppermute | solution.py:675
  250.0 11.6 %pad_maximum_fusion.4 = bf16[16,88,512]{2,1,0:T(8,128)(2,1)S(1)} fusion(bf16[16,22,512]{2,1,0:T(8,128)(2,1)S(1)} %get-tuple-element.341, bf16[16,22,512]{2,1,0:T(8,128)(2,1)S(1)} %get-tuple-element.342, bf16[16,22,512]{2,1,0:T(8,128)(2,1)S(1)} %get-tuple-element.332, bf16[16,22,512]{2,1,0:T(8,128)(2,1)S(1)} %get-tuple-element.331), kind=kLoop, calls=%fused_computation.107 | loop fusion | flops 5767168 | bytes 2883584 | tf_op jit(solution)/shard_map/concatenate | solution.py:58
  267.7 11.9 %attend.2 = (bf16[1408,512]{1,0:T(8,128)(2,1)}, f32[8,2,512]{2,1,0:T(2,128)S(1)}) custom-call(bf16[1408,512]{1,0:T(8,128)(2,1)S(1)} %bitcast.239, bf16[1408,512]{1,0:T(8,128)(2,1)S(1)} %bitcast.237, bf16[1408,512]{1,0:T(8,128)(2,1)S(1)} %collective-permute-done.30.refs_2_.refs_5_, bf16[1408,512]{1,0:T(8,128)(2,1)} %convolution_convert_fusion.2.refs_3_.refs_6_, ...), custom_call_target="tpu_custom_call" | custom-call | flops 4294967296 | bytes 10092544 | tf_op jit(solution)/shard_map/attend/pallas_call | solution.py:114
  284.2 19.5 %collective-permute-done.38 = bf16[320,1408]{1,0:T(8,128)(2,1)S(1)} collective-permute-done((bf16[320,1408]{1,0:T(8,128)(2,1)S(1)}, bf16[320,1408]{1,0:T(8,128)(2,1)S(1)}, u32[]{:S(2)}, u32[]{:S(2)}) %collective-permute-start.38) | collective-permute-done | bytes 901152 | tf_op jit(solution)/shard_map/ppermute | solution.py:726
  309.2 13.3 %collective-permute-start.41 = (bf16[352,1024]{1,0:T(8,128)(2,1)}, bf16[352,1024]{1,0:T(8,128)(2,1)S(1)}, u32[]{:S(2)}, u32[]{:S(2)}) collective-permute-start(bf16[352,1024]{1,0:T(8,128)(2,1)} %get-tuple-element.150.refs_1_), channel_id=1, source_target_pairs={{0,4},{4,0},{1,5},{5,1},{2,6},{6,2},{3,7},{7,3},{8,12},{12,8},{9,1... | collective-permute-start | bytes 2162696 | tf_op jit(solution)/shard_map/ppermute | solution.py:675
  343.1 10.1 assemble.8
  384.9 8.9 attend.3
  422.4 14.2 %collective-permute-done.50.refs_4_ = bf16[176,768]{1,0:T(8,128)(2,1)S(1)} collective-permute-done((bf16[176,768]{1,0:T(8,128)(2,1)S(1)}, bf16[176,768]{1,0:T(8,128)(2,1)S(1)}, u32[]{:S(2)}, u32[]{:S(2)}) %collective-permute-start.50) | collective-permute-done | bytes 270368 | tf_op jit(solution)/shard_map/ppermute | solution.py:790
  438.0 9.7 collective-permute-done.49.refs_3_
  449.2 9.0 collective-permute-done.48.refs_2_
  466.2 22.2 %all-gather.19.cloned.1.call-done = bf16[11264,512]{1,0:T(8,128)(2,1)} async-done(((bf16[1408,512]{1,0:T(8,128)(2,1)}), bf16[11264,512]{1,0:T(8,128)(2,1)}) %all-gather.19.cloned.1.call-update) | async-done | bytes 11534352 | tf_op jit(solution)/shard_map/all_gather | solution.py:1072
  490.0 18.0 %mlp_up.1 = (f32[8,768,512]{2,1,0:T(8,128)}, bf16[8,768,512]{2,1,0:T(8,128)(2,1)}) custom-call(bf16[768,1408]{1,0:T(8,128)(2,1)S(1)} %copy-done.13, bf16[8,1408,512]{2,1,0:T(8,128)(2,1)} %bitcast.327), custom_call_target="tpu_custom_call" | custom-call | flops 8858370048 | bytes 30408704 | tf_op jit(solution)/shard_map/mlp_up/pallas_call | solution.py:535
  508.0 28.4 %mlp_back.1 = (bf16[8,768,512]{2,1,0:T(8,128)(2,1)}, bf16[8,1408,512]{2,1,0:T(8,128)(2,1)}) custom-call(bf16[768,1408]{1,0:T(8,128)(2,1)S(1)} %bitcast.234, bf16[1408,768]{1,0:T(8,128)(2,1)S(1)} %bitcast.235, bf16[8,1408,512]{2,1,0:T(8,128)(2,1)} %bitcast.325, f32[8,768,512]{2,1,0:T(8,128)} %get-tuple-element.183.hidden_ref), custom_call_target="tpu_custom_call" | custom-call | flops 17716740096 | bytes 44564480 | tf_op jit(solution)/shard_map/mlp_back/pallas_call | solution.py:535
  536.6 13.7 %mlp_outer.2 = bf16[1408,768]{1,0:T(8,128)(2,1)S(1)} custom-call(bf16[8,1408,512]{2,1,0:T(8,128)(2,1)} %bitcast.326, bf16[8,768,512]{2,1,0:T(8,128)(2,1)} %get-tuple-element.188.b_ref.act_ref), custom_call_target="tpu_custom_call" | custom-call | flops 8858370048 | bytes 17825792 | tf_op jit(solution)/shard_map/mlp_outer/pallas_call | solution.py:535
  554.4 14.7 %mlp_outer.3.up_ref = bf16[768,1408]{1,0:T(8,128)(2,1)S(1)} custom-call(bf16[8,768,512]{2,1,0:T(8,128)(2,1)} %get-tuple-element.187.a_ref, bf16[8,1408,512]{2,1,0:T(8,128)(2,1)} %bitcast.328), custom_call_target="tpu_custom_call" | custom-call | flops 8858370048 | bytes 17825792 | tf_op jit(solution)/shard_map/mlp_outer/pallas_call | solution.py:535
  574.5 13.8 %mlp_down.1 = bf16[8,1408,512]{2,1,0:T(8,128)(2,1)} custom-call(bf16[1408,768]{1,0:T(8,128)(2,1)S(1)} %assemble.10.down_ref, bf16[8,768,512]{2,1,0:T(8,128)(2,1)} %get-tuple-element.188.b_ref.act_ref), custom_call_target="tpu_custom_call" | custom-call | flops 8858370048 | bytes 23592960 | tf_op jit(solution)/shard_map/mlp_down/pallas_call | solution.py:535
  588.3 8.9 collective-permute-done.63.refs_4_
  597.2 11.6 %collective-permute-done.61.refs_2_ = bf16[176,768]{1,0:T(8,128)(2,1)} collective-permute-done((bf16[176,768]{1,0:T(8,128)(2,1)}, bf16[176,768]{1,0:T(8,128)(2,1)}, u32[]{:S(2)}, u32[]{:S(2)}) %collective-permute-start.61) | collective-permute-done | bytes 270368 | tf_op jit(solution)/shard_map/ppermute | solution.py:790
  617.0 27.5 %reduce-scatter.5.cloned.1.call-done = bf16[1,1408,512]{2,1,0:T(8,128)(2,1)} async-done(((bf16[8,1408,512]{2,1,0:T(8,128)(2,1)}), bf16[1,1408,512]{2,1,0:T(8,128)(2,1)}) %reduce-scatter.5.cloned.1.call-update) | async-done | bytes 1441808 | tf_op jit(solution)/shard_map/reduce_scatter | solution.py:1095
  661.0 13.5 %attend_back.2 = (f32[1408,512]{1,0:T(8,128)}, f32[1408,128]{1,0:T(8,128)}, bf16[1408,128]{1,0:T(8,128)(2,1)}, f32[1408,128]{1,0:T(8,128)}, bf16[1408,128]{1,0:T(8,128)(2,1)}) custom-call(bf16[1408,512]{1,0:T(8,128)(2,1)} %copy-done.21, bf16[1408,512]{1,0:T(8,128)(2,1)} %convolution_convert_fusion.1.refs_1_, ...), custom_call_target="tpu_custom_call" | custom-call | flops 2684354560 | bytes 12976128 | tf_op jit(solution)/shard_map/attend_back/pallas_call | solution.py:176
  694.3 15.6 %outer_blocks.3 = (bf16[352,1408]{1,0:T(8,128)(2,1)}, bf16[352,1408]{1,0:T(8,128)(2,1)}, bf16[704,1408]{1,0:T(8,128)(2,1)}, bf16[704,1408]{1,0:T(8,128)(2,1)}, bf16[704,1408]{1,0:T(8,128)(2,1)}) custom-call(s32[4]{0:T(128)} %pad_add_fusion.3.place_ref, bf16[1408,512]{1,0:T(8,128)(2,1)} %fusion.31.refs_0_, bf16[1408,512]{1,0:T(8,128)(2,1)} %collective-permute-done.68.refs_1_, ...), custom_call_target="tpu_custom_call" | custom-call | flops 8120172544 | bytes 22347776 | tf_op jit(solution)/shard_map/outer_blocks/pallas_call | solution.py:321
  716.1 27.7 %attend_back.3 = (f32[1408,512]{1,0:T(8,128)}, f32[1408,512]{1,0:T(8,128)}, bf16[1408,512]{1,0:T(8,128)(2,1)}, f32[1408,512]{1,0:T(8,128)}, bf16[1408,512]{1,0:T(8,128)(2,1)}) custom-call(bf16[1408,512]{1,0:T(8,128)(2,1)} %bitcast.240, bf16[1408,512]{1,0:T(8,128)(2,1)} %convolution_convert_fusion.refs_1_, ...), custom_call_target="tpu_custom_call" | custom-call | flops 10737418240 | bytes 25952256 | tf_op jit(solution)/shard_map/attend_back/pallas_call | solution.py:176
  806.0 17.4 %outer_blocks.4 = (bf16[352,1408]{1,0:T(8,128)(2,1)}, bf16[352,1408]{1,0:T(8,128)(2,1)}, bf16[704,1408]{1,0:T(8,128)(2,1)}, bf16[704,1408]{1,0:T(8,128)(2,1)}, bf16[704,1408]{1,0:T(8,128)(2,1)}) custom-call(s32[4]{0:T(128)} %pad_add_fusion.3.place_ref, bf16[1408,512]{1,0:T(8,128)(2,1)} %fusion.57.refs_0_, bf16[1408,512]{1,0:T(8,128)(2,1)} %collective-permute-done.74.refs_1_, ...), custom_call_target="tpu_custom_call" | custom-call | flops 8120172544 | bytes 22347776 | tf_op jit(solution)/shard_map/outer_blocks/pallas_call | solution.py:321
  825.1 9.0 fusion.26
  883.0 29.6 %collective-permute-start.90 = (bf16[1408,512]{1,0:T(8,128)(2,1)}, bf16[1408,512]{1,0:T(8,128)(2,1)}, u32[]{:S(2)}, u32[]{:S(2)}) collective-permute-start(bf16[1408,512]{1,0:T(8,128)(2,1)} %bitcast.79.refs_0_), channel_id=1, source_target_pairs={{0,4},{4,0},{1,5},{5,1},{2,6},{6,2},{3,7},{7,3},{8,12},{12,8},{9,1... | collective-permute-start | bytes 4325384 | tf_op jit(solution)/shard_map/ppermute | solution.py:675
  919.1 10.0 stack_sum.1
  931.1 9.4 outer_blocks.5
  942.1 10.9 %fusion.90 = f32[512,2816]{1,0:T(8,128)} fusion(bf16[512,1408]{0,1:T(8,128)(2,1)} %bitcast.107, bf16[1408,2816]{1,0:T(8,128)(2,1)} %copy-done.3), kind=kOutput, calls=%fused_computation.324 | convolution fusion | flops 4060086272 | bytes 15138816 | tf_op jit(solution)/shard_map/dot_general | solution.py:70
  983.0 14.0 %collective-permute-done.92.refs_1_ = bf16[176,2816]{1,0:T(8,128)(2,1)S(1)} collective-permute-done((bf16[176,2816]{1,0:T(8,128)(2,1)}, bf16[176,2816]{1,0:T(8,128)(2,1)S(1)}, u32[]{:S(2)}, u32[]{:S(2)}) %collective-permute-start.92) | collective-permute-done | bytes 991264 | tf_op jit(solution)/shard_map/ppermute | solution.py:675
  (822 shorter events, 550.9 us)
Async XLA Ops:
  7.2 76.1 %all-gather.11.cloned.1.call-start = ((), (), s32[]{:S(2)}) async-start(), calls=%async_computation.8 | async-start | bytes 2703360 | tf_op jit(solution)/shard_map/all_gather | solution.py:918
  10.3 181.8 %all-gather.13.cloned.1.call-start = ((), (), s32[]{:S(2)}) async-start(), calls=%async_computation.9 | async-start | bytes 3379200 | tf_op jit(solution)/shard_map/all_gather | solution.py:919
  50.5 308.5 %all-gather.15.cloned.1.call-start = ((), (), s32[]{:S(2)}) async-start(), calls=%async_computation.10 | async-start | bytes 5652480 | tf_op jit(solution)/shard_map/all_gather | solution.py:952
  93.7 44.8 %collective-permute-start.14 = (bf16[704,1408]{1,0:T(8,128)(2,1)S(1)}, bf16[704,1408]{1,0:T(8,128)(2,1)S(1)}, u32[]{:S(2)}, u32[]{:S(2)}) collective-permute-start(bf16[704,1408]{1,0:T(8,128)(2,1)S(1)} %join_gathered.1.refs_1_), channel_id=1, source_target_pairs={{0,8},{8,0},{1,9},{9,1},{2,10},{10,2},{3,11},{11,3},{4,12},{12,4},... | collective-permute-start | bytes 5947400 | tf_op jit(solution)/shard_map/ppermute | solution.py:675
  94.3 44.5 %collective-permute-start.15 = (bf16[704,1408]{1,0:T(8,128)(2,1)S(1)}, bf16[704,1408]{1,0:T(8,128)(2,1)S(1)}, u32[]{:S(2)}, u32[]{:S(2)}) collective-permute-start(bf16[704,1408]{1,0:T(8,128)(2,1)S(1)} %join_gathered.1.refs_1_), channel_id=1, source_target_pairs={{0,16},{16,0},{1,17},{17,1},{2,18},{18,2},{3,19},{19,3},{4,20},{20... | collective-permute-start | bytes 5947400 | tf_op jit(solution)/shard_map/ppermute | solution.py:675
  99.6 75.7 %collective-permute-start.25 = (bf16[2,1408]{1,0:T(2,128)(2,1)S(1)}, bf16[2,1408]{1,0:T(2,128)(2,1)S(1)}, u32[]{:S(2)}, u32[]{:S(2)}) collective-permute-start(bf16[2,1408]{1,0:T(2,128)(2,1)S(1)} %copy-done.163), channel_id=1, source_target_pairs={{0,4},{4,0},{1,5},{5,1},{2,6},{6,2},{3,7},{7,3},{8,12},{12,8},{9,1... | collective-permute-start | bytes 16904 | tf_op jit(solution)/shard_map/ppermute | solution.py:675
  141.4 46.5 %collective-permute-start.16 = (bf16[352,1408]{1,0:T(8,128)(2,1)}, bf16[352,1408]{1,0:T(8,128)(2,1)S(1)}, u32[]{:S(2)}, u32[]{:S(2)}) collective-permute-start(bf16[352,1408]{1,0:T(8,128)(2,1)} %slice.227), channel_id=1, source_target_pairs={{0,16},{16,0},{1,17},{17,1},{2,18},{18,2},{3,19},{19,3},{4,20},{20... | collective-permute-start | bytes 2973704 | tf_op jit(solution)/shard_map/ppermute | solution.py:675
  159.8 45.5 %collective-permute-start.20 = (bf16[704,1408]{1,0:T(8,128)(2,1)S(1)}, bf16[704,1408]{1,0:T(8,128)(2,1)}, u32[]{:S(2)}, u32[]{:S(2)}) collective-permute-start(bf16[704,1408]{1,0:T(8,128)(2,1)S(1)} %join_gathered.1.refs_1_), channel_id=1, source_target_pairs={{0,4},{4,0},{1,5},{5,1},{2,6},{6,2},{3,7},{7,3},{8,12},{12,8},{9,1... | collective-permute-start | bytes 5947400 | tf_op jit(solution)/shard_map/ppermute | solution.py:675
  201.6 199.1 %all-gather.17.cloned.1.call-start = ((), (), s32[]{:S(2)}) async-start(), calls=%async_computation.11 | async-start | bytes 12976128 | tf_op jit(solution)/shard_map/all_gather | solution.py:1052
  205.3 57.3 %collective-permute-start.18 = (bf16[528,1408]{1,0:T(8,128)(2,1)}, bf16[528,1408]{1,0:T(8,128)(2,1)}, u32[]{:S(2)}, u32[]{:S(2)}) collective-permute-start(bf16[528,1408]{1,0:T(8,128)(2,1)} %get-tuple-element.142.refs_1_), channel_id=1, source_target_pairs={{0,8},{8,0},{1,9},{9,1},{2,10},{10,2},{3,11},{11,3},{4,12},{12,4},... | collective-permute-start | bytes 4460552 | tf_op jit(solution)/shard_map/ppermute | solution.py:675
  205.9 58.3 %collective-permute-start.19 = (bf16[528,1408]{1,0:T(8,128)(2,1)}, bf16[528,1408]{1,0:T(8,128)(2,1)S(1)}, u32[]{:S(2)}, u32[]{:S(2)}) collective-permute-start(bf16[528,1408]{1,0:T(8,128)(2,1)} %get-tuple-element.142.refs_1_), channel_id=1, source_target_pairs={{0,16},{16,0},{1,17},{17,1},{2,18},{18,2},{3,19},{19,3},{4,20},{20... | collective-permute-start | bytes 4460552 | tf_op jit(solution)/shard_map/ppermute | solution.py:675
  206.4 55.4 %collective-permute-start.28 = (bf16[352,1024]{1,0:T(8,128)(2,1)}, bf16[352,1024]{1,0:T(8,128)(2,1)}, u32[]{:S(2)}, u32[]{:S(2)}) collective-permute-start(bf16[352,1024]{1,0:T(8,128)(2,1)} %get-tuple-element.150.refs_1_), channel_id=1, source_target_pairs={{0,8},{8,0},{1,9},{9,1},{2,10},{10,2},{3,11},{11,3},{4,12},{12,4},... | collective-permute-start | bytes 2162696 | tf_op jit(solution)/shard_map/ppermute | solution.py:675
  262.6 41.2 %collective-permute-start.38 = (bf16[320,1408]{1,0:T(8,128)(2,1)S(1)}, bf16[320,1408]{1,0:T(8,128)(2,1)S(1)}, u32[]{:S(2)}, u32[]{:S(2)}) collective-permute-start(bf16[320,1408]{1,0:T(8,128)(2,1)S(1)} %get-tuple-element.368), channel_id=1, source_target_pairs={{0,1},{1,0},{2,5},{3,4},{4,3},{5,2},{6,7},{7,6},{8,9},{9,8},{10,13... | collective-permute-start | bytes 2703368 | tf_op jit(solution)/shard_map/ppermute | solution.py:726
  309.2 179.2 %all-gather.19.cloned.1.call-start = ((), (), s32[]{:S(2)}) async-start(), calls=%async_computation.12 | async-start | bytes 12976128 | tf_op jit(solution)/shard_map/all_gather | solution.py:1072
  342.6 42.3 %collective-permute-start.46 = (bf16[1408,128]{1,0:T(8,128)(2,1)}, bf16[1408,128]{1,0:T(8,128)(2,1)}, u32[]{:S(2)}, u32[]{:S(2)}) collective-permute-start(bf16[1408,128]{1,0:T(8,128)(2,1)} %fusion.51.refs_1_.refs_4_), channel_id=1, source_target_pairs={{0,4},{4,0},{1,5},{5,1},{2,6},{6,2},{3,7},{7,3},{8,12},{12,8},{9,1... | collective-permute-start | bytes 1081352 | tf_op jit(solution)/shard_map/ppermute | solution.py:675
  343.0 41.9 %collective-permute-start.47 = (bf16[1408,128]{1,0:T(8,128)(2,1)}, bf16[1408,128]{1,0:T(8,128)(2,1)}, u32[]{:S(2)}, u32[]{:S(2)}) collective-permute-start(bf16[1408,128]{1,0:T(8,128)(2,1)} %slice.429.refs_3_.refs_6_), channel_id=1, source_target_pairs={{0,4},{4,0},{1,5},{5,1},{2,6},{6,2},{3,7},{7,3},{8,12},{12,8},{9,1... | collective-permute-start | bytes 1081352 | tf_op jit(solution)/shard_map/ppermute | solution.py:675
  400.8 243.7 %reduce-scatter.5.cloned.1.call-start = ((), (), s32[]{:S(2)}) async-start(), calls=%async_computation.4 | async-start | bytes 12976128 | tf_op jit(solution)/shard_map/reduce_scatter | solution.py:1095
  404.9 56.9 %collective-permute-start.55 = (bf16[1408,512]{1,0:T(8,128)(2,1)}, bf16[1408,512]{1,0:T(8,128)(2,1)}, u32[]{:S(2)}, u32[]{:S(2)}) collective-permute-start(bf16[1408,512]{1,0:T(8,128)(2,1)} %fusion.23.refs_8_), channel_id=1, source_target_pairs={{0,4},{4,0},{1,5},{5,1},{2,6},{6,2},{3,7},{7,3},{8,12},{12,8},{9,1... | collective-permute-start | bytes 4325384 | tf_op jit(solution)/shard_map/ppermute | solution.py:675
  406.9 54.9 %collective-permute-start.56 = (bf16[1408,512]{1,0:T(8,128)(2,1)}, bf16[1408,512]{1,0:T(8,128)(2,1)}, u32[]{:S(2)}, u32[]{:S(2)}) collective-permute-start(bf16[1408,512]{1,0:T(8,128)(2,1)} %get-tuple-element.162.refs_2_.refs_6_), channel_id=1, source_target_pairs={{0,4},{4,0},{1,5},{5,1},{2,6},{6,2},{3,7},{7,3},{8,12},{12,8},{9,1... | collective-permute-start | bytes 4325384 | tf_op jit(solution)/shard_map/ppermute | solution.py:675
  411.4 50.4 %collective-permute-start.59 = (bf16[1408,512]{1,0:T(8,128)(2,1)}, bf16[1408,512]{1,0:T(8,128)(2,1)}, u32[]{:S(2)}, u32[]{:S(2)}) collective-permute-start(bf16[1408,512]{1,0:T(8,128)(2,1)} %get-tuple-element.170.refs_2_.refs_6_), channel_id=1, source_target_pairs={{0,4},{4,0},{1,5},{5,1},{2,6},{6,2},{3,7},{7,3},{8,12},{12,8},{9,1... | collective-permute-start | bytes 4325384 | tf_op jit(solution)/shard_map/ppermute | solution.py:675
  417.4 44.5 %collective-permute-start.57 = (bf16[1408,512]{1,0:T(8,128)(2,1)}, bf16[1408,512]{1,0:T(8,128)(2,1)}, u32[]{:S(2)}, u32[]{:S(2)}) collective-permute-start(bf16[1408,512]{1,0:T(8,128)(2,1)} %multiply_convert_fusion.1.refs_8_), channel_id=1, source_target_pairs={{0,4},{4,0},{1,5},{5,1},{2,6},{6,2},{3,7},{7,3},{8,12},{12,8},{9,1... | collective-permute-start | bytes 4325384 | tf_op jit(solution)/shard_map/ppermute | solution.py:675
  536.5 224.2 %reduce-scatter.7.cloned.1.call-start = ((), (), s32[]{:S(2)}) async-start(), calls=%async_computation.5 | async-start | bytes 12976128 | tf_op jit(solution)/shard_map/reduce_scatter | solution.py:1184
  644.5 216.4 %reduce-scatter.9.cloned.1.call-start = ((), (), s32[]{:S(2)}) async-start(), calls=%async_computation.6 | async-start | bytes 5652480 | tf_op jit(solution)/shard_map/reduce_scatter | solution.py:1188
  711.2 41.4 %collective-permute-start.78 = (bf16[352,1408]{1,0:T(8,128)(2,1)}, bf16[352,1408]{1,0:T(8,128)(2,1)}, u32[]{:S(2)}, u32[]{:S(2)}) collective-permute-start(bf16[352,1408]{1,0:T(8,128)(2,1)} %get-tuple-element.215), channel_id=1, source_target_pairs={{0,16},{16,0},{1,17},{17,1},{2,18},{18,2},{3,19},{19,3},{4,20},{20... | collective-permute-start | bytes 2973704 | tf_op jit(solution)/shard_map/ppermute | solution.py:675
  743.9 300.9 %reduce-scatter.11.cloned.1.call-start = ((), (), s32[]{:S(2)}) async-start(), calls=%async_computation.7 | async-start | bytes 5406720 | tf_op jit(solution)/shard_map/reduce_scatter | solution.py:1238
  783.1 56.1 %collective-permute-start.82 = (bf16[704,1408]{1,0:T(8,128)(2,1)}, bf16[704,1408]{1,0:T(8,128)(2,1)}, u32[]{:S(2)}, u32[]{:S(2)}) collective-permute-start(bf16[704,1408]{1,0:T(8,128)(2,1)} %add_dynamic-update-slice_fusion.3), channel_id=1, source_target_pairs={{0,16},{16,0},{1,17},{17,1},{2,18},{18,2},{3,19},{19,3},{4,20},{20... | collective-permute-start | bytes 5947400 | tf_op jit(solution)/shard_map/ppermute | solution.py:675
  784.5 55.7 %collective-permute-start.83 = (bf16[704,1408]{1,0:T(8,128)(2,1)}, bf16[704,1408]{1,0:T(8,128)(2,1)}, u32[]{:S(2)}, u32[]{:S(2)}) collective-permute-start(bf16[704,1408]{1,0:T(8,128)(2,1)} %add_dynamic-update-slice_fusion.2), channel_id=1, source_target_pairs={{0,8},{8,0},{1,9},{9,1},{2,10},{10,2},{3,11},{11,3},{4,12},{12,4},... | collective-permute-start | bytes 5947400 | tf_op jit(solution)/shard_map/ppermute | solution.py:675
  795.6 54.9 %collective-permute-start.81 = (bf16[320,1408]{1,0:T(8,128)(2,1)}, bf16[320,1408]{1,0:T(8,128)(2,1)}, u32[]{:S(2)}, u32[]{:S(2)}) collective-permute-start(bf16[320,1408]{1,0:T(8,128)(2,1)} %get-tuple-element.365), channel_id=1, source_target_pairs={{1,0},{0,1},{5,2},{4,3},{3,4},{2,5},{7,6},{6,7},{9,8},{8,9},{13,10... | collective-permute-start | bytes 2703368 | tf_op jit(solution)/shard_map/ppermute | solution.py:735
  797.2 53.4 %collective-permute-start.73 = (bf16[320,1408]{1,0:T(8,128)(2,1)}, bf16[320,1408]{1,0:T(8,128)(2,1)}, u32[]{:S(2)}, u32[]{:S(2)}) collective-permute-start(bf16[320,1408]{1,0:T(8,128)(2,1)} %get-tuple-element.366), channel_id=1, source_target_pairs={{0,0},{1,1},{4,2},{5,3},{2,4},{3,5},{6,6},{7,7},{8,8},{9,9},{12,10... | collective-permute-start | bytes 2703368 | tf_op jit(solution)/shard_map/ppermute | solution.py:735
  865.9 53.2 %collective-permute-start.88 = (bf16[704,1408]{1,0:T(8,128)(2,1)}, bf16[704,1408]{1,0:T(8,128)(2,1)}, u32[]{:S(2)}, u32[]{:S(2)}) collective-permute-start(bf16[704,1408]{1,0:T(8,128)(2,1)} %add_dynamic-update-slice_fusion.1), channel_id=1, source_target_pairs={{0,16},{16,0},{1,17},{17,1},{2,18},{18,2},{3,19},{19,3},{4,20},{20... | collective-permute-start | bytes 5947400 | tf_op jit(solution)/shard_map/ppermute | solution.py:675
  870.0 49.1 %collective-permute-start.89 = (bf16[704,1408]{1,0:T(8,128)(2,1)}, bf16[704,1408]{1,0:T(8,128)(2,1)}, u32[]{:S(2)}, u32[]{:S(2)}) collective-permute-start(bf16[704,1408]{1,0:T(8,128)(2,1)} %add_dynamic-update-slice_fusion), channel_id=1, source_target_pairs={{0,8},{8,0},{1,9},{9,1},{2,10},{10,2},{3,11},{11,3},{4,12},{12,4},... | collective-permute-start | bytes 5947400 | tf_op jit(solution)/shard_map/ppermute | solution.py:675
  883.0 48.1 %collective-permute-start.90 = (bf16[1408,512]{1,0:T(8,128)(2,1)}, bf16[1408,512]{1,0:T(8,128)(2,1)}, u32[]{:S(2)}, u32[]{:S(2)}) collective-permute-start(bf16[1408,512]{1,0:T(8,128)(2,1)} %bitcast.79.refs_0_), channel_id=1, source_target_pairs={{0,4},{4,0},{1,5},{5,1},{2,6},{6,2},{3,7},{7,3},{8,12},{12,8},{9,1... | collective-permute-start | bytes 4325384 | tf_op jit(solution)/shard_map/ppermute | solution.py:675
  (263 other events, 3135.7 us)
Sparse Core Ops, SparseCore 0:
  10.4 64.2 all-gather.10
  76.3 55.6 all-gather.12
  201.7 102.0 all-gather.14
  309.3 88.0 all-gather.16
  400.9 87.4 all-gather.18
  536.6 107.8 reduce-scatter.4
  648.0 103.1 reduce-scatter.6
  753.5 107.3 reduce-scatter.8
  942.2 78.0 reduce-scatter.10

commit v5 on v4

--- a/solution.py
+++ b/solution.py
@@ -1298,7 +1298,8 @@
         shift_plane = held[:, 0].reshape(plane, cores, width).sum(axis=1)
         gain_plane = sum(held[i, 1:-lat_count] for i in range(8))
         cond_rows = held[:, -lat_count:].reshape(-1, width)
-        columns = z_order(z_send(jnp.concatenate([gain_plane, shift_plane], axis=0)))
+        sums = after(jnp.concatenate([gain_plane, shift_plane], axis=0), *skip_sum)
+        columns = z_order(z_send(sums))
         gain_rows = len(gain_plane)
         grad_gains = sum(column[:gain_rows] for column in columns).reshape(-1)
         shift_grads = jnp.stack([column[gain_rows:] for column in columns], axis=1)

time: 1090 us -> 1090 us (level)
  transfers between devices with their start and end apart: 117 -> 117, of which waited for: 35 -> 34; matrix products, arithmetic and copies ran while one was open for 29% -> 28% of each run, Pallas kernels for 18% -> 18%
where the time goes in v5:
time: 1090 us; the launch traced here: 1080 us
  waiting for transfers between devices  276 us (25%)
  Pallas kernels  252 us (23%)
  starting transfers between devices  172 us (16%)
  other arithmetic  147 us (13%)
  local copies, waits for them, and re-layouts  136 us (12%)
  matrix products  76.1 us (7%)
  between operations  16.9 us (2%)
    ppermute x70, starting transfers between devices, swap(): return lax.ppermute(values, axis, SWAP)  103 us
    pallas_call x5, Pallas kernels, mlp_call(): pl.pallas_call(kernel, grid=(count,), in_specs=[kept(x.shape) for x in he...  88.7 us
    dot_general x15, matrix products, dot(): return lax.dot_general(a, b, (dims, ((), ())), preferred_element_type=f32)  75 us
    ppermute x70, waiting for transfers between devices, swap(): return lax.ppermute(values, axis, SWAP)  72.9 us
    unnamed x373, local copies, waits for them, and re-layouts  68.5 us
    ppermute x21, waiting for transfers between devices, to_rank(): return lax.ppermute(values, axes, [(i, last - i) for i in range(last + 1)])  66 us
    ppermute x9, waiting for transfers between devices, z_shift(): lax.ppermute(values, 'z', [(z, (z + step) % seq) for z in range(seq)])  44.8 us
    pallas_call x3, Pallas kernels, outer_blocks(): pl.pallas_call(functools.partial(outer_kernel, heights, sharing, half), g...  42.5 us
  transfers between devices with their start and end apart: 117, of which 34 were waited for; matrix products, arithmetic and copies ran while one was open for 28% of the time, Pallas kernels for 18%

profile of v5, /device:TPU:0, one launch (start us, length us, event | category | flops | bytes accessed | tf_op | source)
XLA Modules:
  0.0 1076.5 jit_solution(16073637081108188858)
XLA Ops:
  23.1 22.4 %collective-permute-done.1.refs_2_ = bf16[176,704]{1,0:T(8,128)(2,1)S(1)} collective-permute-done((bf16[176,704]{1,0:T(8,128)(2,1)}, bf16[176,704]{1,0:T(8,128)(2,1)S(1)}, u32[]{:S(2)}, u32[]{:S(2)}) %collective-permute-start.1) | collective-permute-done | bytes 247840 | tf_op jit(solution)/shard_map/ppermute | solution.py:752
  58.9 11.4 %collective-permute-done.4.refs_3_ = bf16[176,2816]{1,0:T(8,128)(2,1)} collective-permute-done((bf16[176,2816]{1,0:T(8,128)(2,1)S(1)}, bf16[176,2816]{1,0:T(8,128)(2,1)}, u32[]{:S(2)}, u32[]{:S(2)}) %collective-permute-start.4) | collective-permute-done | bytes 991264 | tf_op jit(solution)/shard_map/ppermute | solution.py:675
  108.9 29.6 %collective-permute-done.14.refs_2_ = bf16[704,1408]{1,0:T(8,128)(2,1)S(1)} collective-permute-done((bf16[704,1408]{1,0:T(8,128)(2,1)S(1)}, bf16[704,1408]{1,0:T(8,128)(2,1)S(1)}, u32[]{:S(2)}, u32[]{:S(2)}) %collective-permute-start.14) | collective-permute-done | bytes 1982496 | tf_op jit(solution)/shard_map/ppermute | solution.py:675
  159.8 13.3 %collective-permute-start.20 = (bf16[704,1408]{1,0:T(8,128)(2,1)S(1)}, bf16[704,1408]{1,0:T(8,128)(2,1)}, u32[]{:S(2)}, u32[]{:S(2)}) collective-permute-start(bf16[704,1408]{1,0:T(8,128)(2,1)S(1)} %join_gathered.1.refs_1_), channel_id=1, source_target_pairs={{0,4},{4,0},{1,5},{5,1},{2,6},{6,2},{3,7},{7,3},{8,12},{12,8},{9,1... | collective-permute-start | bytes 5947400 | tf_op jit(solution)/shard_map/ppermute | solution.py:675
  250.0 11.6 %pad_maximum_fusion.4 = bf16[16,88,512]{2,1,0:T(8,128)(2,1)S(1)} fusion(bf16[16,22,512]{2,1,0:T(8,128)(2,1)S(1)} %get-tuple-element.343, bf16[16,22,512]{2,1,0:T(8,128)(2,1)S(1)} %get-tuple-element.344, bf16[16,22,512]{2,1,0:T(8,128)(2,1)S(1)} %get-tuple-element.334, bf16[16,22,512]{2,1,0:T(8,128)(2,1)S(1)} %get-tuple-element.333), kind=kLoop, calls=%fused_computation.107 | loop fusion | flops 5767168 | bytes 2883584 | tf_op jit(solution)/shard_map/concatenate | solution.py:58
  267.7 11.9 %attend.2 = (bf16[1408,512]{1,0:T(8,128)(2,1)}, f32[8,2,512]{2,1,0:T(2,128)S(1)}) custom-call(bf16[1408,512]{1,0:T(8,128)(2,1)S(1)} %bitcast.239, bf16[1408,512]{1,0:T(8,128)(2,1)S(1)} %bitcast.237, bf16[1408,512]{1,0:T(8,128)(2,1)S(1)} %collective-permute-done.30.refs_2_.refs_5_, bf16[1408,512]{1,0:T(8,128)(2,1)} %convolution_convert_fusion.2.refs_3_.refs_6_, ...), custom_call_target="tpu_custom_call" | custom-call | flops 4294967296 | bytes 10092544 | tf_op jit(solution)/shard_map/attend/pallas_call | solution.py:114
  284.2 19.5 %collective-permute-done.38 = bf16[320,1408]{1,0:T(8,128)(2,1)S(1)} collective-permute-done((bf16[320,1408]{1,0:T(8,128)(2,1)S(1)}, bf16[320,1408]{1,0:T(8,128)(2,1)S(1)}, u32[]{:S(2)}, u32[]{:S(2)}) %collective-permute-start.38) | collective-permute-done | bytes 901152 | tf_op jit(solution)/shard_map/ppermute | solution.py:726
  309.2 13.3 %collective-permute-start.41 = (bf16[352,1024]{1,0:T(8,128)(2,1)}, bf16[352,1024]{1,0:T(8,128)(2,1)S(1)}, u32[]{:S(2)}, u32[]{:S(2)}) collective-permute-start(bf16[352,1024]{1,0:T(8,128)(2,1)} %get-tuple-element.151.refs_1_), channel_id=1, source_target_pairs={{0,4},{4,0},{1,5},{5,1},{2,6},{6,2},{3,7},{7,3},{8,12},{12,8},{9,1... | collective-permute-start | bytes 2162696 | tf_op jit(solution)/shard_map/ppermute | solution.py:675
  343.1 10.1 assemble.8
  384.9 8.9 attend.3
  422.4 14.2 %collective-permute-done.50.refs_4_ = bf16[176,768]{1,0:T(8,128)(2,1)S(1)} collective-permute-done((bf16[176,768]{1,0:T(8,128)(2,1)S(1)}, bf16[176,768]{1,0:T(8,128)(2,1)S(1)}, u32[]{:S(2)}, u32[]{:S(2)}) %collective-permute-start.50) | collective-permute-done | bytes 270368 | tf_op jit(solution)/shard_map/ppermute | solution.py:790
  438.0 9.7 collective-permute-done.49.refs_3_
  449.2 9.0 collective-permute-done.48.refs_2_
  466.2 22.2 %all-gather.19.cloned.1.call-done = bf16[11264,512]{1,0:T(8,128)(2,1)} async-done(((bf16[1408,512]{1,0:T(8,128)(2,1)}), bf16[11264,512]{1,0:T(8,128)(2,1)}) %all-gather.19.cloned.1.call-update) | async-done | bytes 11534352 | tf_op jit(solution)/shard_map/all_gather | solution.py:1072
  490.0 18.0 %mlp_up.1 = (f32[8,768,512]{2,1,0:T(8,128)}, bf16[8,768,512]{2,1,0:T(8,128)(2,1)}) custom-call(bf16[768,1408]{1,0:T(8,128)(2,1)S(1)} %copy-done.13, bf16[8,1408,512]{2,1,0:T(8,128)(2,1)} %bitcast.327), custom_call_target="tpu_custom_call" | custom-call | flops 8858370048 | bytes 30408704 | tf_op jit(solution)/shard_map/mlp_up/pallas_call | solution.py:535
  508.0 28.4 %mlp_back.1 = (bf16[8,768,512]{2,1,0:T(8,128)(2,1)}, bf16[8,1408,512]{2,1,0:T(8,128)(2,1)}) custom-call(bf16[768,1408]{1,0:T(8,128)(2,1)S(1)} %bitcast.234, bf16[1408,768]{1,0:T(8,128)(2,1)S(1)} %bitcast.235, bf16[8,1408,512]{2,1,0:T(8,128)(2,1)} %bitcast.325, f32[8,768,512]{2,1,0:T(8,128)} %get-tuple-element.184.hidden_ref), custom_call_target="tpu_custom_call" | custom-call | flops 17716740096 | bytes 44564480 | tf_op jit(solution)/shard_map/mlp_back/pallas_call | solution.py:535
  536.6 13.7 %mlp_outer.2 = bf16[1408,768]{1,0:T(8,128)(2,1)S(1)} custom-call(bf16[8,1408,512]{2,1,0:T(8,128)(2,1)} %bitcast.326, bf16[8,768,512]{2,1,0:T(8,128)(2,1)} %get-tuple-element.189.b_ref.act_ref), custom_call_target="tpu_custom_call" | custom-call | flops 8858370048 | bytes 17825792 | tf_op jit(solution)/shard_map/mlp_outer/pallas_call | solution.py:535
  554.4 14.7 %mlp_outer.3.up_ref = bf16[768,1408]{1,0:T(8,128)(2,1)S(1)} custom-call(bf16[8,768,512]{2,1,0:T(8,128)(2,1)} %get-tuple-element.188.a_ref, bf16[8,1408,512]{2,1,0:T(8,128)(2,1)} %bitcast.328), custom_call_target="tpu_custom_call" | custom-call | flops 8858370048 | bytes 17825792 | tf_op jit(solution)/shard_map/mlp_outer/pallas_call | solution.py:535
  574.5 13.8 %mlp_down.1 = bf16[8,1408,512]{2,1,0:T(8,128)(2,1)} custom-call(bf16[1408,768]{1,0:T(8,128)(2,1)S(1)} %assemble.10.down_ref, bf16[8,768,512]{2,1,0:T(8,128)(2,1)} %get-tuple-element.189.b_ref.act_ref), custom_call_target="tpu_custom_call" | custom-call | flops 8858370048 | bytes 23592960 | tf_op jit(solution)/shard_map/mlp_down/pallas_call | solution.py:535
  597.2 11.6 %collective-permute-done.61.refs_2_ = bf16[176,768]{1,0:T(8,128)(2,1)} collective-permute-done((bf16[176,768]{1,0:T(8,128)(2,1)}, bf16[176,768]{1,0:T(8,128)(2,1)}, u32[]{:S(2)}, u32[]{:S(2)}) %collective-permute-start.61) | collective-permute-done | bytes 270368 | tf_op jit(solution)/shard_map/ppermute | solution.py:790
  617.0 27.5 %reduce-scatter.5.cloned.1.call-done = bf16[1,1408,512]{2,1,0:T(8,128)(2,1)} async-done(((bf16[8,1408,512]{2,1,0:T(8,128)(2,1)}), bf16[1,1408,512]{2,1,0:T(8,128)(2,1)}) %reduce-scatter.5.cloned.1.call-update) | async-done | bytes 1441808 | tf_op jit(solution)/shard_map/reduce_scatter | solution.py:1095
  661.0 13.5 %attend_back.2 = (f32[1408,512]{1,0:T(8,128)}, f32[1408,128]{1,0:T(8,128)}, bf16[1408,128]{1,0:T(8,128)(2,1)}, f32[1408,128]{1,0:T(8,128)}, bf16[1408,128]{1,0:T(8,128)(2,1)}) custom-call(bf16[1408,512]{1,0:T(8,128)(2,1)} %copy-done.21, bf16[1408,512]{1,0:T(8,128)(2,1)} %convolution_convert_fusion.1.refs_1_, ...), custom_call_target="tpu_custom_call" | custom-call | flops 2684354560 | bytes 12976128 | tf_op jit(solution)/shard_map/attend_back/pallas_call | solution.py:176
  694.3 15.6 %outer_blocks.3 = (bf16[352,1408]{1,0:T(8,128)(2,1)}, bf16[352,1408]{1,0:T(8,128)(2,1)}, bf16[704,1408]{1,0:T(8,128)(2,1)}, bf16[704,1408]{1,0:T(8,128)(2,1)}, bf16[704,1408]{1,0:T(8,128)(2,1)}) custom-call(s32[4]{0:T(128)} %pad_add_fusion.3.place_ref, bf16[1408,512]{1,0:T(8,128)(2,1)} %fusion.31.refs_0_, bf16[1408,512]{1,0:T(8,128)(2,1)} %collective-permute-done.68.refs_1_, ...), custom_call_target="tpu_custom_call" | custom-call | flops 8120172544 | bytes 22347776 | tf_op jit(solution)/shard_map/outer_blocks/pallas_call | solution.py:321
  716.1 27.7 %attend_back.3 = (f32[1408,512]{1,0:T(8,128)}, f32[1408,512]{1,0:T(8,128)}, bf16[1408,512]{1,0:T(8,128)(2,1)}, f32[1408,512]{1,0:T(8,128)}, bf16[1408,512]{1,0:T(8,128)(2,1)}) custom-call(bf16[1408,512]{1,0:T(8,128)(2,1)} %bitcast.240, bf16[1408,512]{1,0:T(8,128)(2,1)} %convolution_convert_fusion.refs_1_, ...), custom_call_target="tpu_custom_call" | custom-call | flops 10737418240 | bytes 25952256 | tf_op jit(solution)/shard_map/attend_back/pallas_call | solution.py:176
  806.0 17.4 %outer_blocks.4 = (bf16[352,1408]{1,0:T(8,128)(2,1)}, bf16[352,1408]{1,0:T(8,128)(2,1)}, bf16[704,1408]{1,0:T(8,128)(2,1)}, bf16[704,1408]{1,0:T(8,128)(2,1)}, bf16[704,1408]{1,0:T(8,128)(2,1)}) custom-call(s32[4]{0:T(128)} %pad_add_fusion.3.place_ref, bf16[1408,512]{1,0:T(8,128)(2,1)} %fusion.57.refs_0_, bf16[1408,512]{1,0:T(8,128)(2,1)} %collective-permute-done.74.refs_1_, ...), custom_call_target="tpu_custom_call" | custom-call | flops 8120172544 | bytes 22347776 | tf_op jit(solution)/shard_map/outer_blocks/pallas_call | solution.py:321
  825.1 9.0 fusion.26
  883.0 29.6 %collective-permute-start.90 = (bf16[1408,512]{1,0:T(8,128)(2,1)}, bf16[1408,512]{1,0:T(8,128)(2,1)}, u32[]{:S(2)}, u32[]{:S(2)}) collective-permute-start(bf16[1408,512]{1,0:T(8,128)(2,1)} %bitcast.79.refs_0_), channel_id=1, source_target_pairs={{0,4},{4,0},{1,5},{5,1},{2,6},{6,2},{3,7},{7,3},{8,12},{12,8},{9,1... | collective-permute-start | bytes 4325384 | tf_op jit(solution)/shard_map/ppermute | solution.py:675
  919.1 10.0 stack_sum.1
  931.1 9.4 outer_blocks.5
  942.1 10.9 %fusion.90 = f32[512,2816]{1,0:T(8,128)} fusion(bf16[512,1408]{0,1:T(8,128)(2,1)} %bitcast.107, bf16[1408,2816]{1,0:T(8,128)(2,1)} %copy-done.3), kind=kOutput, calls=%fused_computation.324 | convolution fusion | flops 4060086272 | bytes 15138816 | tf_op jit(solution)/shard_map/dot_general | solution.py:70
  983.0 14.0 %collective-permute-done.92.refs_1_ = bf16[176,2816]{1,0:T(8,128)(2,1)S(1)} collective-permute-done((bf16[176,2816]{1,0:T(8,128)(2,1)}, bf16[176,2816]{1,0:T(8,128)(2,1)S(1)}, u32[]{:S(2)}, u32[]{:S(2)}) %collective-permute-start.92) | collective-permute-done | bytes 991264 | tf_op jit(solution)/shard_map/ppermute | solution.py:675
  1033.0 10.8 %collective-permute-done.103 = bf16[176,704]{1,0:T(8,128)(2,1)} collective-permute-done((bf16[176,704]{1,0:T(8,128)(2,1)S(1)}, bf16[176,704]{1,0:T(8,128)(2,1)}, u32[]{:S(2)}, u32[]{:S(2)}) %collective-permute-start.103) | collective-permute-done | bytes 247840 | tf_op jit(solution)/shard_map/ppermute | solution.py:752
  (822 shorter events, 556.7 us)
Async XLA Ops:
  7.2 76.1 %all-gather.11.cloned.1.call-start = ((), (), s32[]{:S(2)}) async-start(), calls=%async_computation.8 | async-start | bytes 2703360 | tf_op jit(solution)/shard_map/all_gather | solution.py:918
  10.3 181.8 %all-gather.13.cloned.1.call-start = ((), (), s32[]{:S(2)}) async-start(), calls=%async_computation.9 | async-start | bytes 3379200 | tf_op jit(solution)/shard_map/all_gather | solution.py:919
  50.5 308.5 %all-gather.15.cloned.1.call-start = ((), (), s32[]{:S(2)}) async-start(), calls=%async_computation.10 | async-start | bytes 5652480 | tf_op jit(solution)/shard_map/all_gather | solution.py:952
  93.7 44.8 %collective-permute-start.14 = (bf16[704,1408]{1,0:T(8,128)(2,1)S(1)}, bf16[704,1408]{1,0:T(8,128)(2,1)S(1)}, u32[]{:S(2)}, u32[]{:S(2)}) collective-permute-start(bf16[704,1408]{1,0:T(8,128)(2,1)S(1)} %join_gathered.1.refs_1_), channel_id=1, source_target_pairs={{0,8},{8,0},{1,9},{9,1},{2,10},{10,2},{3,11},{11,3},{4,12},{12,4},... | collective-permute-start | bytes 5947400 | tf_op jit(solution)/shard_map/ppermute | solution.py:675
  94.3 44.5 %collective-permute-start.15 = (bf16[704,1408]{1,0:T(8,128)(2,1)S(1)}, bf16[704,1408]{1,0:T(8,128)(2,1)S(1)}, u32[]{:S(2)}, u32[]{:S(2)}) collective-permute-start(bf16[704,1408]{1,0:T(8,128)(2,1)S(1)} %join_gathered.1.refs_1_), channel_id=1, source_target_pairs={{0,16},{16,0},{1,17},{17,1},{2,18},{18,2},{3,19},{19,3},{4,20},{20... | collective-permute-start | bytes 5947400 | tf_op jit(solution)/shard_map/ppermute | solution.py:675
  99.6 75.7 %collective-permute-start.25 = (bf16[2,1408]{1,0:T(2,128)(2,1)S(1)}, bf16[2,1408]{1,0:T(2,128)(2,1)S(1)}, u32[]{:S(2)}, u32[]{:S(2)}) collective-permute-start(bf16[2,1408]{1,0:T(2,128)(2,1)S(1)} %copy-done.163), channel_id=1, source_target_pairs={{0,4},{4,0},{1,5},{5,1},{2,6},{6,2},{3,7},{7,3},{8,12},{12,8},{9,1... | collective-permute-start | bytes 16904 | tf_op jit(solution)/shard_map/ppermute | solution.py:675
  141.4 46.5 %collective-permute-start.16 = (bf16[352,1408]{1,0:T(8,128)(2,1)}, bf16[352,1408]{1,0:T(8,128)(2,1)S(1)}, u32[]{:S(2)}, u32[]{:S(2)}) collective-permute-start(bf16[352,1408]{1,0:T(8,128)(2,1)} %slice.227), channel_id=1, source_target_pairs={{0,16},{16,0},{1,17},{17,1},{2,18},{18,2},{3,19},{19,3},{4,20},{20... | collective-permute-start | bytes 2973704 | tf_op jit(solution)/shard_map/ppermute | solution.py:675
  159.8 45.5 %collective-permute-start.20 = (bf16[704,1408]{1,0:T(8,128)(2,1)S(1)}, bf16[704,1408]{1,0:T(8,128)(2,1)}, u32[]{:S(2)}, u32[]{:S(2)}) collective-permute-start(bf16[704,1408]{1,0:T(8,128)(2,1)S(1)} %join_gathered.1.refs_1_), channel_id=1, source_target_pairs={{0,4},{4,0},{1,5},{5,1},{2,6},{6,2},{3,7},{7,3},{8,12},{12,8},{9,1... | collective-permute-start | bytes 5947400 | tf_op jit(solution)/shard_map/ppermute | solution.py:675
  201.6 199.1 %all-gather.17.cloned.1.call-start = ((), (), s32[]{:S(2)}) async-start(), calls=%async_computation.11 | async-start | bytes 12976128 | tf_op jit(solution)/shard_map/all_gather | solution.py:1052
  205.3 57.3 %collective-permute-start.18 = (bf16[528,1408]{1,0:T(8,128)(2,1)}, bf16[528,1408]{1,0:T(8,128)(2,1)}, u32[]{:S(2)}, u32[]{:S(2)}) collective-permute-start(bf16[528,1408]{1,0:T(8,128)(2,1)} %get-tuple-element.143.refs_1_), channel_id=1, source_target_pairs={{0,8},{8,0},{1,9},{9,1},{2,10},{10,2},{3,11},{11,3},{4,12},{12,4},... | collective-permute-start | bytes 4460552 | tf_op jit(solution)/shard_map/ppermute | solution.py:675
  205.9 58.3 %collective-permute-start.19 = (bf16[528,1408]{1,0:T(8,128)(2,1)}, bf16[528,1408]{1,0:T(8,128)(2,1)S(1)}, u32[]{:S(2)}, u32[]{:S(2)}) collective-permute-start(bf16[528,1408]{1,0:T(8,128)(2,1)} %get-tuple-element.143.refs_1_), channel_id=1, source_target_pairs={{0,16},{16,0},{1,17},{17,1},{2,18},{18,2},{3,19},{19,3},{4,20},{20... | collective-permute-start | bytes 4460552 | tf_op jit(solution)/shard_map/ppermute | solution.py:675
  206.4 55.4 %collective-permute-start.28 = (bf16[352,1024]{1,0:T(8,128)(2,1)}, bf16[352,1024]{1,0:T(8,128)(2,1)}, u32[]{:S(2)}, u32[]{:S(2)}) collective-permute-start(bf16[352,1024]{1,0:T(8,128)(2,1)} %get-tuple-element.151.refs_1_), channel_id=1, source_target_pairs={{0,8},{8,0},{1,9},{9,1},{2,10},{10,2},{3,11},{11,3},{4,12},{12,4},... | collective-permute-start | bytes 2162696 | tf_op jit(solution)/shard_map/ppermute | solution.py:675
  262.6 41.2 %collective-permute-start.38 = (bf16[320,1408]{1,0:T(8,128)(2,1)S(1)}, bf16[320,1408]{1,0:T(8,128)(2,1)S(1)}, u32[]{:S(2)}, u32[]{:S(2)}) collective-permute-start(bf16[320,1408]{1,0:T(8,128)(2,1)S(1)} %get-tuple-element.370), channel_id=1, source_target_pairs={{0,1},{1,0},{2,5},{3,4},{4,3},{5,2},{6,7},{7,6},{8,9},{9,8},{10,13... | collective-permute-start | bytes 2703368 | tf_op jit(solution)/shard_map/ppermute | solution.py:726
  309.2 179.2 %all-gather.19.cloned.1.call-start = ((), (), s32[]{:S(2)}) async-start(), calls=%async_computation.12 | async-start | bytes 12976128 | tf_op jit(solution)/shard_map/all_gather | solution.py:1072
  342.6 42.3 %collective-permute-start.46 = (bf16[1408,128]{1,0:T(8,128)(2,1)}, bf16[1408,128]{1,0:T(8,128)(2,1)}, u32[]{:S(2)}, u32[]{:S(2)}) collective-permute-start(bf16[1408,128]{1,0:T(8,128)(2,1)} %fusion.51.refs_1_.refs_4_), channel_id=1, source_target_pairs={{0,4},{4,0},{1,5},{5,1},{2,6},{6,2},{3,7},{7,3},{8,12},{12,8},{9,1... | collective-permute-start | bytes 1081352 | tf_op jit(solution)/shard_map/ppermute | solution.py:675
  343.0 41.9 %collective-permute-start.47 = (bf16[1408,128]{1,0:T(8,128)(2,1)}, bf16[1408,128]{1,0:T(8,128)(2,1)}, u32[]{:S(2)}, u32[]{:S(2)}) collective-permute-start(bf16[1408,128]{1,0:T(8,128)(2,1)} %slice.429.refs_3_.refs_6_), channel_id=1, source_target_pairs={{0,4},{4,0},{1,5},{5,1},{2,6},{6,2},{3,7},{7,3},{8,12},{12,8},{9,1... | collective-permute-start | bytes 1081352 | tf_op jit(solution)/shard_map/ppermute | solution.py:675
  400.8 243.7 %reduce-scatter.5.cloned.1.call-start = ((), (), s32[]{:S(2)}) async-start(), calls=%async_computation.4 | async-start | bytes 12976128 | tf_op jit(solution)/shard_map/reduce_scatter | solution.py:1095
  404.9 56.9 %collective-permute-start.55 = (bf16[1408,512]{1,0:T(8,128)(2,1)}, bf16[1408,512]{1,0:T(8,128)(2,1)}, u32[]{:S(2)}, u32[]{:S(2)}) collective-permute-start(bf16[1408,512]{1,0:T(8,128)(2,1)} %fusion.23.refs_8_), channel_id=1, source_target_pairs={{0,4},{4,0},{1,5},{5,1},{2,6},{6,2},{3,7},{7,3},{8,12},{12,8},{9,1... | collective-permute-start | bytes 4325384 | tf_op jit(solution)/shard_map/ppermute | solution.py:675
  406.9 54.9 %collective-permute-start.56 = (bf16[1408,512]{1,0:T(8,128)(2,1)}, bf16[1408,512]{1,0:T(8,128)(2,1)}, u32[]{:S(2)}, u32[]{:S(2)}) collective-permute-start(bf16[1408,512]{1,0:T(8,128)(2,1)} %get-tuple-element.163.refs_2_.refs_6_), channel_id=1, source_target_pairs={{0,4},{4,0},{1,5},{5,1},{2,6},{6,2},{3,7},{7,3},{8,12},{12,8},{9,1... | collective-permute-start | bytes 4325384 | tf_op jit(solution)/shard_map/ppermute | solution.py:675
  411.4 50.4 %collective-permute-start.59 = (bf16[1408,512]{1,0:T(8,128)(2,1)}, bf16[1408,512]{1,0:T(8,128)(2,1)}, u32[]{:S(2)}, u32[]{:S(2)}) collective-permute-start(bf16[1408,512]{1,0:T(8,128)(2,1)} %get-tuple-element.171.refs_2_.refs_6_), channel_id=1, source_target_pairs={{0,4},{4,0},{1,5},{5,1},{2,6},{6,2},{3,7},{7,3},{8,12},{12,8},{9,1... | collective-permute-start | bytes 4325384 | tf_op jit(solution)/shard_map/ppermute | solution.py:675
  417.4 44.5 %collective-permute-start.57 = (bf16[1408,512]{1,0:T(8,128)(2,1)}, bf16[1408,512]{1,0:T(8,128)(2,1)}, u32[]{:S(2)}, u32[]{:S(2)}) collective-permute-start(bf16[1408,512]{1,0:T(8,128)(2,1)} %multiply_convert_fusion.1.refs_8_), channel_id=1, source_target_pairs={{0,4},{4,0},{1,5},{5,1},{2,6},{6,2},{3,7},{7,3},{8,12},{12,8},{9,1... | collective-permute-start | bytes 4325384 | tf_op jit(solution)/shard_map/ppermute | solution.py:675
  536.5 224.2 %reduce-scatter.7.cloned.1.call-start = ((), (), s32[]{:S(2)}) async-start(), calls=%async_computation.5 | async-start | bytes 12976128 | tf_op jit(solution)/shard_map/reduce_scatter | solution.py:1184
  644.5 216.4 %reduce-scatter.9.cloned.1.call-start = ((), (), s32[]{:S(2)}) async-start(), calls=%async_computation.6 | async-start | bytes 5652480 | tf_op jit(solution)/shard_map/reduce_scatter | solution.py:1188
  711.2 41.4 %collective-permute-start.78 = (bf16[352,1408]{1,0:T(8,128)(2,1)}, bf16[352,1408]{1,0:T(8,128)(2,1)}, u32[]{:S(2)}, u32[]{:S(2)}) collective-permute-start(bf16[352,1408]{1,0:T(8,128)(2,1)} %get-tuple-element.216), channel_id=1, source_target_pairs={{0,16},{16,0},{1,17},{17,1},{2,18},{18,2},{3,19},{19,3},{4,20},{20... | collective-permute-start | bytes 2973704 | tf_op jit(solution)/shard_map/ppermute | solution.py:675
  743.9 317.7 %reduce-scatter.11.cloned.1.call-start = ((), (), s32[]{:S(2)}) async-start(), calls=%async_computation.7 | async-start | bytes 5406720 | tf_op jit(solution)/shard_map/reduce_scatter | solution.py:1238
  783.1 56.1 %collective-permute-start.82 = (bf16[704,1408]{1,0:T(8,128)(2,1)}, bf16[704,1408]{1,0:T(8,128)(2,1)}, u32[]{:S(2)}, u32[]{:S(2)}) collective-permute-start(bf16[704,1408]{1,0:T(8,128)(2,1)} %add_dynamic-update-slice_fusion.3), channel_id=1, source_target_pairs={{0,16},{16,0},{1,17},{17,1},{2,18},{18,2},{3,19},{19,3},{4,20},{20... | collective-permute-start | bytes 5947400 | tf_op jit(solution)/shard_map/ppermute | solution.py:675
  784.5 55.7 %collective-permute-start.83 = (bf16[704,1408]{1,0:T(8,128)(2,1)}, bf16[704,1408]{1,0:T(8,128)(2,1)}, u32[]{:S(2)}, u32[]{:S(2)}) collective-permute-start(bf16[704,1408]{1,0:T(8,128)(2,1)} %add_dynamic-update-slice_fusion.2), channel_id=1, source_target_pairs={{0,8},{8,0},{1,9},{9,1},{2,10},{10,2},{3,11},{11,3},{4,12},{12,4},... | collective-permute-start | bytes 5947400 | tf_op jit(solution)/shard_map/ppermute | solution.py:675
  795.6 54.9 %collective-permute-start.81 = (bf16[320,1408]{1,0:T(8,128)(2,1)}, bf16[320,1408]{1,0:T(8,128)(2,1)}, u32[]{:S(2)}, u32[]{:S(2)}) collective-permute-start(bf16[320,1408]{1,0:T(8,128)(2,1)} %get-tuple-element.367), channel_id=1, source_target_pairs={{1,0},{0,1},{5,2},{4,3},{3,4},{2,5},{7,6},{6,7},{9,8},{8,9},{13,10... | collective-permute-start | bytes 2703368 | tf_op jit(solution)/shard_map/ppermute | solution.py:735
  797.2 53.4 %collective-permute-start.73 = (bf16[320,1408]{1,0:T(8,128)(2,1)}, bf16[320,1408]{1,0:T(8,128)(2,1)}, u32[]{:S(2)}, u32[]{:S(2)}) collective-permute-start(bf16[320,1408]{1,0:T(8,128)(2,1)} %get-tuple-element.368), channel_id=1, source_target_pairs={{0,0},{1,1},{4,2},{5,3},{2,4},{3,5},{6,6},{7,7},{8,8},{9,9},{12,10... | collective-permute-start | bytes 2703368 | tf_op jit(solution)/shard_map/ppermute | solution.py:735
  865.9 53.2 %collective-permute-start.88 = (bf16[704,1408]{1,0:T(8,128)(2,1)}, bf16[704,1408]{1,0:T(8,128)(2,1)}, u32[]{:S(2)}, u32[]{:S(2)}) collective-permute-start(bf16[704,1408]{1,0:T(8,128)(2,1)} %add_dynamic-update-slice_fusion.1), channel_id=1, source_target_pairs={{0,16},{16,0},{1,17},{17,1},{2,18},{18,2},{3,19},{19,3},{4,20},{20... | collective-permute-start | bytes 5947400 | tf_op jit(solution)/shard_map/ppermute | solution.py:675
  870.0 49.1 %collective-permute-start.89 = (bf16[704,1408]{1,0:T(8,128)(2,1)}, bf16[704,1408]{1,0:T(8,128)(2,1)}, u32[]{:S(2)}, u32[]{:S(2)}) collective-permute-start(bf16[704,1408]{1,0:T(8,128)(2,1)} %add_dynamic-update-slice_fusion), channel_id=1, source_target_pairs={{0,8},{8,0},{1,9},{9,1},{2,10},{10,2},{3,11},{11,3},{4,12},{12,4},... | collective-permute-start | bytes 5947400 | tf_op jit(solution)/shard_map/ppermute | solution.py:675
  883.0 48.1 %collective-permute-start.90 = (bf16[1408,512]{1,0:T(8,128)(2,1)}, bf16[1408,512]{1,0:T(8,128)(2,1)}, u32[]{:S(2)}, u32[]{:S(2)}) collective-permute-start(bf16[1408,512]{1,0:T(8,128)(2,1)} %bitcast.79.refs_0_), channel_id=1, source_target_pairs={{0,4},{4,0},{1,5},{5,1},{2,6},{6,2},{3,7},{7,3},{8,12},{12,8},{9,1... | collective-permute-start | bytes 4325384 | tf_op jit(solution)/shard_map/ppermute | solution.py:675
  (263 other events, 3158.5 us)
Sparse Core Ops, SparseCore 0:
  10.4 64.2 all-gather.10
  76.3 55.6 all-gather.12
  201.7 102.0 all-gather.14
  309.3 88.0 all-gather.16
  400.9 87.4 all-gather.18
  536.6 107.8 reduce-scatter.4
  648.0 103.1 reduce-scatter.6
  753.5 107.3 reduce-scatter.8
  942.2 78.0 reduce-scatter.10
